TPU v7x, 32 devices: a whole 2x2x4 slice. The times are simulated.
32 devices in a mesh: strip: 4 (over y, core), cell: 8 (over z, x).
Axes of the slice: x: 2, y: 2, z: 4, core: 2. Of those that a mesh axis runs over, the one named last changes fastest.
Arguments:
- features: bfloat16 [8192, 256], P(('strip', 'cell')), may hold values from -6 to 6
- pair_atom: int32 [131072], P(('strip', 'cell')), may hold values from 0 to 255
- partner_row: int32 [131072], P(('strip', 'cell')), may hold values from 0 to 383, as said below
- transpose_slot: int32 [131072], P(('strip', 'cell')), may hold values from 0 to 6143, as said below
- distance: float32 [131072], P(('strip', 'cell')), may hold values from 1 to 8
- send_rows: int32 [256, 48], P(('strip', 'cell')), may hold values from 0 to 767, as said below
- w_left: bfloat16 [256, 256], replicated, may hold values from -0.375 to 0.375
- w_right: bfloat16 [256, 256], replicated, may hold values from -0.375 to 0.375
- w_radial_in: bfloat16 [128, 256], replicated, may hold values from -4 to 4
- w_radial_out: bfloat16 [256, 256], replicated, may hold values from -0.375 to 0.375
- w_mix: bfloat16 [256, 256], replicated, may hold values from -0.375 to 0.375
- w_out: bfloat16 [256, 169], replicated, may hold values from -0.375 to 0.375
Outputs:
- own_blocks: bfloat16 [169, 131072], P(None, ('strip', 'cell'))
- partner_blocks: bfloat16 [169, 196608], P(None, ('strip', 'cell'))
Inputs may be any that keep to these rules, and one draw needn't show every extreme that they name: `transpose_slot`: within one device the values are distinct; at most 256 of them share t // 256, and on every device one such group holds exactly 256. For pair slot p with transpose_slot t: partner_row // 48 equals (t // 256) % 8, and partner_row % 3 equals t // 2048. `send_rows`: entry k lies in [(k % 3) * 256, (k % 3 + 1) * 256); part k % 3 names the device of strip s - 1, s, s + 1 (cyclic) with the same cell index.
All inputs are finite; a program needn't handle non-finite values.
Results may differ from a plain program's by a relative error of at most 0.0084.
Values may be sent and summed in bfloat16 or wider, within the bound.
No kernel may reach another device: no remote copies, remote signals or barrier semaphores. Data moves between devices by JAX's collectives and lax.ppermute only.
A program may use at most 64 MiB of HBM per device.

v0:
```python
import jax
import jax.numpy as jnp
import numpy as np
from jax import lax
from jax.sharding import PartitionSpec as P

cutoff = 8.0


def padded(cells, sides, width):
    for axis, dim in sides:
        count = lax.axis_size(axis)
        head = lax.slice_in_dim(cells, 0, width, axis=dim)
        tail = lax.slice_in_dim(cells, cells.shape[dim] - width, cells.shape[dim], axis=dim)
        cells = jnp.concatenate(
            [
                lax.ppermute(tail, axis, [(i, (i + 1) % count) for i in range(count)]),
                cells,
                lax.ppermute(head, axis, [((i + 1) % count, i) for i in range(count)]),
            ],
            axis=dim,
        )
    return cells


def passed_along(x, axis, by):
    peers = lax.axis_size(axis)
    return lax.ppermute(x, axis, [(i, (i + by) % peers) for i in range(peers)])


def radial_basis(distance, count):
    centers = jnp.arange(count, dtype=jnp.float32) * (cutoff / (count - 1))
    spacing = 2.0 * cutoff / count
    scaled = (distance[:, None] - centers[None, :]) / spacing
    envelope = 0.5 * (jnp.cos(jnp.pi * distance / cutoff) + 1.0)
    return (jnp.exp(-scaled * scaled) * envelope[:, None]).astype(jnp.bfloat16)


def select_rows(index, table):
    picker = (index[:, None] == jnp.arange(table.shape[0], dtype=jnp.int32)[None, :]).astype(
        jnp.bfloat16
    )
    return jnp.dot(picker, table, preferred_element_type=jnp.float32).astype(jnp.bfloat16)


def body(
    features,
    pair_atom,
    partner_row,
    transpose_slot,
    distance,
    send_rows,
    w_left,
    w_right,
    w_radial_in,
    w_radial_out,
    w_mix,
    w_out,
):
    atom_count = features.shape[0]
    width = features.shape[1]
    cells = lax.axis_size("cell")
    extended = padded(features[None], (("strip", 0),), 1)
    nearby = extended.reshape(3 * atom_count, width)
    outgoing = nearby[send_rows]
    fetched = lax.all_to_all(outgoing, "cell", split_axis=0, concat_axis=0, tiled=True)
    fetched = fetched.reshape(-1, width)
    left = jnp.dot(features, w_left, preferred_element_type=jnp.float32).astype(jnp.bfloat16)
    right = jnp.dot(fetched, w_right, preferred_element_type=jnp.float32).astype(jnp.bfloat16)
    left_rows = select_rows(pair_atom, left)
    right_rows = select_rows(partner_row, right)
    basis = radial_basis(distance, w_radial_in.shape[0])
    radial = jax.nn.silu(jnp.dot(basis, w_radial_in, preferred_element_type=jnp.float32)).astype(
        jnp.bfloat16
    )
    gate = jnp.dot(radial, w_radial_out, preferred_element_type=jnp.float32)
    edge = (left_rows.astype(jnp.float32) * right_rows.astype(jnp.float32) * gate).astype(
        jnp.bfloat16
    )
    mixed = jax.nn.silu(jnp.dot(edge, w_mix, preferred_element_type=jnp.float32)).astype(
        jnp.bfloat16
    )
    own_blocks = lax.dot_general(
        w_out, mixed, (((0,), (1,)), ((), ())), preferred_element_type=jnp.float32
    ).astype(jnp.bfloat16)
    entries = w_out.shape[1]
    orbitals = int(np.sqrt(entries) + 0.5)
    order = np.arange(entries).reshape(orbitals, orbitals).T.reshape(-1)
    w_flipped = w_out[:, order]
    slot_total = 3 * cells * (pair_atom.shape[0] // (2 * cells))
    placed = jnp.zeros((slot_total, width), jnp.bfloat16).at[transpose_slot].set(mixed)
    outbox = lax.dot_general(
        w_flipped, placed, (((0,), (1,)), ((), ())), preferred_element_type=jnp.float32
    ).astype(jnp.bfloat16)
    outbox = outbox.reshape(entries, 3, slot_total // 3)
    arrived = lax.all_to_all(outbox, "cell", split_axis=2, concat_axis=2, tiled=True)
    pieces = [None, arrived[:, 1], None]
    for which, offset in ((0, -1), (2, 1)):
        pieces[which] = passed_along(arrived[:, which], "strip", offset)
    gathered = jnp.stack(pieces, 1)
    partner_blocks = gathered.reshape(entries, slot_total)
    return (own_blocks, partner_blocks)


def solution(mesh):
    in_specs = (
        P(("strip", "cell"), None),
        P(("strip", "cell")),
        P(("strip", "cell")),
        P(("strip", "cell")),
        P(("strip", "cell")),
        P(("strip", "cell"), None),
        P(),
        P(),
        P(),
        P(),
        P(),
        P(),
    )
    out_specs = (P(None, ("strip", "cell")), P(None, ("strip", "cell")))
    return jax.shard_map(body, mesh=mesh, in_specs=in_specs, out_specs=out_specs, check_vma=False)
```

profile of v0, /device:TPU:0, one launch (start us, length us, event | category | flops | bytes accessed | tf_op | source)
XLA Modules:
  0.0 190.1 jit_solution(9059176191922762308)
XLA Ops:
  0.7 2.5 %collective-permute-start.1 = (bf16[1,256,256]{2,1,0:T(8,128)(2,1)}, bf16[1,256,256]{2,1,0:T(8,128)(2,1)S(1)}, u32[]{:S(2)}, u32[]{:S(2)}) collective-permute-start(bf16[1,256,256]{2,1,0:T(8,128)(2,1)} %bitcast.34), channel_id=1, source_target_pairs={{8,0},{16,8},{24,16},{0,24},{9,1},{17,9},{25,17},{1,25},{10,2},{18... | collective-permute-start | bytes 393224 | tf_op jit(solution)/shard_map/ppermute | solution.py:19
  4.7 2.6 %collective-permute-done.1 = bf16[1,256,256]{2,1,0:T(8,128)(2,1)S(1)} collective-permute-done((bf16[1,256,256]{2,1,0:T(8,128)(2,1)}, bf16[1,256,256]{2,1,0:T(8,128)(2,1)S(1)}, u32[]{:S(2)}, u32[]{:S(2)}) %collective-permute-start.1) | collective-permute-done | bytes 131104 | tf_op jit(solution)/shard_map/ppermute | solution.py:19
  9.2 2.6 %gather_fusion = bf16[384,256]{1,0:T(8,128)(2,1)} fusion(bf16[768,256]{1,0:T(8,128)(2,1)S(1)} %bitcast.31, s32[1024]{0:T(1024)S(1)} %pad_clamp_fusion.1), kind=kCustom, calls=%fused_computation | custom fusion | bytes 394752 | tf_op jit(solution)/shard_map/gather | solution.py:65
  11.8 5.8 %all-to-all-start = ((bf16[8,48,256]{2,1,0:T(8,128)(2,1)}), bf16[8,48,256]{2,1,0:T(8,128)(2,1)S(1)}, u32[]{:S(2)}, u32[]{:S(2)}) async-start(bf16[8,48,256]{2,1,0:T(8,128)(2,1)} %bitcast.2), calls=%async_computation | async-start | bytes 393216 | tf_op jit(solution)/shard_map/all_to_all | solution.py:66
  17.6 2.1 %multiply_convert_fusion.1 = bf16[4096,256]{1,0:T(8,128)(2,1)S(1)} fusion(bf16[128,256]{1,0:T(8,128)(2,1)S(1)} %copy-done.11, f32[4096]{0:T(1024)S(1)} %add_multiply_fusion, f32[128]{0:T(128)S(1)} %iota_multiply_fusion, f32[4096]{0:T(1024)S(1)} %copy-done.6), kind=kOutput, calls=%fused_computation.16 | convolution fusion | flops 276824064 | bytes 2195968 | tf_op jit(solution)/shard_map/dot_general | solution.py:73
  20.8 4.6 %all-to-all-done = bf16[8,48,256]{2,1,0:T(8,128)(2,1)S(1)} async-done(((bf16[8,48,256]{2,1,0:T(8,128)(2,1)}), bf16[8,48,256]{2,1,0:T(8,128)(2,1)S(1)}, u32[]{:S(2)}, u32[]{:S(2)}) %all-to-all-start) | async-done | bytes 196640 | tf_op jit(solution)/shard_map/all_to_all | solution.py:66
  25.4 3.5 %fusion.5 = f32[4096,256]{1,0:T(8,128)} fusion(s32[4096]{0:T(1024)S(1)} %copy-done.4, bf16[384,256]{1,0:T(8,128)(2,1)S(1)} %bitcast.33, bf16[256,256]{1,0:T(8,128)(2,1)S(1)} %copy-done), kind=kOutput, calls=%fused_computation.12 | convolution fusion | flops 859406336 | bytes 4538368 | tf_op jit(solution)/shard_map/dot_general | solution.py:43
  28.9 4.3 %fusion.2 = f32[4096,256]{1,0:T(8,128)} fusion(f32[4096,256]{1,0:T(8,128)} %fusion.5, s32[4096]{0:T(1024)S(1)} %copy-done.5, bf16[256,256]{1,0:T(8,128)(2,1)S(1)} %copy-done.2, bf16[256,256]{1,0:T(8,128)(2,1)S(1)} %copy-done.3), kind=kOutput, calls=%fused_computation.9 | convolution fusion | flops 574685184 | bytes 8667136 | tf_op jit(solution)/shard_map/dot_general | solution.py:43
  33.2 4.9 %multiply_convert_fusion = bf16[4096,256]{1,0:T(8,128)(2,1)} fusion(bf16[256,256]{1,0:T(8,128)(2,1)S(1)} %copy-done.9, f32[4096,256]{1,0:T(8,128)} %fusion.2, bf16[4096,256]{1,0:T(8,128)(2,1)S(1)} %multiply_convert_fusion.1, bf16[256,256]{1,0:T(8,128)(2,1)S(1)} %copy-done.10), kind=kOutput, calls=%fused_computation.15 | convolution fusion | flops 1081081856 | bytes 8650752 | tf_op jit(solution)/shard_map/dot_general | solution.py:80
  38.1 19.5 %scatter_custom_fusion = bf16[6144,256]{1,0:T(8,128)(2,1)S(1)} fusion(s32[4096]{0:T(1024)S(1)} %compare_select_fusion, bf16[4096,256]{1,0:T(8,128)(2,1)} %multiply_convert_fusion, bf16[]{:T(256)} %constant.30.clone.1), kind=kCustom, calls=%fused_computation.26 | custom fusion | bytes 3146240 | tf_op jit(solution)/shard_map/scatter | solution.py:91
  57.6 2.5 %convolution_convert_fusion = bf16[169,6144]{1,0:T(8,128)(2,1)} fusion(bf16[169,256]{1,0:T(8,128)(2,1)S(1)} %gather_fusion.1, bf16[6144,256]{1,0:T(8,128)(2,1)S(1)} %scatter_custom_fusion), kind=kOutput, calls=%fused_computation.3 | convolution fusion | flops 532666368 | bytes 5308928 | tf_op jit(solution)/shard_map/dot_general | solution.py:92
  60.2 5.9 %reshape.26 = bf16[169,3,2048]{2,1,0:T(4,128)(2,1)S(1)} reshape(bf16[169,6144]{1,0:T(8,128)(2,1)} %convolution_convert_fusion) | data formatting | bytes 4153344 | tf_op jit(solution)/shard_map/reshape | solution.py:95
  66.1 7.6 %copy.29 = bf16[169,3,2048]{0,1,2:T(4,128)(2,1)} copy(bf16[169,3,2048]{2,1,0:T(4,128)(2,1)S(1)} %reshape.26) | data formatting | bytes 4153344 | tf_op jit(solution)/shard_map/reshape | solution.py:95
  73.7 9.0 %reshape.57 = bf16[8,2,64896]{2,1,0:T(2,128)(2,1)S(1)} reshape(bf16[2048,3,169]{2,1,0:T(4,128)(2,1)} %bitcast.29) | data formatting | bytes 4153344
  82.6 49.2 %all_to_all.10 = bf16[8,2,64896]{2,1,0:T(2,128)(2,1)} all-to-all(bf16[8,2,64896]{2,1,0:T(2,128)(2,1)S(1)} %reshape.57), channel_id=1, replica_groups=mesh['strip'=4,'cell'=8] {'cell'}, dimensions={0} | all-to-all | bytes 4153344 | tf_op jit(solution)/shard_map/all_to_all | solution.py:96
  131.9 10.1 %reshape.58 = bf16[2048,3,169]{2,1,0:T(4,128)(2,1)} reshape(bf16[8,2,64896]{2,1,0:T(2,128)(2,1)} %all_to_all.10) | data formatting | bytes 4153344
  141.9 11.1 %fusion.21 = (bf16[169,1,2048]{0,1,2:T(2,128)(2,1)}, bf16[169,1,2048]{0,1,2:T(2,128)(2,1)S(1)}, bf16[169,1,2048]{0,1,2:T(2,128)(2,1)}) fusion(bf16[169,3,2048]{0,1,2:T(4,128)(2,1)} %bitcast.28), kind=kLoop, calls=%fused_computation.42 | loop fusion | bytes 4153344 | tf_op jit(solution)/shard_map/slice | solution.py:99
  153.0 5.8 %copy.34 = bf16[169,1,2048]{2,0,1:T(8,128)(2,1)} copy(bf16[169,1,2048]{0,1,2:T(2,128)(2,1)} %get-tuple-element.2) | data formatting | bytes 1384448
  158.8 5.7 %copy.36 = bf16[169,1,2048]{2,0,1:T(8,128)(2,1)} copy(bf16[169,1,2048]{0,1,2:T(2,128)(2,1)} %get-tuple-element.4) | data formatting | bytes 1384448
  166.3 3.5 %fusion.6 = bf16[169,4096]{1,0:T(8,128)(2,1)} fusion(bf16[4096,256]{1,0:T(8,128)(2,1)} %multiply_convert_fusion, bf16[256,169]{0,1:T(8,128)(2,1)S(1)} %copy-done.1), kind=kOutput, calls=%fused_computation.14 | convolution fusion | flops 355110912 | bytes 3568128 | tf_op jit(solution)/shard_map/dot_general | solution.py:83
  171.0 8.6 %collective-permute-done.3 = bf16[169,2048]{1,0:T(8,128)(2,1)} collective-permute-done((bf16[169,2048]{1,0:T(8,128)(2,1)}, bf16[169,2048]{1,0:T(8,128)(2,1)}, u32[]{:S(2)}, u32[]{:S(2)}) %collective-permute-start.3) | collective-permute-done | bytes 692256 | tf_op jit(solution)/shard_map/ppermute | solution.py:28
  179.6 2.5 %collective-permute-done.2 = bf16[169,2048]{1,0:T(8,128)(2,1)} collective-permute-done((bf16[169,2048]{1,0:T(8,128)(2,1)}, bf16[169,2048]{1,0:T(8,128)(2,1)}, u32[]{:S(2)}, u32[]{:S(2)}) %collective-permute-start.2) | collective-permute-done | bytes 692256 | tf_op jit(solution)/shard_map/ppermute | solution.py:28
  183.7 1.8 copy.33
  187.0 3.2 %copy.37 = bf16[22,8,3,2048]{3,1,2,0:T(8,128)(2,1)} copy(bf16[22,8,3,2048]{3,2,1,0:T(4,128)(2,1)S(1)} %bitcast.30) | data formatting | bytes 4325376
  (40 shorter events, 10.5 us)
Async XLA Ops:
  0.6 24.7 %copy-start = (bf16[256,256]{1,0:T(8,128)(2,1)S(1)}, bf16[256,256]{1,0:T(8,128)(2,1)}, u32[]{:S(2)}) copy-start(bf16[256,256]{1,0:T(8,128)(2,1)} %param.21) | copy-start | bytes 393220
  0.6 16.9 %copy-start.6 = (f32[4096]{0:T(1024)S(1)}, f32[4096]{0:T(1024)}, u32[]{:S(2)}) copy-start(f32[4096]{0:T(1024)} %param.18) | copy-start | bytes 49156
  0.7 16.9 %copy-start.11 = (bf16[128,256]{1,0:T(8,128)(2,1)S(1)}, bf16[128,256]{1,0:T(8,128)(2,1)}, u32[]{:S(2)}) copy-start(bf16[128,256]{1,0:T(8,128)(2,1)} %param.22) | copy-start | bytes 196612
  0.7 6.6 %collective-permute-start.1 = (bf16[1,256,256]{2,1,0:T(8,128)(2,1)}, bf16[1,256,256]{2,1,0:T(8,128)(2,1)S(1)}, u32[]{:S(2)}, u32[]{:S(2)}) collective-permute-start(bf16[1,256,256]{2,1,0:T(8,128)(2,1)} %bitcast.34), channel_id=1, source_target_pairs={{8,0},{16,8},{24,16},{0,24},{9,1},{17,9},{25,17},{1,25},{10,2},{18... | collective-permute-start | bytes 393224 | tf_op jit(solution)/shard_map/ppermute | solution.py:19
  3.1 5.1 %collective-permute-start = (bf16[1,256,256]{2,1,0:T(8,128)(2,1)}, bf16[1,256,256]{2,1,0:T(8,128)(2,1)S(1)}, u32[]{:S(2)}, u32[]{:S(2)}) collective-permute-start(bf16[1,256,256]{2,1,0:T(8,128)(2,1)} %bitcast.35), channel_id=1, source_target_pairs={{0,8},{8,16},{16,24},{24,0},{1,9},{9,17},{17,25},{25,1},{2,10},{10... | collective-permute-start | bytes 393224 | tf_op jit(solution)/shard_map/ppermute | solution.py:17
  11.8 13.6 %all-to-all-start = ((bf16[8,48,256]{2,1,0:T(8,128)(2,1)}), bf16[8,48,256]{2,1,0:T(8,128)(2,1)S(1)}, u32[]{:S(2)}, u32[]{:S(2)}) async-start(bf16[8,48,256]{2,1,0:T(8,128)(2,1)} %bitcast.2), calls=%async_computation | async-start | bytes 393216 | tf_op jit(solution)/shard_map/all_to_all | solution.py:66
  17.6 2.2 %copy-start.8 = (s32[169]{0:T(256)S(1)}, s32[169]{0:T(256)}, u32[]{:S(2)}) copy-start(s32[169]{0:T(256)} %constant.36) | copy-start | bytes 2032
  17.6 2.2 %copy-start.1 = (bf16[256,169]{0,1:T(8,128)(2,1)S(1)}, bf16[256,169]{0,1:T(8,128)(2,1)}, u32[]{:S(2)}) copy-start(bf16[256,169]{0,1:T(8,128)(2,1)} %param.25) | copy-start | bytes 259588
  17.6 3.2 %copy-start.7 = (s32[4096]{0:T(1024)S(1)}, s32[4096]{0:T(1024)}, u32[]{:S(2)}) copy-start(s32[4096]{0:T(1024)} %param.17) | copy-start | bytes 49156
  17.6 7.7 %copy-start.4 = (s32[4096]{0:T(1024)S(1)}, s32[4096]{0:T(1024)}, u32[]{:S(2)}) copy-start(s32[4096]{0:T(1024)} %param.16) | copy-start | bytes 49156
  25.4 3.5 %copy-start.2 = (bf16[256,256]{1,0:T(8,128)(2,1)S(1)}, bf16[256,256]{1,0:T(8,128)(2,1)}, u32[]{:S(2)}) copy-start(bf16[256,256]{1,0:T(8,128)(2,1)} %param.14) | copy-start | bytes 393220
  25.4 3.5 %copy-start.3 = (bf16[256,256]{1,0:T(8,128)(2,1)S(1)}, bf16[256,256]{1,0:T(8,128)(2,1)}, u32[]{:S(2)}) copy-start(bf16[256,256]{1,0:T(8,128)(2,1)} %param.20) | copy-start | bytes 393220
  25.4 3.5 %copy-start.5 = (s32[4096]{0:T(1024)S(1)}, s32[4096]{0:T(1024)}, u32[]{:S(2)}) copy-start(s32[4096]{0:T(1024)} %param.15) | copy-start | bytes 49156
  28.8 4.4 %copy-start.9 = (bf16[256,256]{1,0:T(8,128)(2,1)S(1)}, bf16[256,256]{1,0:T(8,128)(2,1)}, u32[]{:S(2)}) copy-start(bf16[256,256]{1,0:T(8,128)(2,1)} %param.24) | copy-start | bytes 393220
  28.9 4.4 %copy-start.10 = (bf16[256,256]{1,0:T(8,128)(2,1)S(1)}, bf16[256,256]{1,0:T(8,128)(2,1)}, u32[]{:S(2)}) copy-start(bf16[256,256]{1,0:T(8,128)(2,1)} %param.23) | copy-start | bytes 393220
  164.5 15.1 %collective-permute-start.3 = (bf16[169,2048]{1,0:T(8,128)(2,1)}, bf16[169,2048]{1,0:T(8,128)(2,1)}, u32[]{:S(2)}, u32[]{:S(2)}) collective-permute-start(bf16[169,2048]{1,0:T(8,128)(2,1)} %bitcast.7), channel_id=1, source_target_pairs={{0,8},{8,16},{16,24},{24,0},{1,9},{9,17},{17,25},{25,1},{2,10},{10... | collective-permute-start | bytes 2076680 | tf_op jit(solution)/shard_map/ppermute | solution.py:28
  164.5 17.6 %collective-permute-start.2 = (bf16[169,2048]{1,0:T(8,128)(2,1)}, bf16[169,2048]{1,0:T(8,128)(2,1)}, u32[]{:S(2)}, u32[]{:S(2)}) collective-permute-start(bf16[169,2048]{1,0:T(8,128)(2,1)} %bitcast.5), channel_id=1, source_target_pairs={{0,24},{8,0},{16,8},{24,16},{1,25},{9,1},{17,9},{25,17},{2,26},{10... | collective-permute-start | bytes 2076680 | tf_op jit(solution)/shard_map/ppermute | solution.py:28
where the time goes:
time: 192 us; the launch traced here: 190 us
  local copies, waits for them, and re-layouts  85.9 us (45%)
  blocking collectives  49.2 us (26%)
  matrix products  20.9 us (11%)
  waiting for transfers between devices  19.2 us (10%)
  starting transfers between devices  10 us (5%)
  other arithmetic  4.02 us (2%)
    all_to_all x1, blocking collectives, body(): lax.all_to_all(outbox, 'cell', split_axis=2, concat_axis=2, tiled=True)  49.2 us
    unnamed x31, local copies, waits for them, and re-layouts  36.4 us
    scatter x1, local copies, waits for them, and re-layouts, body(): jnp.zeros((slot_total, width), jnp.bfloat16).at[transpose_slot].set(mixed)  19.5 us
    reshape x2, local copies, waits for them, and re-layouts, body(): outbox = outbox.reshape(entries, 3, slot_total // 3)  13.5 us
    slice x1, local copies, waits for them, and re-layouts, body(): pieces[which] = passed_along(arrived[:, which], 'strip', offset)  11.1 us
    ppermute x2, waiting for transfers between devices, passed_along(): return lax.ppermute(x, axis, [(i, (i + by) % peers) for i in range(peers)])  11.1 us
    dot_general x2, matrix products, select_rows(): jnp.dot(picker, table, preferred_element_type=jnp.float32)  7.79 us
    all_to_all x1, starting transfers between devices, body(): lax.all_to_all(outgoing, 'cell', split_axis=0, concat_axis=0, tiled=True)  5.81 us
  transfers between devices with their start and end apart: 5, of which 5 were waited for; matrix products, arithmetic and copies ran while one was open for 5% of the time, Pallas kernels for 0%

commit v1 on v0

v1 whole, which is shorter than its diff:
```python
import functools

import jax
import jax.numpy as jnp
from jax import lax
from jax.experimental import pallas as pl
from jax.experimental.pallas import tpu as pltpu
from jax.sharding import PartitionSpec as P

cutoff = 8.0
PLANES = 5
BF16 = jnp.bfloat16
F32 = jnp.float32
AXES = ("strip", "cell")


def up(n, by):
    return -(-n // by) * by


def whole_div(x, by):
    return jnp.floor((x.astype(F32) + 0.5) * (1.0 / by)).astype(jnp.int32)


def dot(a, b, ca=1, cb=0):
    return lax.dot_general(a, b, (((ca,), (cb,)), ((), ())), preferred_element_type=F32)


def silu(x):
    half = 0.5 * x
    return half + half * jnp.tanh(half)


def onehot(index, count):
    rows = lax.broadcasted_iota(jnp.int32, (count, index.shape[1]), 0)
    return (rows == index).astype(BF16)


def gate_of(distance, w_in_t, w_out_t):
    count = w_in_t.shape[1]
    centers = lax.broadcasted_iota(jnp.int32, (count, 1), 0).astype(F32) * (cutoff / (count - 1))
    scaled = (distance - centers) * (count / (2.0 * cutoff))
    envelope = 0.5 * (jnp.cos(distance * (jnp.pi / cutoff)) + 1.0)
    basis = (jnp.exp(-scaled * scaled) * envelope).astype(BF16)
    radial = silu(dot(w_in_t, basis)).astype(BF16)
    return dot(w_out_t, radial)


def whole(a):
    return pl.BlockSpec(a.shape, lambda *_: (0,) * a.ndim)


def cost(flops, nbytes=1 << 20):
    return pl.CostEstimate(flops=flops, bytes_accessed=nbytes, transcendentals=0)


class Sizes:
    def __init__(self, features, pair_atom, send_rows, w_radial_in, w_out):
        self.atoms, self.width = features.shape
        self.pairs = pair_atom.shape[0]
        self.cells, self.fetch = send_rows.shape
        self.strips = lax.axis_size("strip")
        self.inner = 2
        self.outer = self.cells // 2
        self.slot = self.pairs // (2 * self.cells)
        self.part = self.fetch // 3
        self.groups = 3 * self.inner
        self.meta = up(PLANES * self.groups, 16)
        self.lists = up(self.cells, 16)
        self.rows = self.atoms + self.meta + self.lists
        self.entries = w_out.shape[1]


def where_am_i():
    strip, cell = lax.axis_index("strip"), lax.axis_index("cell")
    even = lax.rem(strip, 2) == 0
    return cell, lax.div(cell, 2), lax.rem(cell, 2), even


def tiles_kernel(n, atom_ref, row_ref, slot_ref, dist_ref, list_ref, feat_ref, *outs):
    _, zi, _, _ = where_am_i()
    slot = slot_ref[...]
    hi = whole_div(slot, n.slot)
    lo = slot - hi * n.slot
    row = row_ref[...]
    k = row - whole_div(row, n.fetch) * n.fetch
    dist = dist_ref[...]
    d1 = dist.astype(BF16)
    rest = dist - d1.astype(F32)
    d2 = rest.astype(BF16)
    d3 = (rest - d2.astype(F32)).astype(BF16)
    planes = [
        d1.astype(F32),
        d2.astype(F32),
        d3.astype(F32),
        (atom_ref[...] + 1).astype(F32),
        whole_div(k, 3).astype(F32),
    ]
    total = 3 * n.cells
    mask = lax.broadcasted_iota(jnp.int32, (total, n.pairs), 0) == hi
    spread = jnp.concatenate([jnp.where(mask, p, 0.0) for p in planes], 0).astype(BF16)
    placed = dot(spread, onehot(lo, n.slot), 1, 1).astype(BF16)
    shape = (n.meta, PLANES * total)
    r = lax.broadcasted_iota(jnp.int32, shape, 0)
    q = lax.broadcasted_iota(jnp.int32, shape, 1)
    plane = whole_div(r, n.groups)
    g = r - plane * n.groups
    base = plane * total + whole_div(g, n.inner) * n.cells + (g - whole_div(g, n.inner) * n.inner)
    e = list_ref[...]
    kk = lax.broadcasted_iota(jnp.int32, e.shape, 1)
    e = (e - (kk - whole_div(kk, 3) * 3) * n.atoms).astype(F32)
    feat = feat_ref[...]
    for b, out in enumerate(outs):
        zz = jnp.bitwise_xor(zi, b)
        pick = ((base + zz * n.inner == q) & (r < PLANES * n.groups)).astype(BF16)
        out[0 : n.atoms, :] = feat
        tail = dot(pick, placed)
        if n.slot < n.width:
            tail = jnp.concatenate([tail, jnp.zeros((n.meta, n.width - n.slot), F32)], 1)
        out[n.atoms : n.atoms + n.meta, :] = tail.astype(BF16)
        out[n.atoms + n.meta :, :] = jnp.zeros((n.lists, n.width), BF16)
        out[n.atoms + n.meta : n.atoms + n.meta + n.cells, 0 : n.fetch] = e.astype(BF16)


def make_tiles(n, pair_atom, partner_row, transpose_slot, distance, send_rows, features):
    args = (pair_atom, partner_row, transpose_slot, distance, send_rows, features)
    return pl.pallas_call(
        functools.partial(tiles_kernel, n),
        out_shape=[jax.ShapeDtypeStruct((n.rows, n.width), BF16)] * n.outer,
        compiler_params=pltpu.CompilerParams(vmem_limit_bytes=48 << 20),
        cost_estimate=cost(600_000_000),
        name="place_pairs",
    )(*args)


def prepare_kernel(*refs):
    half = len(refs) // 2
    for src, dst in zip(refs[:half], refs[half:]):
        dst[...] = src[...].T


def prepare(weights):
    return pl.pallas_call(
        prepare_kernel,
        out_shape=[jax.ShapeDtypeStruct(w.shape[::-1], w.dtype) for w in weights],
        cost_estimate=cost(100_000_000),
        name="transpose_weights",
    )(*weights)


def own_gate_kernel(dist_ref, atom_ref, feat_ref, w_left_ref, w_in_ref, w_ro_ref, out_ref):
    gate = gate_of(dist_ref[...], w_in_ref[...], w_ro_ref[...])
    left = dot(w_left_ref[...], feat_ref[...], 1, 1).astype(BF16)
    out_ref[...] = gate * dot(left, onehot(atom_ref[...], left.shape[1]))


def own_gate(n, step, distance, pair_atom, features, w_left_t, w_in_t, w_ro_t):
    row = pl.BlockSpec((1, step), lambda i: (0, i))
    return pl.pallas_call(
        own_gate_kernel,
        grid=(n.pairs // step,),
        in_specs=[row, row] + [whole(a) for a in (features, w_left_t, w_in_t, w_ro_t)],
        out_specs=pl.BlockSpec((n.width, step), lambda i: (0, i)),
        out_shape=jax.ShapeDtypeStruct((n.width, n.pairs), F32),
        compiler_params=pltpu.CompilerParams(vmem_limit_bytes=48 << 20),
        cost_estimate=cost(3_000_000_000),
        name="own_gate",
    )(distance, pair_atom, features, w_left_t, w_in_t, w_ro_t)


def partner_tables_kernel(n, own_ref, sib_ref, oth_ref, w_right_ref, out_ref):
    _, _, _, even = where_am_i()
    right = dot(w_right_ref[...], own_ref[0 : n.atoms, :], 1, 1).astype(BF16)
    lanes = n.cells * n.part
    shape = (n.fetch, lanes)
    k = lax.broadcasted_iota(jnp.int32, shape, 0)
    lane = lax.broadcasted_iota(jnp.int32, shape, 1)
    m3 = (lane - whole_div(lane, n.part) * n.part) * 3
    mine = lax.broadcasted_iota(jnp.int32, (n.cells, lanes), 0)
    cell = whole_div(lax.broadcasted_iota(jnp.int32, (n.cells, lanes), 1), n.part)
    o_sib = jnp.where(even, 0, 2)
    for role, (ref, o) in enumerate(((own_ref, 1), (sib_ref, o_sib), (oth_ref, 2 - o_sib))):
        lists = ref[n.atoms + n.meta : n.atoms + n.meta + n.cells, 0 : n.fetch]
        per = dot(lists, (k == m3 + o).astype(BF16))
        index = jnp.sum(jnp.where(mine == cell, per, 0.0), 0, keepdims=True)
        out_ref[role] = dot(right, onehot(index.astype(jnp.int32), n.atoms)).astype(BF16)


def partner_tables(n, own, sib, oth, w_right_t):
    return pl.pallas_call(
        functools.partial(partner_tables_kernel, n),
        out_shape=jax.ShapeDtypeStruct((3, n.width, n.cells * n.part), BF16),
        cost_estimate=cost(200_000_000),
        name="partner_tables",
    )(own, sib, oth, w_right_t)


def received_kernel(n, b, direct, column_ref, *refs):
    tiles, refs = refs[:6], refs[6:]
    table_ref, w_left_ref, w_in_ref, w_ro_ref, w_mix_ref, w_out_ref = refs[:6]
    block_ref, rows_ref = refs[-3:-1] if direct else refs[-2:]
    held = refs[-1] if direct else None

    def compute():
        me, zi, xi, even = where_am_i()
        o_sib = jnp.where(even, 0, 2)
        roles = (1, o_sib, 2 - o_sib)
        r = lax.broadcasted_iota(jnp.int32, (8, n.meta), 0)
        q = lax.broadcasted_iota(jnp.int32, (8, n.meta), 1)
        m3 = 3 * lax.broadcasted_iota(jnp.int32, (n.part, n.fetch), 0)
        k = lax.broadcasted_iota(jnp.int32, (n.part, n.fetch), 1)
        mine = lax.broadcasted_iota(jnp.int32, (n.cells, n.fetch), 0) == me
        metas, lefts, rights = [], [], []
        for at in range(n.inner):
            cell = jnp.bitwise_xor(zi, b) * n.inner + jnp.bitwise_xor(xi, at)
            lists = tiles[3 * at][n.atoms + n.meta : n.atoms + n.meta + n.cells, 0 : n.fetch]
            row = jnp.sum(jnp.where(mine, lists.astype(F32), 0.0), 0, keepdims=True)
            for role, o in enumerate(roles):
                tile = tiles[3 * at + role]
                feat = tile[0 : n.atoms, :]
                here = 3 * at + role
                o_own = 1 if role == 0 else 2 - o
                index = jnp.sum(jnp.where(k == m3 + o_own, row, 0.0), 1, keepdims=True)
                atom = lax.broadcasted_iota(jnp.int32, (n.part, n.atoms), 1)
                pick = (atom == index.astype(jnp.int32)).astype(BF16)
                rows_ref[here * n.part : (here + 1) * n.part, :] = dot(pick, feat).astype(BF16)
                wanted = (q == r * n.groups + o * n.inner + xi) & (r < PLANES)
                meta = dot(wanted.astype(BF16), tile[n.atoms : n.atoms + n.meta, :])
                meta = meta[:, 0 : n.slot]
                left = dot(w_left_ref[...], feat, 1, 1).astype(BF16)
                lefts.append(dot(left, onehot(meta[3:4].astype(jnp.int32) - 1, n.atoms)))
                place = meta[4:5].astype(jnp.int32) + cell * n.part
                rights.append(dot(table_ref[role], onehot(place, n.cells * n.part)))
                metas.append(meta[0:1] + meta[1:2] + meta[2:3])
        gate = gate_of(jnp.concatenate(metas, 1), w_in_ref[...], w_ro_ref[...])
        edge = jnp.concatenate(lefts, 1) * jnp.concatenate(rights, 1) * gate
        mixed = silu(dot(w_mix_ref[...], edge.astype(BF16))).astype(BF16)
        blocks = dot(w_out_ref[...], mixed).astype(BF16)
        if direct:
            for g in range(6):
                held[g] = blocks[:, g * n.slot : (g + 1) * n.slot]
        else:
            block_ref[...] = blocks

    if direct:
        pl.when(pl.program_id(0) == 0)(compute)
        block_ref[...] = held[pl.program_id(0)]
    else:
        compute()


def received(n, b, columns, tiles, table, weights, into):
    direct = n.slot % 128 == 0
    operands = list(tiles) + [table] + list(weights)
    specs = [whole(a) for a in operands]
    aliases = {}
    if direct:
        block = pl.BlockSpec((n.entries, n.slot), lambda i, column: (0, column[i]))
        shape = (n.entries, 3 * n.cells * n.slot)
        scratch = [pltpu.VMEM((6, n.entries, n.slot), BF16)]
        if into is not None:
            aliases = {1 + len(operands): 0}
            operands.append(into)
            specs.append(pl.BlockSpec(memory_space=pl.ANY))
    else:
        shape = (n.entries, 6 * n.slot)
        block = pl.BlockSpec(shape, lambda i, column: (0, 0))
        scratch = []
    rows = (6 * n.part, n.width)
    return pl.pallas_call(
        functools.partial(received_kernel, n, b, direct),
        grid_spec=pltpu.PrefetchScalarGridSpec(
            num_scalar_prefetch=1,
            grid=(6 if direct else 1,),
            in_specs=specs,
            out_specs=[block, pl.BlockSpec(rows, lambda i, column: (0, 0))],
            scratch_shapes=scratch,
        ),
        out_shape=[jax.ShapeDtypeStruct(shape, BF16), jax.ShapeDtypeStruct(rows, BF16)],
        input_output_aliases=aliases,
        compiler_params=pltpu.CompilerParams(vmem_limit_bytes=48 << 20),
        cost_estimate=cost(3_000_000_000),
        name="received_blocks",
    )(columns, *operands)


def own_blocks_kernel(n, row_ref, held_ref, w_right_ref, w_mix_ref, w_out_ref, *refs):
    tables, out_ref, right_ref = refs[:-2], refs[-2], refs[-1]
    _, zi, xi, even = where_am_i()

    @pl.when(pl.program_id(0) == 0)
    def _():
        rows = jnp.concatenate([t[...] for t in tables], 0)
        right_ref[...] = dot(w_right_ref[...], rows, 1, 1).astype(BF16)

    v = row_ref[...]
    q = whole_div(v, n.fetch)
    k = v - q * n.fetch
    m = whole_div(k, 3)
    o = k - 3 * m
    sibling = jnp.where(even, 2, 0)
    role = jnp.where(o == 1, 0, jnp.where(o == sibling, 1, 2))
    outer = whole_div(q, n.inner)
    inner = q - outer * n.inner
    place = (jnp.bitwise_xor(outer, zi) * n.inner + jnp.bitwise_xor(inner, xi)) * 3 + role
    right = dot(right_ref[...], onehot(place * n.part + m, right_ref.shape[1]))
    edge = (held_ref[...] * right).astype(BF16)
    mixed = silu(dot(w_mix_ref[...], edge)).astype(BF16)
    out_ref[...] = dot(w_out_ref[...], mixed).astype(BF16)


def own_blocks_of(n, step, partner_row, held, w_right_t, w_mix_t, w_out_t, tables):
    return pl.pallas_call(
        functools.partial(own_blocks_kernel, n),
        grid=(n.pairs // step,),
        in_specs=[
            pl.BlockSpec((1, step), lambda i: (0, i)),
            pl.BlockSpec((n.width, step), lambda i: (0, i)),
        ]
        + [whole(a) for a in (w_right_t, w_mix_t, w_out_t, *tables)],
        out_specs=pl.BlockSpec((n.entries, step), lambda i: (0, i)),
        out_shape=jax.ShapeDtypeStruct((n.entries, n.pairs), BF16),
        scratch_shapes=[pltpu.VMEM((n.width, 3 * n.cells * n.part), BF16)],
        compiler_params=pltpu.CompilerParams(vmem_limit_bytes=48 << 20),
        cost_estimate=cost(3_000_000_000),
        name="own_blocks",
    )(partner_row, held, w_right_t, w_mix_t, w_out_t, *tables)


def body(
    features,
    pair_atom,
    partner_row,
    transpose_slot,
    distance,
    send_rows,
    w_left,
    w_right,
    w_radial_in,
    w_radial_out,
    w_mix,
    w_out,
):
    n = Sizes(features, pair_atom, send_rows, w_radial_in, w_out)
    orbitals = int(n.entries**0.5 + 0.5)
    lines = n.strips * n.cells

    def exchange(x, partner):
        pairs = []
        for i in range(lines):
            s, c = partner(i // n.cells, i % n.cells)
            pairs.append((i, s * n.cells + c))
        return lax.ppermute(x, AXES, pairs)

    def along(by):
        return lambda s, c: (s, c ^ (by * n.inner))

    def beside(s, c):
        return s, c ^ 1

    def sibling(s, c):
        return s ^ 1, c

    def other(s, c):
        return (s - 1 if s % 2 == 0 else s + 1) % n.strips, c

    def corner(s, c):
        return other(s, c)[0], c ^ 1

    row = lambda a: a.reshape(1, -1)
    pair_atom, partner_row = row(pair_atom), row(partner_row)
    transpose_slot, distance = row(transpose_slot), row(distance)
    tiles = make_tiles(
        n, pair_atom, partner_row, transpose_slot, distance, send_rows, features
    )
    lines_in = [tiles[0]] + [exchange(tiles[b], along(b)) for b in range(1, n.outer)]
    flip = w_out.reshape(-1, orbitals, orbitals).swapaxes(1, 2).reshape(w_out.shape)
    w_left_t, w_right_t, w_in_t, w_ro_t, w_mix_t, w_out_t, w_flip_t = prepare(
        [w_left, w_right, w_radial_in, w_radial_out, w_mix, w_out, flip]
    )
    step = n.pairs // 2
    held = own_gate(n, step, distance, pair_atom, features, w_left_t, w_in_t, w_ro_t)
    cell = lax.axis_index("cell")
    strip = lax.axis_index("strip")
    o_sib = jnp.where(strip % 2 == 0, 0, 2)
    weights = (w_left_t, w_in_t, w_ro_t, w_mix_t, w_flip_t)
    table, into, tables, parts = None, None, [], []
    for b, tile in enumerate(lines_in):
        across = exchange(tile, beside)
        group = [
            tile,
            exchange(tile, sibling),
            exchange(tile, other),
            across,
            exchange(across, sibling),
            exchange(tile, corner),
        ]
        if b == 0:
            table = partner_tables(n, group[0], group[1], group[2], w_right_t)
        near = cell ^ (b * n.inner)
        columns = jnp.stack(
            [o * n.cells + c for c in (near, near ^ 1) for o in (1, o_sib, 2 - o_sib)]
        ).astype(jnp.int32)
        into, rows = received(n, b, columns, group, table, weights, into)
        tables.append(rows)
        parts.append((columns, into))
    if n.slot % 128:
        into = jnp.zeros((n.entries, 3 * n.cells * n.slot), BF16)
        for columns, blocks in parts:
            for g in range(6):
                piece = blocks[:, g * n.slot : (g + 1) * n.slot]
                into = lax.dynamic_update_slice(into, piece, (0, columns[g] * n.slot))
    own = own_blocks_of(n, step, partner_row, held, w_right_t, w_mix_t, w_out_t, tables)
    return own, into


def solution(mesh):
    split = P(("strip", "cell"))
    wide = P(("strip", "cell"), None)
    in_specs = (wide, split, split, split, split, wide) + (P(),) * 6
    out_specs = (P(None, ("strip", "cell")), P(None, ("strip", "cell")))
    return jax.shard_map(body, mesh=mesh, in_specs=in_specs, out_specs=out_specs, check_vma=False)
```

time: 192 us -> 74.3 us (0.39)
  local copies, waits for them, and re-layouts: 85.9 us -> 14.8 us
  blocking collectives: 49.2 us -> 0 us
  Pallas kernels: 0 us -> 34.4 us
  matrix products: 20.9 us -> 0 us
  waiting for transfers between devices: 19.2 us -> 3.33 us
  starting transfers between devices: 10 us -> 20.2 us
  other arithmetic: 4.02 us -> 0 us
    all_to_all x1 -> x0, blocking collectives: 49.2 us -> none  [body(): lax.all_to_all(outbox, 'cell', split_axis=2, concat_axis=2, tiled=True)]
    pallas_call x0 -> x9, Pallas kernels: none -> 34.4 us  [the longest x4 20.9 us: received(): pl.pallas_call(functools.partial(received_kernel, n, b, direct), grid_spe...]
    unnamed x31 -> x63, local copies, waits for them, and re-layouts: 36.4 us -> 13.6 us
    dot_general x6 -> x0, matrix products: 20.9 us -> none  [the longest x2 7.79 us: select_rows(): jnp.dot(picker, table, preferred_element_type=jnp.float32)]
    scatter x1 -> x0, local copies, waits for them, and re-layouts: 19.5 us -> none  [body(): jnp.zeros((slot_total, width), jnp.bfloat16).at[transpose_slot].set(mixed)]
    ppermute x4 -> x23, starting transfers between devices: 4.21 us -> 20.2 us  [exchange(): return lax.ppermute(x, AXES, pairs)]
    reshape x2 -> x4, local copies, waits for them, and re-layouts: 13.5 us -> 0.88 us  [body(): w_out.reshape(-1, orbitals, orbitals).swapaxes(1, 2).reshape(w_out.shape)]
    ppermute x4 -> x23, waiting for transfers between devices: 14.6 us -> 3.33 us  [exchange(): return lax.ppermute(x, AXES, pairs)]
  transfers between devices with their start and end apart: 5 -> 23, of which waited for: 5 -> 2; matrix products, arithmetic and copies ran while one was open for 5% -> 3% of each run, Pallas kernels for 0% -> 32%
where the time goes in v1:
time: 74.3 us; the launch traced here: 73.6 us
  Pallas kernels  34.4 us (46%)
  starting transfers between devices  20.2 us (27%)
  local copies, waits for them, and re-layouts  14.8 us (20%)
  waiting for transfers between devices  3.33 us (4%)
  between operations  0.89 us (1%)
    pallas_call x4, Pallas kernels, received(): pl.pallas_call(functools.partial(received_kernel, n, b, direct), grid_spe...  20.9 us
    ppermute x23, starting transfers between devices, exchange(): return lax.ppermute(x, AXES, pairs)  20.2 us
    unnamed x63, local copies, waits for them, and re-layouts  13.6 us
    pallas_call x1, Pallas kernels, own_blocks_of(): pl.pallas_call(functools.partial(own_blocks_kernel, n), grid=(n.pairs //...  4.42 us
    ppermute x23, waiting for transfers between devices, exchange(): return lax.ppermute(x, AXES, pairs)  3.33 us
    pallas_call x1, Pallas kernels, own_gate(): pl.pallas_call(own_gate_kernel, grid=(n.pairs // step,), in_specs=[row, r...  3.31 us
    pallas_call x1, Pallas kernels, partner_tables(): pl.pallas_call(functools.partial(partner_tables_kernel, n), out_shape=jax...  2.42 us
    pallas_call x1, Pallas kernels, prepare(): pl.pallas_call(prepare_kernel, out_shape=[jax.ShapeDtypeStruct(w.shape[::...  2.27 us
  transfers between devices with their start and end apart: 23, of which 2 were waited for; matrix products, arithmetic and copies ran while one was open for 3% of the time, Pallas kernels for 32%

profile of v1, /device:TPU:0, one launch (start us, length us, event | category | flops | bytes accessed | tf_op | source)
XLA Modules:
  0.0 73.6 jit_solution(15725137846324384699)
XLA Ops:
  5.1 1.1 %place_pairs.1 = (bf16[304,256]{1,0:T(8,128)(2,1)S(1)}, bf16[304,256]{1,0:T(8,128)(2,1)S(1)}, bf16[304,256]{1,0:T(8,128)(2,1)S(1)}, bf16[304,256]{1,0:T(8,128)(2,1)S(1)}) custom-call(s32[1,4096]{1,0:T(1,128)S(1)} %bitcast.38, s32[1,4096]{1,0:T(1,128)S(1)} %bitcast.40, s32[1,4096]{1,0:T(1,128)S(1)} %bitcast.35, f32[1,4096]{1,0:T(1,128)S(1)} %bitcast.36, ...), custom_call_target="tpu_custom_call" | custom-call | flops 600000000 | bytes 1048576 | tf_op jit(solution)/shard_map/place_pairs/pallas_call | solution.py:127
  6.2 3.1 %collective-permute-start.5 = (bf16[304,256]{1,0:T(8,128)(2,1)S(1)}, bf16[304,256]{1,0:T(8,128)(2,1)S(1)}, u32[]{:S(2)}, u32[]{:S(2)}) collective-permute-start(bf16[304,256]{1,0:T(8,128)(2,1)S(1)} %get-tuple-element.30), channel_id=1, source_target_pairs={{0,2},{1,3},{2,0},{3,1},{4,6},{5,7},{6,4},{7,5},{8,10},{9,11},{10,... | collective-permute-start | bytes 466952 | tf_op jit(solution)/shard_map/ppermute | solution.py:353
  9.3 1.5 %collective-permute-start.2 = (bf16[304,256]{1,0:T(8,128)(2,1)S(1)}, bf16[304,256]{1,0:T(8,128)(2,1)S(1)}, u32[]{:S(2)}, u32[]{:S(2)}) collective-permute-start(bf16[304,256]{1,0:T(8,128)(2,1)S(1)} %get-tuple-element.27.own_ref.refs_0_), channel_id=1, source_target_pairs={{0,1},{1,0},{2,3},{3,2},{4,5},{5,4},{6,7},{7,6},{8,9},{9,8},{10,11... | collective-permute-start | bytes 466952 | tf_op jit(solution)/shard_map/ppermute | solution.py:353
  11.2 1.2 %collective-permute-start = (bf16[304,256]{1,0:T(8,128)(2,1)S(1)}, bf16[304,256]{1,0:T(8,128)(2,1)S(1)}, u32[]{:S(2)}, u32[]{:S(2)}) collective-permute-start(bf16[304,256]{1,0:T(8,128)(2,1)S(1)} %get-tuple-element.27.own_ref.refs_0_), channel_id=1, source_target_pairs={{0,8},{1,9},{2,10},{3,11},{4,12},{5,13},{6,14},{7,15},{8,0},{9,1},... | collective-permute-start | bytes 466952 | tf_op jit(solution)/shard_map/ppermute | solution.py:353
  14.2 2.3 %transpose_weights.1 = (bf16[256,256]{1,0:T(8,128)(2,1)}, bf16[256,256]{1,0:T(8,128)(2,1)}, bf16[256,128]{1,0:T(8,128)(2,1)}, bf16[256,256]{1,0:T(8,128)(2,1)}, ...) custom-call(bf16[256,256]{1,0:T(8,128)(2,1)} %refs_0_.1, bf16[256,256]{1,0:T(8,128)(2,1)} %refs_1_.1, ...), custom_call_target="tpu_custom_call" | custom-call | flops 100000000 | bytes 1048576 | tf_op jit(solution)/shard_map/transpose_weights/pallas_call | solution.py:143
  16.4 2.6 %collective-permute-start.11 = (bf16[304,256]{1,0:T(8,128)(2,1)S(1)}, bf16[304,256]{1,0:T(8,128)(2,1)S(1)}, u32[]{:S(2)}, u32[]{:S(2)}) collective-permute-start(bf16[304,256]{1,0:T(8,128)(2,1)S(1)} %get-tuple-element.33), channel_id=1, source_target_pairs={{0,4},{1,5},{2,6},{3,7},{4,0},{5,1},{6,2},{7,3},{8,12},{9,13},{10,... | collective-permute-start | bytes 466952 | tf_op jit(solution)/shard_map/ppermute | solution.py:353
  19.2 1.2 %collective-permute-done.1.oth_ref.refs_2_ = bf16[304,256]{1,0:T(8,128)(2,1)S(1)} collective-permute-done((bf16[304,256]{1,0:T(8,128)(2,1)S(1)}, bf16[304,256]{1,0:T(8,128)(2,1)S(1)}, u32[]{:S(2)}, u32[]{:S(2)}) %collective-permute-start.1) | collective-permute-done | bytes 155680 | tf_op jit(solution)/shard_map/ppermute | solution.py:353
  21.0 0.9 %copy-done.12 = bf16[256,256]{1,0:T(8,128)(2,1)S(1)} copy-done((bf16[256,256]{1,0:T(8,128)(2,1)S(1)}, bf16[256,256]{1,0:T(8,128)(2,1)}, u32[]{:S(2)}) %copy-start.12) | copy-done | bytes 131096
  23.7 3.3 %own_gate.1.held_ref = f32[256,4096]{1,0:T(8,128)S(1)} custom-call(f32[1,4096]{1,0:T(1,128)S(1)} %bitcast.37, s32[1,4096]{1,0:T(1,128)S(1)} %bitcast.39, bf16[256,256]{1,0:T(8,128)(2,1)S(1)} %copy-done.10, bf16[256,256]{1,0:T(8,128)(2,1)S(1)} %copy-done.12, bf16[256,128]{1,0:T(8,128)(2,1)S(1)} %copy-done.18, bf16[256,256]{1,0:T(8,128)(2,1)S(1)} %copy-done.14), custom_call_target="tpu_custom_call" | custom-call | flops 3000000000 | bytes 1048576 | tf_op jit(solution)/shard_map/own_gate/pallas_call | solution.py:159
  27.0 2.0 %copy-done.28 = f32[256,4096]{1,0:T(8,128)} copy-done((f32[256,4096]{1,0:T(8,128)}, f32[256,4096]{1,0:T(8,128)S(1)}, u32[]{:S(2)}) %copy-start.28) | copy-done | bytes 4194328
  29.3 2.4 %partner_tables.1.refs_6_ = bf16[3,256,128]{2,1,0:T(8,128)(2,1)} custom-call(bf16[304,256]{1,0:T(8,128)(2,1)} %copy-done.2, bf16[304,256]{1,0:T(8,128)(2,1)} %copy-done.6, bf16[304,256]{1,0:T(8,128)(2,1)} %copy-done.4, bf16[256,256]{1,0:T(8,128)(2,1)} %get-tuple-element.24.w_right_ref), custom_call_target="tpu_custom_call" | custom-call | flops 200000000 | bytes 1048576 | tf_op jit(solution)/shard_map/partner_tables/pallas_call | solution.py:190
  31.8 2.0 %collective-permute-start.10 = (bf16[304,256]{1,0:T(8,128)(2,1)S(1)}, bf16[304,256]{1,0:T(8,128)(2,1)S(1)}, u32[]{:S(2)}, u32[]{:S(2)}) collective-permute-start(bf16[304,256]{1,0:T(8,128)(2,1)S(1)} %collective-permute-done.5.refs_0_), channel_id=1, source_target_pairs={{0,25},{1,24},{2,27},{3,26},{4,29},{5,28},{6,31},{7,30},{8,17},{9,... | collective-permute-start | bytes 466952 | tf_op jit(solution)/shard_map/ppermute | solution.py:353
  35.5 0.9 %copy-done = bf16[3,256,128]{2,1,0:T(8,128)(2,1)S(1)} copy-done((bf16[3,256,128]{2,1,0:T(8,128)(2,1)S(1)}, bf16[3,256,128]{2,1,0:T(8,128)(2,1)}, u32[]{:S(2)}) %copy-start) | copy-done | bytes 196632
  36.4 0.9 %copy-done.3 = bf16[304,256]{1,0:T(8,128)(2,1)S(1)} copy-done((bf16[304,256]{1,0:T(8,128)(2,1)S(1)}, bf16[304,256]{1,0:T(8,128)(2,1)}, u32[]{:S(2)}) %copy-start.3) | copy-done | bytes 155672
  37.3 0.9 %copy-done.5 = bf16[304,256]{1,0:T(8,128)(2,1)S(1)} copy-done((bf16[304,256]{1,0:T(8,128)(2,1)S(1)}, bf16[304,256]{1,0:T(8,128)(2,1)}, u32[]{:S(2)}) %copy-start.5) | copy-done | bytes 155672
  38.2 0.9 %copy-done.7 = bf16[304,256]{1,0:T(8,128)(2,1)S(1)} copy-done((bf16[304,256]{1,0:T(8,128)(2,1)S(1)}, bf16[304,256]{1,0:T(8,128)(2,1)}, u32[]{:S(2)}) %copy-start.7) | copy-done | bytes 155672
  39.1 5.2 %received_blocks.4 = (bf16[169,6144]{1,0:T(8,128)(2,1)}, bf16[96,256]{1,0:T(8,128)(2,1)S(1)}) custom-call(s32[6]{0:T(128)S(1)} %stack.90.column_ref, bf16[304,256]{1,0:T(8,128)(2,1)S(1)} %copy-done.3, bf16[304,256]{1,0:T(8,128)(2,1)S(1)} %copy-done.7, bf16[304,256]{1,0:T(8,128)(2,1)S(1)} %copy-done.5, bf16[304,256]{1,0:T(8,128)(2,1)S(1)} %collective-permute-done.2.refs_3_, ...), custom_call_target="tpu_custom_call" | custom-call | flops 3000000000 | bytes 1048576 | tf_op jit(solution)/shard_map/received_blocks/pallas_call | solution.py:270
  44.3 2.1 %collective-permute-start.16 = (bf16[304,256]{1,0:T(8,128)(2,1)S(1)}, bf16[304,256]{1,0:T(8,128)(2,1)S(1)}, u32[]{:S(2)}, u32[]{:S(2)}) collective-permute-start(bf16[304,256]{1,0:T(8,128)(2,1)S(1)} %collective-permute-done.11.refs_0_), channel_id=1, source_target_pairs={{0,25},{1,24},{2,27},{3,26},{4,29},{5,28},{6,31},{7,30},{8,17},{9,... | collective-permute-start | bytes 466952 | tf_op jit(solution)/shard_map/ppermute | solution.py:353
  48.1 5.2 %received_blocks.5 = (bf16[169,6144]{1,0:T(8,128)(2,1)}, bf16[96,256]{1,0:T(8,128)(2,1)S(1)}) custom-call(s32[6]{0:T(128)S(1)} %stack.97.column_ref, bf16[304,256]{1,0:T(8,128)(2,1)S(1)} %collective-permute-done.5.refs_0_, bf16[304,256]{1,0:T(8,128)(2,1)S(1)} %collective-permute-done.6.refs_1_, ...), custom_call_target="tpu_custom_call", output_to_operand_aliasing={{0}: (13, {})} | custom-call | flops 3000000000 | bytes 1048576 | tf_op jit(solution)/shard_map/received_blocks/pallas_call | solution.py:270
  53.2 2.1 %collective-permute-start.22 = (bf16[304,256]{1,0:T(8,128)(2,1)S(1)}, bf16[304,256]{1,0:T(8,128)(2,1)S(1)}, u32[]{:S(2)}, u32[]{:S(2)}) collective-permute-start(bf16[304,256]{1,0:T(8,128)(2,1)S(1)} %collective-permute-done.17.refs_0_), channel_id=1, source_target_pairs={{0,25},{1,24},{2,27},{3,26},{4,29},{5,28},{6,31},{7,30},{8,17},{9,... | collective-permute-start | bytes 466952 | tf_op jit(solution)/shard_map/ppermute | solution.py:353
  56.5 5.2 %received_blocks.6 = (bf16[169,6144]{1,0:T(8,128)(2,1)}, bf16[96,256]{1,0:T(8,128)(2,1)S(1)}) custom-call(s32[6]{0:T(128)S(1)} %stack.104.column_ref, bf16[304,256]{1,0:T(8,128)(2,1)S(1)} %collective-permute-done.11.refs_0_, bf16[304,256]{1,0:T(8,128)(2,1)S(1)} %collective-permute-done.12.refs_1_, ...), custom_call_target="tpu_custom_call", output_to_operand_aliasing={{0}: (13, {})} | custom-call | flops 3000000000 | bytes 1048576 | tf_op jit(solution)/shard_map/received_blocks/pallas_call | solution.py:270
  61.7 2.1 %collective-permute-done.19.refs_2_ = bf16[304,256]{1,0:T(8,128)(2,1)S(1)} collective-permute-done((bf16[304,256]{1,0:T(8,128)(2,1)S(1)}, bf16[304,256]{1,0:T(8,128)(2,1)S(1)}, u32[]{:S(2)}, u32[]{:S(2)}) %collective-permute-start.19) | collective-permute-done | bytes 155680 | tf_op jit(solution)/shard_map/ppermute | solution.py:353
  63.8 5.4 %received_blocks.7 = (bf16[169,6144]{1,0:T(8,128)(2,1)}, bf16[96,256]{1,0:T(8,128)(2,1)S(1)}) custom-call(s32[6]{0:T(128)S(1)} %stack.111.column_ref, bf16[304,256]{1,0:T(8,128)(2,1)S(1)} %collective-permute-done.17.refs_0_, bf16[304,256]{1,0:T(8,128)(2,1)S(1)} %collective-permute-done.18.refs_1_, ...), custom_call_target="tpu_custom_call", output_to_operand_aliasing={{0}: (13, {})} | custom-call | flops 3000000000 | bytes 1048576 | tf_op jit(solution)/shard_map/received_blocks/pallas_call | solution.py:270
  69.2 4.4 %own_blocks.1 = bf16[169,4096]{1,0:T(8,128)(2,1)} custom-call(s32[1,4096]{1,0:T(1,128)S(1)} %bitcast.41, f32[256,4096]{1,0:T(8,128)S(1)} %copy-done.29, bf16[256,256]{1,0:T(8,128)(2,1)S(1)} %copy-done.8, bf16[256,256]{1,0:T(8,128)(2,1)S(1)} %copy-done.11, bf16[169,256]{1,0:T(8,128)(2,1)S(1)} %copy-done.16, bf16[96,256]{1,0:T(8,128)(2,1)S(1)} %get-tuple-element.29.refs_0_, ...), custom_call_target="tpu_custom_call" | custom-call | flops 3000000000 | bytes 1048576 | tf_op jit(solution)/shard_map/own_blocks/pallas_call | solution.py:313
  (102 shorter events, 13.9 us)
Async XLA Ops:
  6.2 20.8 %copy-start.2 = (bf16[304,256]{1,0:T(8,128)(2,1)}, bf16[304,256]{1,0:T(8,128)(2,1)S(1)}, u32[]{:S(2)}) copy-start(bf16[304,256]{1,0:T(8,128)(2,1)S(1)} %get-tuple-element.27.own_ref.refs_0_) | copy-start | bytes 466948
  6.2 10.2 %collective-permute-start.5 = (bf16[304,256]{1,0:T(8,128)(2,1)S(1)}, bf16[304,256]{1,0:T(8,128)(2,1)S(1)}, u32[]{:S(2)}, u32[]{:S(2)}) collective-permute-start(bf16[304,256]{1,0:T(8,128)(2,1)S(1)} %get-tuple-element.30), channel_id=1, source_target_pairs={{0,2},{1,3},{2,0},{3,1},{4,6},{5,7},{6,4},{7,5},{8,10},{9,11},{10,... | collective-permute-start | bytes 466952 | tf_op jit(solution)/shard_map/ppermute | solution.py:353
  9.3 9.8 %collective-permute-start.2 = (bf16[304,256]{1,0:T(8,128)(2,1)S(1)}, bf16[304,256]{1,0:T(8,128)(2,1)S(1)}, u32[]{:S(2)}, u32[]{:S(2)}) collective-permute-start(bf16[304,256]{1,0:T(8,128)(2,1)S(1)} %get-tuple-element.27.own_ref.refs_0_), channel_id=1, source_target_pairs={{0,1},{1,0},{2,3},{3,2},{4,5},{5,4},{6,7},{7,6},{8,9},{9,8},{10,11... | collective-permute-start | bytes 466952 | tf_op jit(solution)/shard_map/ppermute | solution.py:353
  10.8 9.6 %collective-permute-start.1 = (bf16[304,256]{1,0:T(8,128)(2,1)S(1)}, bf16[304,256]{1,0:T(8,128)(2,1)S(1)}, u32[]{:S(2)}, u32[]{:S(2)}) collective-permute-start(bf16[304,256]{1,0:T(8,128)(2,1)S(1)} %get-tuple-element.27.own_ref.refs_0_), channel_id=1, source_target_pairs={{0,24},{1,25},{2,26},{3,27},{4,28},{5,29},{6,30},{7,31},{8,16},{9,... | collective-permute-start | bytes 466952 | tf_op jit(solution)/shard_map/ppermute | solution.py:353
  11.2 9.7 %collective-permute-start = (bf16[304,256]{1,0:T(8,128)(2,1)S(1)}, bf16[304,256]{1,0:T(8,128)(2,1)S(1)}, u32[]{:S(2)}, u32[]{:S(2)}) collective-permute-start(bf16[304,256]{1,0:T(8,128)(2,1)S(1)} %get-tuple-element.27.own_ref.refs_0_), channel_id=1, source_target_pairs={{0,8},{1,9},{2,10},{3,11},{4,12},{5,13},{6,14},{7,15},{8,0},{9,1},... | collective-permute-start | bytes 466952 | tf_op jit(solution)/shard_map/ppermute | solution.py:353
  12.4 22.0 %collective-permute-start.4 = (bf16[304,256]{1,0:T(8,128)(2,1)S(1)}, bf16[304,256]{1,0:T(8,128)(2,1)S(1)}, u32[]{:S(2)}, u32[]{:S(2)}) collective-permute-start(bf16[304,256]{1,0:T(8,128)(2,1)S(1)} %get-tuple-element.27.own_ref.refs_0_), channel_id=1, source_target_pairs={{0,25},{1,24},{2,27},{3,26},{4,29},{5,28},{6,31},{7,30},{8,17},{9,... | collective-permute-start | bytes 466952 | tf_op jit(solution)/shard_map/ppermute | solution.py:353
  16.4 15.3 %collective-permute-start.11 = (bf16[304,256]{1,0:T(8,128)(2,1)S(1)}, bf16[304,256]{1,0:T(8,128)(2,1)S(1)}, u32[]{:S(2)}, u32[]{:S(2)}) collective-permute-start(bf16[304,256]{1,0:T(8,128)(2,1)S(1)} %get-tuple-element.33), channel_id=1, source_target_pairs={{0,4},{1,5},{2,6},{3,7},{4,0},{5,1},{6,2},{7,3},{8,12},{9,13},{10,... | collective-permute-start | bytes 466952 | tf_op jit(solution)/shard_map/ppermute | solution.py:353
  19.1 14.7 %collective-permute-start.17 = (bf16[304,256]{1,0:T(8,128)(2,1)S(1)}, bf16[304,256]{1,0:T(8,128)(2,1)S(1)}, u32[]{:S(2)}, u32[]{:S(2)}) collective-permute-start(bf16[304,256]{1,0:T(8,128)(2,1)S(1)} %get-tuple-element.36), channel_id=1, source_target_pairs={{0,6},{1,7},{2,4},{3,5},{4,2},{5,3},{6,0},{7,1},{8,14},{9,15},{10,... | collective-permute-start | bytes 466952 | tf_op jit(solution)/shard_map/ppermute | solution.py:353
  20.4 14.5 %collective-permute-start.8 = (bf16[304,256]{1,0:T(8,128)(2,1)S(1)}, bf16[304,256]{1,0:T(8,128)(2,1)S(1)}, u32[]{:S(2)}, u32[]{:S(2)}) collective-permute-start(bf16[304,256]{1,0:T(8,128)(2,1)S(1)} %collective-permute-done.5.refs_0_), channel_id=1, source_target_pairs={{0,1},{1,0},{2,3},{3,2},{4,5},{5,4},{6,7},{7,6},{8,9},{9,8},{10,11... | collective-permute-start | bytes 466952 | tf_op jit(solution)/shard_map/ppermute | solution.py:353
  20.9 14.5 %collective-permute-start.3 = (bf16[304,256]{1,0:T(8,128)(2,1)S(1)}, bf16[304,256]{1,0:T(8,128)(2,1)S(1)}, u32[]{:S(2)}, u32[]{:S(2)}) collective-permute-start(bf16[304,256]{1,0:T(8,128)(2,1)S(1)} %collective-permute-done.2.refs_3_), channel_id=1, source_target_pairs={{0,8},{1,9},{2,10},{3,11},{4,12},{5,13},{6,14},{7,15},{8,0},{9,1},... | collective-permute-start | bytes 466952 | tf_op jit(solution)/shard_map/ppermute | solution.py:353
  31.8 12.6 %collective-permute-start.10 = (bf16[304,256]{1,0:T(8,128)(2,1)S(1)}, bf16[304,256]{1,0:T(8,128)(2,1)S(1)}, u32[]{:S(2)}, u32[]{:S(2)}) collective-permute-start(bf16[304,256]{1,0:T(8,128)(2,1)S(1)} %collective-permute-done.5.refs_0_), channel_id=1, source_target_pairs={{0,25},{1,24},{2,27},{3,26},{4,29},{5,28},{6,31},{7,30},{8,17},{9,... | collective-permute-start | bytes 466952 | tf_op jit(solution)/shard_map/ppermute | solution.py:353
  33.8 12.6 %collective-permute-start.7 = (bf16[304,256]{1,0:T(8,128)(2,1)S(1)}, bf16[304,256]{1,0:T(8,128)(2,1)S(1)}, u32[]{:S(2)}, u32[]{:S(2)}) collective-permute-start(bf16[304,256]{1,0:T(8,128)(2,1)S(1)} %collective-permute-done.5.refs_0_), channel_id=1, source_target_pairs={{0,24},{1,25},{2,26},{3,27},{4,28},{5,29},{6,30},{7,31},{8,16},{9,... | collective-permute-start | bytes 466952 | tf_op jit(solution)/shard_map/ppermute | solution.py:353
  34.4 12.6 %collective-permute-start.6 = (bf16[304,256]{1,0:T(8,128)(2,1)S(1)}, bf16[304,256]{1,0:T(8,128)(2,1)S(1)}, u32[]{:S(2)}, u32[]{:S(2)}) collective-permute-start(bf16[304,256]{1,0:T(8,128)(2,1)S(1)} %collective-permute-done.5.refs_0_), channel_id=1, source_target_pairs={{0,8},{1,9},{2,10},{3,11},{4,12},{5,13},{6,14},{7,15},{8,0},{9,1},... | collective-permute-start | bytes 466952 | tf_op jit(solution)/shard_map/ppermute | solution.py:353
  34.9 12.6 %collective-permute-start.14 = (bf16[304,256]{1,0:T(8,128)(2,1)S(1)}, bf16[304,256]{1,0:T(8,128)(2,1)S(1)}, u32[]{:S(2)}, u32[]{:S(2)}) collective-permute-start(bf16[304,256]{1,0:T(8,128)(2,1)S(1)} %collective-permute-done.11.refs_0_), channel_id=1, source_target_pairs={{0,1},{1,0},{2,3},{3,2},{4,5},{5,4},{6,7},{7,6},{8,9},{9,8},{10,11... | collective-permute-start | bytes 466952 | tf_op jit(solution)/shard_map/ppermute | solution.py:353
  35.4 12.6 %collective-permute-start.9 = (bf16[304,256]{1,0:T(8,128)(2,1)S(1)}, bf16[304,256]{1,0:T(8,128)(2,1)S(1)}, u32[]{:S(2)}, u32[]{:S(2)}) collective-permute-start(bf16[304,256]{1,0:T(8,128)(2,1)S(1)} %collective-permute-done.8.refs_3_), channel_id=1, source_target_pairs={{0,8},{1,9},{2,10},{3,11},{4,12},{5,13},{6,14},{7,15},{8,0},{9,1},... | collective-permute-start | bytes 466952 | tf_op jit(solution)/shard_map/ppermute | solution.py:353
  44.3 8.9 %collective-permute-start.16 = (bf16[304,256]{1,0:T(8,128)(2,1)S(1)}, bf16[304,256]{1,0:T(8,128)(2,1)S(1)}, u32[]{:S(2)}, u32[]{:S(2)}) collective-permute-start(bf16[304,256]{1,0:T(8,128)(2,1)S(1)} %collective-permute-done.11.refs_0_), channel_id=1, source_target_pairs={{0,25},{1,24},{2,27},{3,26},{4,29},{5,28},{6,31},{7,30},{8,17},{9,... | collective-permute-start | bytes 466952 | tf_op jit(solution)/shard_map/ppermute | solution.py:353
  46.4 8.9 %collective-permute-start.13 = (bf16[304,256]{1,0:T(8,128)(2,1)S(1)}, bf16[304,256]{1,0:T(8,128)(2,1)S(1)}, u32[]{:S(2)}, u32[]{:S(2)}) collective-permute-start(bf16[304,256]{1,0:T(8,128)(2,1)S(1)} %collective-permute-done.11.refs_0_), channel_id=1, source_target_pairs={{0,24},{1,25},{2,26},{3,27},{4,28},{5,29},{6,30},{7,31},{8,16},{9,... | collective-permute-start | bytes 466952 | tf_op jit(solution)/shard_map/ppermute | solution.py:353
  47.0 9.0 %collective-permute-start.12 = (bf16[304,256]{1,0:T(8,128)(2,1)S(1)}, bf16[304,256]{1,0:T(8,128)(2,1)S(1)}, u32[]{:S(2)}, u32[]{:S(2)}) collective-permute-start(bf16[304,256]{1,0:T(8,128)(2,1)S(1)} %collective-permute-done.11.refs_0_), channel_id=1, source_target_pairs={{0,8},{1,9},{2,10},{3,11},{4,12},{5,13},{6,14},{7,15},{8,0},{9,1},... | collective-permute-start | bytes 466952 | tf_op jit(solution)/shard_map/ppermute | solution.py:353
  47.5 8.9 %collective-permute-start.20 = (bf16[304,256]{1,0:T(8,128)(2,1)S(1)}, bf16[304,256]{1,0:T(8,128)(2,1)S(1)}, u32[]{:S(2)}, u32[]{:S(2)}) collective-permute-start(bf16[304,256]{1,0:T(8,128)(2,1)S(1)} %collective-permute-done.17.refs_0_), channel_id=1, source_target_pairs={{0,1},{1,0},{2,3},{3,2},{4,5},{5,4},{6,7},{7,6},{8,9},{9,8},{10,11... | collective-permute-start | bytes 466952 | tf_op jit(solution)/shard_map/ppermute | solution.py:353
  48.0 8.5 %collective-permute-start.15 = (bf16[304,256]{1,0:T(8,128)(2,1)S(1)}, bf16[304,256]{1,0:T(8,128)(2,1)S(1)}, u32[]{:S(2)}, u32[]{:S(2)}) collective-permute-start(bf16[304,256]{1,0:T(8,128)(2,1)S(1)} %collective-permute-done.14.refs_3_), channel_id=1, source_target_pairs={{0,8},{1,9},{2,10},{3,11},{4,12},{5,13},{6,14},{7,15},{8,0},{9,1},... | collective-permute-start | bytes 466952 | tf_op jit(solution)/shard_map/ppermute | solution.py:353
  53.2 8.4 %collective-permute-start.22 = (bf16[304,256]{1,0:T(8,128)(2,1)S(1)}, bf16[304,256]{1,0:T(8,128)(2,1)S(1)}, u32[]{:S(2)}, u32[]{:S(2)}) collective-permute-start(bf16[304,256]{1,0:T(8,128)(2,1)S(1)} %collective-permute-done.17.refs_0_), channel_id=1, source_target_pairs={{0,25},{1,24},{2,27},{3,26},{4,29},{5,28},{6,31},{7,30},{8,17},{9,... | collective-permute-start | bytes 466952 | tf_op jit(solution)/shard_map/ppermute | solution.py:353
  55.3 8.5 %collective-permute-start.19 = (bf16[304,256]{1,0:T(8,128)(2,1)S(1)}, bf16[304,256]{1,0:T(8,128)(2,1)S(1)}, u32[]{:S(2)}, u32[]{:S(2)}) collective-permute-start(bf16[304,256]{1,0:T(8,128)(2,1)S(1)} %collective-permute-done.17.refs_0_), channel_id=1, source_target_pairs={{0,24},{1,25},{2,26},{3,27},{4,28},{5,29},{6,30},{7,31},{8,16},{9,... | collective-permute-start | bytes 466952 | tf_op jit(solution)/shard_map/ppermute | solution.py:353
  56.0 7.8 %collective-permute-start.18 = (bf16[304,256]{1,0:T(8,128)(2,1)S(1)}, bf16[304,256]{1,0:T(8,128)(2,1)S(1)}, u32[]{:S(2)}, u32[]{:S(2)}) collective-permute-start(bf16[304,256]{1,0:T(8,128)(2,1)S(1)} %collective-permute-done.17.refs_0_), channel_id=1, source_target_pairs={{0,8},{1,9},{2,10},{3,11},{4,12},{5,13},{6,14},{7,15},{8,0},{9,1},... | collective-permute-start | bytes 466952 | tf_op jit(solution)/shard_map/ppermute | solution.py:353
  56.4 7.4 %collective-permute-start.21 = (bf16[304,256]{1,0:T(8,128)(2,1)S(1)}, bf16[304,256]{1,0:T(8,128)(2,1)S(1)}, u32[]{:S(2)}, u32[]{:S(2)}) collective-permute-start(bf16[304,256]{1,0:T(8,128)(2,1)S(1)} %collective-permute-done.20.refs_3_), channel_id=1, source_target_pairs={{0,8},{1,9},{2,10},{3,11},{4,12},{5,13},{6,14},{7,15},{8,0},{9,1},... | collective-permute-start | bytes 466952 | tf_op jit(solution)/shard_map/ppermute | solution.py:353
  (30 other events, 170.0 us)

commit v2 on v1

v2 whole, which is shorter than its diff:
```python
import functools

import jax
import jax.numpy as jnp
from jax import lax
from jax.experimental import pallas as pl
from jax.experimental.pallas import tpu as pltpu
from jax.sharding import PartitionSpec as P

cutoff = 8.0
PLANES = 5
LIST = 64
LIMIT = 36 << 20
BF16 = jnp.bfloat16
F32 = jnp.float32
AXES = ("strip", "cell")


def up(n, by):
    return -(-n // by) * by


def whole_div(x, by):
    return jnp.floor((x.astype(F32) + 0.5) * (1.0 / by)).astype(jnp.int32)


def dot(a, b, ca=1, cb=0):
    return lax.dot_general(a, b, (((ca,), (cb,)), ((), ())), preferred_element_type=F32)


def silu(x):
    half = 0.5 * x
    return half + half * jnp.tanh(half)


def onehot(index, count):
    rows = lax.broadcasted_iota(jnp.int32, (count, index.shape[1]), 0)
    return (rows == index).astype(BF16)


def gate_of(distance, w_in_t, w_out_t):
    count = w_in_t.shape[1]
    centers = lax.broadcasted_iota(jnp.int32, (count, 1), 0).astype(F32) * (cutoff / (count - 1))
    scaled = (distance - centers) * (count / (2.0 * cutoff))
    envelope = 0.5 * (jnp.cos(distance * (jnp.pi / cutoff)) + 1.0)
    basis = (jnp.exp(-scaled * scaled) * envelope).astype(BF16)
    radial = silu(dot(w_in_t, basis)).astype(BF16)
    return dot(w_out_t, radial)


def whole(a):
    return pl.BlockSpec(a.shape, lambda *_: (0,) * a.ndim)


def far(*arrays):
    return [pltpu.with_memory_space_constraint(a, pltpu.HBM) for a in arrays]


def cost(flops, nbytes=1 << 20):
    return pl.CostEstimate(flops=flops, bytes_accessed=nbytes, transcendentals=0)


class Sizes:
    def __init__(self, features, pair_atom, send_rows, w_radial_in, w_out):
        self.atoms, self.width = features.shape
        self.pairs = pair_atom.shape[0]
        self.cells, self.fetch = send_rows.shape
        self.strips = lax.axis_size("strip")
        self.inner = 2
        self.outer = self.cells // 2
        self.slot = self.pairs // (2 * self.cells)
        self.part = self.fetch // 3
        self.groups = 3 * self.inner
        self.meta = PLANES * self.groups
        self.per_row = self.width // LIST
        self.rows = up(self.atoms + self.meta + -(-self.cells // self.per_row), 16)
        self.entries = w_out.shape[1]
        self.orbitals = int(self.entries**0.5 + 0.5)


def where_am_i():
    strip, cell = lax.axis_index("strip"), lax.axis_index("cell")
    even = lax.rem(strip, 2) == 0
    return cell, lax.div(cell, 2), lax.rem(cell, 2), even


def tiles_kernel(n, atom_ref, row_ref, slot_ref, dist_ref, list_ref, feat_ref, *outs):
    _, zi, xi, even = where_am_i()
    slot = slot_ref[...]
    hi = whole_div(slot, n.slot)
    lo = slot - hi * n.slot
    row = row_ref[...]
    k = row - whole_div(row, n.fetch) * n.fetch
    dist = dist_ref[...]
    d1 = dist.astype(BF16)
    rest = dist - d1.astype(F32)
    d2 = rest.astype(BF16)
    d3 = (rest - d2.astype(F32)).astype(BF16)
    planes = [
        d1.astype(F32),
        d2.astype(F32),
        d3.astype(F32),
        (atom_ref[...] + 1).astype(F32),
        whole_div(k, 3).astype(F32),
    ]
    total = 3 * n.cells
    mask = lax.broadcasted_iota(jnp.int32, (total, n.pairs), 0) == hi
    spread = jnp.concatenate([jnp.where(mask, p, 0.0) for p in planes], 0).astype(BF16)
    placed = dot(spread, onehot(lo, n.slot), 1, 1).astype(BF16)
    tail = n.rows - n.atoms
    shape = (tail, PLANES * total)
    r = lax.broadcasted_iota(jnp.int32, shape, 0)
    q = lax.broadcasted_iota(jnp.int32, shape, 1)
    g = whole_div(r, PLANES)
    plane = r - g * PLANES
    role = whole_div(g, n.inner)
    o = jnp.where(role == 0, 1, jnp.where((role == 1) == even, 2, 0))
    base = plane * total + o * n.cells + jnp.bitwise_xor(g - role * n.inner, xi)
    base = jnp.where(r < n.meta, base, -n.pairs)
    e = list_ref[...]
    kk = lax.broadcasted_iota(jnp.int32, e.shape, 1)
    e = (e - (kk - whole_div(kk, 3) * 3) * n.atoms).astype(F32)
    wide = jnp.concatenate([e, jnp.zeros((n.cells, LIST - n.fetch), F32)], 1)
    flat = jnp.concatenate([wide] * n.per_row, 1)
    j = lax.broadcasted_iota(jnp.int32, flat.shape, 0)
    lane = lax.broadcasted_iota(jnp.int32, flat.shape, 1)
    at_row = whole_div(j, n.per_row)
    flat = jnp.where(whole_div(lane, LIST) == j - at_row * n.per_row, flat, 0.0).astype(BF16)
    put_r = lax.broadcasted_iota(jnp.int32, (tail, n.cells), 0)
    put_j = lax.broadcasted_iota(jnp.int32, (tail, n.cells), 1)
    put = (put_r == n.meta + whole_div(put_j, n.per_row)).astype(BF16)
    lists = dot(put, flat)
    feat = feat_ref[...]
    for b, out in enumerate(outs):
        zz = jnp.bitwise_xor(zi, b)
        pick = (base + zz * n.inner == q).astype(BF16)
        out[0 : n.atoms, :] = feat
        pairs = dot(pick, placed)
        if n.slot < n.width:
            pairs = jnp.concatenate([pairs, jnp.zeros((tail, n.width - n.slot), F32)], 1)
        out[n.atoms :, :] = (pairs + lists).astype(BF16)


def lists_of(n, tile):
    tail = tile[n.atoms :, :].astype(F32)
    rows = []
    for j in range(n.cells):
        r = n.meta + j // n.per_row
        lane = LIST * (j % n.per_row)
        rows.append(tail[r : r + 1, lane : lane + n.fetch])
    return jnp.concatenate(rows, 0)


def make_tiles(n, pair_atom, partner_row, transpose_slot, distance, send_rows, features):
    args = (pair_atom, partner_row, transpose_slot, distance, send_rows, features)
    return pl.pallas_call(
        functools.partial(tiles_kernel, n),
        out_shape=[jax.ShapeDtypeStruct((n.rows, n.width), BF16)] * n.outer,
        compiler_params=pltpu.CompilerParams(vmem_limit_bytes=LIMIT),
        cost_estimate=cost(600_000_000),
        name="place_pairs",
    )(*far(*args))


def own_gate_kernel(n, dist_ref, atom_ref, feat_ref, *refs):
    sources, held_ref, flipped, left_ref = refs[:6], refs[6], refs[7:13], refs[13]

    @pl.when(pl.program_id(0) == 0)
    def _():
        for src, dst in zip(sources[:5], flipped[:5]):
            dst[...] = src[...].T
        r = lax.broadcasted_iota(jnp.int32, (n.entries, n.entries), 0)
        q = lax.broadcasted_iota(jnp.int32, (n.entries, n.entries), 1)
        first = whole_div(r, n.orbitals)
        swap = (q == (r - first * n.orbitals) * n.orbitals + first).astype(BF16)
        flipped[5][...] = dot(swap, sources[5][...]).astype(BF16)
        left_ref[...] = dot(flipped[0][...], feat_ref[...], 1, 1).astype(BF16)

    gate = gate_of(dist_ref[...], flipped[2][...], flipped[3][...])
    held_ref[...] = gate * dot(left_ref[...], onehot(atom_ref[...], n.atoms))


def own_gate(n, step, distance, pair_atom, features, weights):
    row = pl.BlockSpec((1, step), lambda i: (0, i))
    turned = [jax.ShapeDtypeStruct(w.shape[::-1], BF16) for w in weights[:5]]
    turned.append(jax.ShapeDtypeStruct(weights[5].shape, BF16))
    out = pl.pallas_call(
        functools.partial(own_gate_kernel, n),
        grid=(n.pairs // step,),
        in_specs=[row, row] + [whole(a) for a in (features, *weights)],
        out_specs=[pl.BlockSpec((n.width, step), lambda i: (0, i))] + [whole(a) for a in turned],
        out_shape=[jax.ShapeDtypeStruct((n.width, n.pairs), F32)] + turned,
        scratch_shapes=[pltpu.VMEM((n.width, n.atoms), BF16)],
        compiler_params=pltpu.CompilerParams(vmem_limit_bytes=LIMIT),
        cost_estimate=cost(3_000_000_000),
        name="own_gate",
    )(*far(distance, pair_atom, features, *weights))
    return out[0], out[1:]


def partner_table(n, even, tiles, w_right_t, table_ref):
    right = dot(w_right_t, tiles[0][0 : n.atoms, :], 1, 1).astype(BF16)
    lanes = n.cells * n.part
    k = lax.broadcasted_iota(jnp.int32, (n.fetch, lanes), 0)
    lane = lax.broadcasted_iota(jnp.int32, (n.fetch, lanes), 1)
    m3 = (lane - whole_div(lane, n.part) * n.part) * 3
    mine = lax.broadcasted_iota(jnp.int32, (n.cells, lanes), 0)
    cell = whole_div(lax.broadcasted_iota(jnp.int32, (n.cells, lanes), 1), n.part)
    o_sib = jnp.where(even, 0, 2)
    for role, o in enumerate((1, o_sib, 2 - o_sib)):
        lists = lists_of(n, tiles[role]).astype(BF16)
        per = dot(lists, (k == m3 + o).astype(BF16))
        index = jnp.sum(jnp.where(mine == cell, per, 0.0), 0, keepdims=True)
        table_ref[role] = dot(right, onehot(index.astype(jnp.int32), n.atoms)).astype(BF16)


def received_kernel(n, steps, first, direct, count, *refs):
    held, refs = refs[:count], refs[count:]
    if not first and direct:
        refs = refs[1:]
    outs, refs = refs[: 3 if first else 2], refs[3 if first else 2 :]
    blocks_buf, sem_out = refs
    block_ref, rows_buf = outs[:2]
    need = held.__getitem__

    me, zi, xi, even = where_am_i()
    o_sib = jnp.where(even, 0, 2)
    roles = (1, o_sib, 2 - o_sib)
    base = 6 * len(steps)
    near = [(i, at) for i in range(len(steps)) for at in range(n.inner)]
    order = [(role, i, at) for role in range(3) for i, at in near]
    number = {key: g for g, key in enumerate(order)}
    cells = {
        (i, at): jnp.bitwise_xor(zi, steps[i]) * n.inner + jnp.bitwise_xor(xi, at) for i, at in near
    }
    tiles = {(role, i, at): need(6 * i + 3 * at + role) for role, i, at in order}
    done = []
    if first:
        own = [tiles[role, 0, 0] for role in range(3)]
        table = outs[2]
        partner_table(n, even, own, need(base + 5)[...], table)
    else:
        table = need(base + 5)
    feats = jnp.concatenate([tiles[key][0 : n.atoms, :] for key in order], 0)
    left = dot(need(base)[...], feats, 1, 1).astype(BF16)

    slabs = []
    for role, i, at in order:
        top = (role * n.inner + at) * PLANES
        tail = tiles[role, i, at][n.atoms :, 0 : n.slot].astype(F32)
        slabs.append(tail[top : top + PLANES])
    meta = jnp.concatenate(slabs, 1)
    dists = meta[0:1] + meta[1:2] + meta[2:3]
    atoms = meta[3:4].astype(jnp.int32) - 1
    spots = meta[4:5].astype(jnp.int32)

    def cut(x, g):
        return x[:, g * n.slot : (g + 1) * n.slot]

    gate = gate_of(dists, need(base + 1)[...], need(base + 2)[...])
    rights = []
    for role in range(3):
        place = [cut(spots, number[role, i, at]) + cells[i, at] * n.part for i, at in near]
        rights.append(dot(table[role], onehot(jnp.concatenate(place, 1), n.cells * n.part)))
    lefts = [
        dot(left[:, g * n.atoms : (g + 1) * n.atoms], onehot(cut(atoms, g), n.atoms))
        for g in range(len(order))
    ]
    edge = jnp.concatenate(lefts, 1) * jnp.concatenate(rights, 1) * gate
    mixed = silu(dot(need(base + 3)[...], edge.astype(BF16))).astype(BF16)
    blocks_buf[...] = dot(need(base + 4)[...], mixed).astype(BF16)
    if direct:
        for g, (role, i, at) in enumerate(order):
            place = roles[role] * n.cells + cells[i, at]
            start = pl.multiple_of(place * n.slot, n.slot)
            out = pltpu.make_async_copy(
                blocks_buf.at[:, pl.ds(g * n.slot, n.slot)],
                block_ref.at[:, pl.ds(start, n.slot)],
                sem_out.at[g],
            )
            out.start()
            done.append(out)

    rows = len(order) * n.part
    mine = lax.broadcasted_iota(jnp.int32, (n.cells, n.fetch), 0) == me
    index = []
    k = lax.broadcasted_iota(jnp.int32, (n.part, n.fetch), 1)
    m3 = 3 * lax.broadcasted_iota(jnp.int32, (n.part, n.fetch), 0)
    asked = {}
    for i, at in near:
        lists = lists_of(n, tiles[0, i, at])
        asked[i, at] = jnp.sum(jnp.where(mine, lists, 0.0), 0, keepdims=True)
    for g, (role, i, at) in enumerate(order):
        o_own = 1 if role == 0 else 2 - roles[role]
        here = jnp.sum(jnp.where(k == m3 + o_own, asked[i, at], 0.0), 1, keepdims=True)
        index.append(here.astype(jnp.int32) + g * n.atoms)
    lane = lax.broadcasted_iota(jnp.int32, (rows, len(order) * n.atoms), 1)
    pick = (lane == jnp.concatenate(index, 0)).astype(BF16)
    rows_buf[...] = dot(pick, feats).astype(BF16)
    if not direct:
        out = pltpu.make_async_copy(blocks_buf, block_ref, sem_out.at[0])
        out.start()
        done.append(out)
    for out in done:
        out.wait()


def received(n, steps, tiles, weights, table, w_right_t, into):
    first = table is None
    direct = n.slot % 128 == 0
    operands = list(tiles) + list(weights) + [w_right_t if first else table]
    count = len(operands)
    blocks = (n.entries, 6 * len(steps) * n.slot)
    rows = (6 * len(steps) * n.part, n.width)
    shape = (3, n.width, n.cells * n.part)
    out_shape = [
        jax.ShapeDtypeStruct((n.entries, 3 * n.cells * n.slot) if direct else blocks, BF16),
        jax.ShapeDtypeStruct(rows, BF16),
    ]
    if first:
        out_shape.append(jax.ShapeDtypeStruct(shape, BF16))
    aliases = {}
    if direct and not first:
        aliases = {count: 0}
        operands.append(into)
    out = pl.pallas_call(
        functools.partial(received_kernel, n, steps, first, direct, count),
        in_specs=[pl.BlockSpec(memory_space=pltpu.VMEM)] * count + [pl.BlockSpec(memory_space=pl.ANY)] * (len(operands) - count),
        out_specs=[pl.BlockSpec(memory_space=pl.ANY)] + [pl.BlockSpec(memory_space=pltpu.VMEM)] * (len(out_shape) - 1),
        out_shape=out_shape,
        scratch_shapes=[
            pltpu.VMEM(blocks, BF16),
            pltpu.SemaphoreType.DMA((6 * len(steps),)),
        ],
        input_output_aliases=aliases,
        compiler_params=pltpu.CompilerParams(vmem_limit_bytes=LIMIT),
        cost_estimate=cost(3_000_000_000 * len(steps)),
        name="received_blocks",
    )(*operands)
    return out[0], out[1], out[2] if first else table


def own_blocks_kernel(n, per_call, row_ref, held_ref, w_right_ref, w_mix_ref, w_out_ref, *refs):
    tables, out_ref, right_ref = refs[:-2], refs[-2], refs[-1]
    _, zi, xi, even = where_am_i()

    @pl.when(pl.program_id(0) == 0)
    def _():
        rows = jnp.concatenate([t[...] for t in tables], 0)
        right_ref[...] = dot(w_right_ref[...], rows, 1, 1).astype(BF16)

    v = row_ref[...]
    q = whole_div(v, n.fetch)
    k = v - q * n.fetch
    m = whole_div(k, 3)
    o = k - 3 * m
    sibling = jnp.where(even, 2, 0)
    role = jnp.where(o == 1, 0, jnp.where(o == sibling, 1, 2))
    outer = whole_div(q, n.inner)
    inner = q - outer * n.inner
    b = jnp.bitwise_xor(outer, zi)
    call = whole_div(b, per_call)
    place = (call * 3 + role) * per_call + b - call * per_call
    place = place * n.inner + jnp.bitwise_xor(inner, xi)
    right = dot(right_ref[...], onehot(place * n.part + m, right_ref.shape[1]))
    edge = (held_ref[...] * right).astype(BF16)
    mixed = silu(dot(w_mix_ref[...], edge)).astype(BF16)
    out_ref[...] = dot(w_out_ref[...], mixed).astype(BF16)


def own_blocks_of(n, step, partner_row, held, w_right_t, w_mix_t, w_out_t, tables):
    return pl.pallas_call(
        functools.partial(own_blocks_kernel, n, n.outer // len(tables)),
        grid=(n.pairs // step,),
        in_specs=[
            pl.BlockSpec((1, step), lambda i: (0, i)),
            pl.BlockSpec((n.width, step), lambda i: (0, i)),
        ]
        + [whole(a) for a in (w_right_t, w_mix_t, w_out_t, *tables)],
        out_specs=pl.BlockSpec((n.entries, step), lambda i: (0, i)),
        out_shape=jax.ShapeDtypeStruct((n.entries, n.pairs), BF16),
        scratch_shapes=[pltpu.VMEM((n.width, 3 * n.cells * n.part), BF16)],
        compiler_params=pltpu.CompilerParams(vmem_limit_bytes=LIMIT),
        cost_estimate=cost(3_000_000_000),
        name="own_blocks",
    )(*far(partner_row), held, w_right_t, w_mix_t, w_out_t, *tables)


def body(
    features,
    pair_atom,
    partner_row,
    transpose_slot,
    distance,
    send_rows,
    w_left,
    w_right,
    w_radial_in,
    w_radial_out,
    w_mix,
    w_out,
):
    n = Sizes(features, pair_atom, send_rows, w_radial_in, w_out)
    lines = n.strips * n.cells

    def exchange(x, partner):
        pairs = []
        for i in range(lines):
            s, c = partner(i // n.cells, i % n.cells)
            pairs.append((i, s * n.cells + c))
        return lax.ppermute(x, AXES, pairs)

    def along(by):
        return lambda s, c: (s, c ^ (by * n.inner))

    def beside(s, c):
        return s, c ^ 1

    def sibling(s, c):
        return s ^ 1, c

    def other(s, c):
        return (s - 1 if s % 2 == 0 else s + 1) % n.strips, c

    def corner(s, c):
        return other(s, c)[0], c ^ 1

    row = lambda a: a.reshape(1, -1)
    pair_atom, partner_row = row(pair_atom), row(partner_row)
    transpose_slot, distance = row(transpose_slot), row(distance)
    tiles = make_tiles(
        n, pair_atom, partner_row, transpose_slot, distance, send_rows, features
    )
    lines_in = [tiles[0]] + [exchange(tiles[b], along(b)) for b in range(1, n.outer)]
    step = n.pairs // 2
    held, turned = own_gate(
        n,
        step,
        distance,
        pair_atom,
        features,
        (w_left, w_right, w_radial_in, w_radial_out, w_mix, w_out.T),
    )
    w_left_t, w_right_t, w_in_t, w_ro_t, w_mix_t, w_flip_t = turned
    weights = (w_left_t, w_in_t, w_ro_t, w_mix_t, w_flip_t)
    table, into, tables, parts = None, None, [], []
    half = 1
    for at in range(0, n.outer, half):
        steps, group = tuple(range(at, at + half)), []
        for b in steps:
            tile = lines_in[b]
            across = exchange(tile, beside)
            group += [
                tile,
                exchange(tile, sibling),
                exchange(tile, other),
                across,
                exchange(across, sibling),
                exchange(tile, corner),
            ]
        into, rows, table = received(n, steps, group, weights, table, w_right_t, into)
        tables.append(rows)
        parts.append((steps, into))
    if n.slot % 128:
        cell, strip = lax.axis_index("cell"), lax.axis_index("strip")
        o_sib = jnp.where(strip % 2 == 0, 0, 2)
        into = jnp.zeros((n.entries, 3 * n.cells * n.slot), BF16)
        for steps, blocks in parts:
            order = [(o, b, at) for o in (1, o_sib, 2 - o_sib) for b in steps for at in (0, 1)]
            for g, (o, b, at) in enumerate(order):
                piece = blocks[:, g * n.slot : (g + 1) * n.slot]
                spot = o * n.cells + (cell ^ (b * n.inner + at))
                into = lax.dynamic_update_slice(into, piece, (0, spot * n.slot))
    own = own_blocks_of(n, step, partner_row, held, w_right_t, w_mix_t, w_out.T, tables)
    return own, into


def solution(mesh):
    split = P(("strip", "cell"))
    wide = P(("strip", "cell"), None)
    in_specs = (wide, split, split, split, split, wide) + (P(),) * 6
    out_specs = (P(None, ("strip", "cell")), P(None, ("strip", "cell")))
    return jax.shard_map(body, mesh=mesh, in_specs=in_specs, out_specs=out_specs, check_vma=False)
```

time: 74.3 us -> 58.3 us (0.78)
  local copies, waits for them, and re-layouts: 14.8 us -> 0.01 us
  Pallas kernels: 34.4 us -> 23.3 us
  waiting for transfers between devices: 3.33 us -> 11.2 us
  starting transfers between devices: 20.2 us -> 22.7 us
    unnamed x63 -> x2, local copies, waits for them, and re-layouts: 13.6 us -> 0.01 us
    pallas_call x8 -> x6, Pallas kernels: 33.3 us -> 21.2 us  [the longest x4 11.7 us: received(): pl.pallas_call(functools.partial(received_kernel, n, steps, first, direct...]
    ppermute x23, waiting for transfers between devices: 3.33 us -> 11.2 us  [exchange(): return lax.ppermute(x, AXES, pairs)]
    ppermute x23, starting transfers between devices: 20.2 us -> 22.7 us  [exchange(): return lax.ppermute(x, AXES, pairs)]
    pallas_call x1, Pallas kernels: 1.08 us -> 2.1 us  [make_tiles(): pl.pallas_call(functools.partial(tiles_kernel, n), out_shape=[jax.ShapeDt...]
    reshape x4 -> x0, local copies, waits for them, and re-layouts: 0.88 us -> none  [body(): w_out.reshape(-1, orbitals, orbitals).swapaxes(1, 2).reshape(w_out.shape)]
  transfers between devices with their start and end apart: 23 -> 23, of which waited for: 2 -> 4; matrix products, arithmetic and copies ran while one was open for 3% -> 0% of each run, Pallas kernels for 32% -> 23%
where the time goes in v2:
time: 58.3 us; the launch traced here: 57.9 us
  Pallas kernels  23.3 us (40%)
  starting transfers between devices  22.7 us (39%)
  waiting for transfers between devices  11.2 us (19%)
  between operations  0.75 us (1%)
    ppermute x23, starting transfers between devices, exchange(): return lax.ppermute(x, AXES, pairs)  22.7 us
    pallas_call x4, Pallas kernels, received(): pl.pallas_call(functools.partial(received_kernel, n, steps, first, direct...  11.7 us
    ppermute x23, waiting for transfers between devices, exchange(): return lax.ppermute(x, AXES, pairs)  11.2 us
    pallas_call x1, Pallas kernels, own_blocks_of(): pl.pallas_call(functools.partial(own_blocks_kernel, n, n.outer // len(tab...  4.88 us
    pallas_call x1, Pallas kernels, own_gate(): pl.pallas_call(functools.partial(own_gate_kernel, n), grid=(n.pairs // st...  4.65 us
    pallas_call x1, Pallas kernels, make_tiles(): pl.pallas_call(functools.partial(tiles_kernel, n), out_shape=[jax.ShapeDt...  2.1 us
  transfers between devices with their start and end apart: 23, of which 4 were waited for; matrix products, arithmetic and copies ran while one was open for 0% of the time, Pallas kernels for 23%

profile of v2, /device:TPU:0, one launch (start us, length us, event | category | flops | bytes accessed | tf_op | source)
XLA Modules:
  0.0 57.9 jit_solution(2454957390735171875)
XLA Ops:
  0.6 2.1 %place_pairs.1 = (bf16[288,256]{1,0:T(8,128)(2,1)S(1)}, bf16[288,256]{1,0:T(8,128)(2,1)S(1)}, bf16[288,256]{1,0:T(8,128)(2,1)S(1)}, bf16[288,256]{1,0:T(8,128)(2,1)S(1)}) custom-call(s32[1,4096]{1,0:T(1,128)} %bitcast.10, s32[1,4096]{1,0:T(1,128)} %bitcast.12, s32[1,4096]{1,0:T(1,128)} %bitcast.7, f32[1,4096]{1,0:T(1,128)} %bitcast.8, s32[8,48]{1,0:T(8,128)} %list_ref.1, ...), custom_call_target="tpu_custom_call" | custom-call | flops 600000000 | bytes 1048576 | tf_op jit(solution)/shard_map/place_pairs/pallas_call | solution.py:156
  3.3 2.6 %collective-permute-start.1 = (bf16[288,256]{1,0:T(8,128)(2,1)S(1)}, bf16[288,256]{1,0:T(8,128)(2,1)S(1)}, u32[]{:S(2)}, u32[]{:S(2)}) collective-permute-start(bf16[288,256]{1,0:T(8,128)(2,1)S(1)} %get-tuple-element.25.refs_0_), channel_id=1, source_target_pairs={{0,24},{1,25},{2,26},{3,27},{4,28},{5,29},{6,30},{7,31},{8,16},{9,... | collective-permute-start | bytes 442376 | tf_op jit(solution)/shard_map/ppermute | solution.py:411
  5.9 1.5 %collective-permute-start.2 = (bf16[288,256]{1,0:T(8,128)(2,1)S(1)}, bf16[288,256]{1,0:T(8,128)(2,1)S(1)}, u32[]{:S(2)}, u32[]{:S(2)}) collective-permute-start(bf16[288,256]{1,0:T(8,128)(2,1)S(1)} %get-tuple-element.25.refs_0_), channel_id=1, source_target_pairs={{0,1},{1,0},{2,3},{3,2},{4,5},{5,4},{6,7},{7,6},{8,9},{9,8},{10,11... | collective-permute-start | bytes 442376 | tf_op jit(solution)/shard_map/ppermute | solution.py:411
  7.4 1.6 %collective-permute-start.5 = (bf16[288,256]{1,0:T(8,128)(2,1)S(1)}, bf16[288,256]{1,0:T(8,128)(2,1)S(1)}, u32[]{:S(2)}, u32[]{:S(2)}) collective-permute-start(bf16[288,256]{1,0:T(8,128)(2,1)S(1)} %get-tuple-element.31), channel_id=1, source_target_pairs={{0,2},{1,3},{2,0},{3,1},{4,6},{5,7},{6,4},{7,5},{8,10},{9,11},{10,... | collective-permute-start | bytes 442376 | tf_op jit(solution)/shard_map/ppermute | solution.py:411
  9.0 2.6 %collective-permute-start.11 = (bf16[288,256]{1,0:T(8,128)(2,1)S(1)}, bf16[288,256]{1,0:T(8,128)(2,1)S(1)}, u32[]{:S(2)}, u32[]{:S(2)}) collective-permute-start(bf16[288,256]{1,0:T(8,128)(2,1)S(1)} %get-tuple-element.35), channel_id=1, source_target_pairs={{0,4},{1,5},{2,6},{3,7},{4,0},{5,1},{6,2},{7,3},{8,12},{9,13},{10,... | collective-permute-start | bytes 442376 | tf_op jit(solution)/shard_map/ppermute | solution.py:411
  11.6 1.9 %collective-permute-start.17 = (bf16[288,256]{1,0:T(8,128)(2,1)S(1)}, bf16[288,256]{1,0:T(8,128)(2,1)S(1)}, u32[]{:S(2)}, u32[]{:S(2)}) collective-permute-start(bf16[288,256]{1,0:T(8,128)(2,1)S(1)} %get-tuple-element.38), channel_id=1, source_target_pairs={{0,6},{1,7},{2,4},{3,5},{4,2},{5,3},{6,0},{7,1},{8,14},{9,15},{10,... | collective-permute-start | bytes 442376 | tf_op jit(solution)/shard_map/ppermute | solution.py:411
  13.9 1.5 %collective-permute-start.8 = (bf16[288,256]{1,0:T(8,128)(2,1)S(1)}, bf16[288,256]{1,0:T(8,128)(2,1)S(1)}, u32[]{:S(2)}, u32[]{:S(2)}) collective-permute-start(bf16[288,256]{1,0:T(8,128)(2,1)S(1)} %collective-permute-done.5.refs_0_), channel_id=1, source_target_pairs={{0,1},{1,0},{2,3},{3,2},{4,5},{5,4},{6,7},{7,6},{8,9},{9,8},{10,11... | collective-permute-start | bytes 442376 | tf_op jit(solution)/shard_map/ppermute | solution.py:411
  15.4 4.7 %own_gate.1 = (f32[256,4096]{1,0:T(8,128)S(1)}, bf16[256,256]{1,0:T(8,128)(2,1)S(1)}, bf16[256,256]{1,0:T(8,128)(2,1)S(1)}, bf16[256,128]{1,0:T(8,128)(2,1)S(1)}...) custom-call(f32[1,4096]{1,0:T(1,128)} %bitcast.9, s32[1,4096]{1,0:T(1,128)} %bitcast.11, ...), custom_call_target="tpu_custom_call" | custom-call | flops 3000000000 | bytes 1048576 | tf_op jit(solution)/shard_map/own_gate/pallas_call | solution.py:187
  20.2 2.7 %collective-permute-done.11.refs_0_ = bf16[288,256]{1,0:T(8,128)(2,1)S(1)} collective-permute-done((bf16[288,256]{1,0:T(8,128)(2,1)S(1)}, bf16[288,256]{1,0:T(8,128)(2,1)S(1)}, u32[]{:S(2)}, u32[]{:S(2)}) %collective-permute-start.11) | collective-permute-done | bytes 147488 | tf_op jit(solution)/shard_map/ppermute | solution.py:411
  22.8 0.9 %collective-permute-start.7 = (bf16[288,256]{1,0:T(8,128)(2,1)S(1)}, bf16[288,256]{1,0:T(8,128)(2,1)S(1)}, u32[]{:S(2)}, u32[]{:S(2)}) collective-permute-start(bf16[288,256]{1,0:T(8,128)(2,1)S(1)} %collective-permute-done.5.refs_0_), channel_id=1, source_target_pairs={{0,24},{1,25},{2,26},{3,27},{4,28},{5,29},{6,30},{7,31},{8,16},{9,... | collective-permute-start | bytes 442376 | tf_op jit(solution)/shard_map/ppermute | solution.py:411
  23.7 1.5 %collective-permute-start.10 = (bf16[288,256]{1,0:T(8,128)(2,1)S(1)}, bf16[288,256]{1,0:T(8,128)(2,1)S(1)}, u32[]{:S(2)}, u32[]{:S(2)}) collective-permute-start(bf16[288,256]{1,0:T(8,128)(2,1)S(1)} %collective-permute-done.5.refs_0_), channel_id=1, source_target_pairs={{0,25},{1,24},{2,27},{3,26},{4,29},{5,28},{6,31},{7,30},{8,17},{9,... | collective-permute-start | bytes 442376 | tf_op jit(solution)/shard_map/ppermute | solution.py:411
  25.2 0.9 %collective-permute-start.14 = (bf16[288,256]{1,0:T(8,128)(2,1)S(1)}, bf16[288,256]{1,0:T(8,128)(2,1)S(1)}, u32[]{:S(2)}, u32[]{:S(2)}) collective-permute-start(bf16[288,256]{1,0:T(8,128)(2,1)S(1)} %collective-permute-done.11.refs_0_), channel_id=1, source_target_pairs={{0,1},{1,0},{2,3},{3,2},{4,5},{5,4},{6,7},{7,6},{8,9},{9,8},{10,11... | collective-permute-start | bytes 442376 | tf_op jit(solution)/shard_map/ppermute | solution.py:411
  26.1 3.1 %received_blocks.4 = (bf16[169,6144]{1,0:T(8,128)(2,1)}, bf16[96,256]{1,0:T(8,128)(2,1)S(1)}, bf16[3,256,128]{2,1,0:T(8,128)(2,1)S(1)}) custom-call(bf16[288,256]{1,0:T(8,128)(2,1)S(1)} %get-tuple-element.25.refs_0_, bf16[288,256]{1,0:T(8,128)(2,1)S(1)} %collective-permute-done.refs_1_, bf16[288,256]{1,0:T(8,128)(2,1)S(1)} %collective-permute-done.1.refs_2_, ...), custom_call_target="tpu_custom_call" | custom-call | flops 3000000000 | bytes 1048576 | tf_op jit(solution)/shard_map/received_blocks/pallas_call | solution.py:326
  29.8 2.1 %collective-permute-done.7.refs_2_ = bf16[288,256]{1,0:T(8,128)(2,1)S(1)} collective-permute-done((bf16[288,256]{1,0:T(8,128)(2,1)S(1)}, bf16[288,256]{1,0:T(8,128)(2,1)S(1)}, u32[]{:S(2)}, u32[]{:S(2)}) %collective-permute-start.7) | collective-permute-done | bytes 147488 | tf_op jit(solution)/shard_map/ppermute | solution.py:411
  31.8 1.2 %collective-permute-start.13 = (bf16[288,256]{1,0:T(8,128)(2,1)S(1)}, bf16[288,256]{1,0:T(8,128)(2,1)S(1)}, u32[]{:S(2)}, u32[]{:S(2)}) collective-permute-start(bf16[288,256]{1,0:T(8,128)(2,1)S(1)} %collective-permute-done.11.refs_0_), channel_id=1, source_target_pairs={{0,24},{1,25},{2,26},{3,27},{4,28},{5,29},{6,30},{7,31},{8,16},{9,... | collective-permute-start | bytes 442376 | tf_op jit(solution)/shard_map/ppermute | solution.py:411
  33.0 1.1 %collective-permute-start.16 = (bf16[288,256]{1,0:T(8,128)(2,1)S(1)}, bf16[288,256]{1,0:T(8,128)(2,1)S(1)}, u32[]{:S(2)}, u32[]{:S(2)}) collective-permute-start(bf16[288,256]{1,0:T(8,128)(2,1)S(1)} %collective-permute-done.11.refs_0_), channel_id=1, source_target_pairs={{0,25},{1,24},{2,27},{3,26},{4,29},{5,28},{6,31},{7,30},{8,17},{9,... | collective-permute-start | bytes 442376 | tf_op jit(solution)/shard_map/ppermute | solution.py:411
  34.1 0.9 %collective-permute-start.20 = (bf16[288,256]{1,0:T(8,128)(2,1)S(1)}, bf16[288,256]{1,0:T(8,128)(2,1)S(1)}, u32[]{:S(2)}, u32[]{:S(2)}) collective-permute-start(bf16[288,256]{1,0:T(8,128)(2,1)S(1)} %collective-permute-done.17.refs_0_), channel_id=1, source_target_pairs={{0,1},{1,0},{2,3},{3,2},{4,5},{5,4},{6,7},{7,6},{8,9},{9,8},{10,11... | collective-permute-start | bytes 442376 | tf_op jit(solution)/shard_map/ppermute | solution.py:411
  35.1 2.9 %received_blocks.5 = (bf16[169,6144]{1,0:T(8,128)(2,1)}, bf16[96,256]{1,0:T(8,128)(2,1)S(1)}) custom-call(bf16[288,256]{1,0:T(8,128)(2,1)S(1)} %collective-permute-done.5.refs_0_, bf16[288,256]{1,0:T(8,128)(2,1)S(1)} %collective-permute-done.6.refs_1_, bf16[288,256]{1,0:T(8,128)(2,1)S(1)} %collective-permute-done.7.refs_2_, ...), custom_call_target="tpu_custom_call", output_to_operand_aliasing={{0}: (12, {})} | custom-call | flops 3000000000 | bytes 1048576 | tf_op jit(solution)/shard_map/received_blocks/pallas_call | solution.py:326
  38.5 2.6 %collective-permute-done.13.refs_2_ = bf16[288,256]{1,0:T(8,128)(2,1)S(1)} collective-permute-done((bf16[288,256]{1,0:T(8,128)(2,1)S(1)}, bf16[288,256]{1,0:T(8,128)(2,1)S(1)}, u32[]{:S(2)}, u32[]{:S(2)}) %collective-permute-start.13) | collective-permute-done | bytes 147488 | tf_op jit(solution)/shard_map/ppermute | solution.py:411
  42.0 0.9 %collective-permute-start.22 = (bf16[288,256]{1,0:T(8,128)(2,1)S(1)}, bf16[288,256]{1,0:T(8,128)(2,1)S(1)}, u32[]{:S(2)}, u32[]{:S(2)}) collective-permute-start(bf16[288,256]{1,0:T(8,128)(2,1)S(1)} %collective-permute-done.17.refs_0_), channel_id=1, source_target_pairs={{0,25},{1,24},{2,27},{3,26},{4,29},{5,28},{6,31},{7,30},{8,17},{9,... | collective-permute-start | bytes 442376 | tf_op jit(solution)/shard_map/ppermute | solution.py:411
  43.6 2.9 %received_blocks.6 = (bf16[169,6144]{1,0:T(8,128)(2,1)}, bf16[96,256]{1,0:T(8,128)(2,1)S(1)}) custom-call(bf16[288,256]{1,0:T(8,128)(2,1)S(1)} %collective-permute-done.11.refs_0_, bf16[288,256]{1,0:T(8,128)(2,1)S(1)} %collective-permute-done.12.refs_1_, bf16[288,256]{1,0:T(8,128)(2,1)S(1)} %collective-permute-done.13.refs_2_, ...), custom_call_target="tpu_custom_call", output_to_operand_aliasing={{0}: (12, {})} | custom-call | flops 3000000000 | bytes 1048576 | tf_op jit(solution)/shard_map/received_blocks/pallas_call | solution.py:326
  46.4 3.7 %collective-permute-done.19.refs_2_ = bf16[288,256]{1,0:T(8,128)(2,1)S(1)} collective-permute-done((bf16[288,256]{1,0:T(8,128)(2,1)S(1)}, bf16[288,256]{1,0:T(8,128)(2,1)S(1)}, u32[]{:S(2)}, u32[]{:S(2)}) %collective-permute-start.19) | collective-permute-done | bytes 147488 | tf_op jit(solution)/shard_map/ppermute | solution.py:411
  50.2 2.9 %received_blocks.7 = (bf16[169,6144]{1,0:T(8,128)(2,1)}, bf16[96,256]{1,0:T(8,128)(2,1)S(1)}) custom-call(bf16[288,256]{1,0:T(8,128)(2,1)S(1)} %collective-permute-done.17.refs_0_, bf16[288,256]{1,0:T(8,128)(2,1)S(1)} %collective-permute-done.18.refs_1_, bf16[288,256]{1,0:T(8,128)(2,1)S(1)} %collective-permute-done.19.refs_2_, ...), custom_call_target="tpu_custom_call", output_to_operand_aliasing={{0}: (12, {})} | custom-call | flops 3000000000 | bytes 1048576 | tf_op jit(solution)/shard_map/received_blocks/pallas_call | solution.py:326
  53.1 4.9 %own_blocks.1 = bf16[169,4096]{1,0:T(8,128)(2,1)} custom-call(s32[1,4096]{1,0:T(1,128)} %bitcast.13, f32[256,4096]{1,0:T(8,128)S(1)} %get-tuple-element.22.held_ref, bf16[256,256]{1,0:T(8,128)(2,1)S(1)} %get-tuple-element.23.refs_11_.w_right_ref, bf16[256,256]{1,0:T(8,128)(2,1)S(1)} %get-tuple-element.24.refs_9_.w_mix_ref, bf16[169,256]{1,0:T(8,128)(2,1)S(1)} %bitcast.6, ...), custom_call_target="tpu_custom_call" | custom-call | flops 3000000000 | bytes 1048576 | tf_op jit(solution)/shard_map/own_blocks/pallas_call | solution.py:372
  (31 shorter events, 3.6 us)
Async XLA Ops:
  2.7 6.2 %collective-permute-start = (bf16[288,256]{1,0:T(8,128)(2,1)S(1)}, bf16[288,256]{1,0:T(8,128)(2,1)S(1)}, u32[]{:S(2)}, u32[]{:S(2)}) collective-permute-start(bf16[288,256]{1,0:T(8,128)(2,1)S(1)} %get-tuple-element.25.refs_0_), channel_id=1, source_target_pairs={{0,8},{1,9},{2,10},{3,11},{4,12},{5,13},{6,14},{7,15},{8,0},{9,1},... | collective-permute-start | bytes 442376 | tf_op jit(solution)/shard_map/ppermute | solution.py:411
  3.3 8.3 %collective-permute-start.1 = (bf16[288,256]{1,0:T(8,128)(2,1)S(1)}, bf16[288,256]{1,0:T(8,128)(2,1)S(1)}, u32[]{:S(2)}, u32[]{:S(2)}) collective-permute-start(bf16[288,256]{1,0:T(8,128)(2,1)S(1)} %get-tuple-element.25.refs_0_), channel_id=1, source_target_pairs={{0,24},{1,25},{2,26},{3,27},{4,28},{5,29},{6,30},{7,31},{8,16},{9,... | collective-permute-start | bytes 442376 | tf_op jit(solution)/shard_map/ppermute | solution.py:411
  5.9 7.6 %collective-permute-start.2 = (bf16[288,256]{1,0:T(8,128)(2,1)S(1)}, bf16[288,256]{1,0:T(8,128)(2,1)S(1)}, u32[]{:S(2)}, u32[]{:S(2)}) collective-permute-start(bf16[288,256]{1,0:T(8,128)(2,1)S(1)} %get-tuple-element.25.refs_0_), channel_id=1, source_target_pairs={{0,1},{1,0},{2,3},{3,2},{4,5},{5,4},{6,7},{7,6},{8,9},{9,8},{10,11... | collective-permute-start | bytes 442376 | tf_op jit(solution)/shard_map/ppermute | solution.py:411
  7.4 6.5 %collective-permute-start.5 = (bf16[288,256]{1,0:T(8,128)(2,1)S(1)}, bf16[288,256]{1,0:T(8,128)(2,1)S(1)}, u32[]{:S(2)}, u32[]{:S(2)}) collective-permute-start(bf16[288,256]{1,0:T(8,128)(2,1)S(1)} %get-tuple-element.31), channel_id=1, source_target_pairs={{0,2},{1,3},{2,0},{3,1},{4,6},{5,7},{6,4},{7,5},{8,10},{9,11},{10,... | collective-permute-start | bytes 442376 | tf_op jit(solution)/shard_map/ppermute | solution.py:411
  9.0 11.1 %collective-permute-start.4 = (bf16[288,256]{1,0:T(8,128)(2,1)S(1)}, bf16[288,256]{1,0:T(8,128)(2,1)S(1)}, u32[]{:S(2)}, u32[]{:S(2)}) collective-permute-start(bf16[288,256]{1,0:T(8,128)(2,1)S(1)} %get-tuple-element.25.refs_0_), channel_id=1, source_target_pairs={{0,25},{1,24},{2,27},{3,26},{4,29},{5,28},{6,31},{7,30},{8,17},{9,... | collective-permute-start | bytes 442376 | tf_op jit(solution)/shard_map/ppermute | solution.py:411
  9.0 13.9 %collective-permute-start.11 = (bf16[288,256]{1,0:T(8,128)(2,1)S(1)}, bf16[288,256]{1,0:T(8,128)(2,1)S(1)}, u32[]{:S(2)}, u32[]{:S(2)}) collective-permute-start(bf16[288,256]{1,0:T(8,128)(2,1)S(1)} %get-tuple-element.35), channel_id=1, source_target_pairs={{0,4},{1,5},{2,6},{3,7},{4,0},{5,1},{6,2},{7,3},{8,12},{9,13},{10,... | collective-permute-start | bytes 442376 | tf_op jit(solution)/shard_map/ppermute | solution.py:411
  11.6 12.1 %collective-permute-start.17 = (bf16[288,256]{1,0:T(8,128)(2,1)S(1)}, bf16[288,256]{1,0:T(8,128)(2,1)S(1)}, u32[]{:S(2)}, u32[]{:S(2)}) collective-permute-start(bf16[288,256]{1,0:T(8,128)(2,1)S(1)} %get-tuple-element.38), channel_id=1, source_target_pairs={{0,6},{1,7},{2,4},{3,5},{4,2},{5,3},{6,0},{7,1},{8,14},{9,15},{10,... | collective-permute-start | bytes 442376 | tf_op jit(solution)/shard_map/ppermute | solution.py:411
  13.5 11.6 %collective-permute-start.3 = (bf16[288,256]{1,0:T(8,128)(2,1)S(1)}, bf16[288,256]{1,0:T(8,128)(2,1)S(1)}, u32[]{:S(2)}, u32[]{:S(2)}) collective-permute-start(bf16[288,256]{1,0:T(8,128)(2,1)S(1)} %collective-permute-done.2.refs_3_), channel_id=1, source_target_pairs={{0,8},{1,9},{2,10},{3,11},{4,12},{5,13},{6,14},{7,15},{8,0},{9,1},... | collective-permute-start | bytes 442376 | tf_op jit(solution)/shard_map/ppermute | solution.py:411
  13.9 12.1 %collective-permute-start.8 = (bf16[288,256]{1,0:T(8,128)(2,1)S(1)}, bf16[288,256]{1,0:T(8,128)(2,1)S(1)}, u32[]{:S(2)}, u32[]{:S(2)}) collective-permute-start(bf16[288,256]{1,0:T(8,128)(2,1)S(1)} %collective-permute-done.5.refs_0_), channel_id=1, source_target_pairs={{0,1},{1,0},{2,3},{3,2},{4,5},{5,4},{6,7},{7,6},{8,9},{9,8},{10,11... | collective-permute-start | bytes 442376 | tf_op jit(solution)/shard_map/ppermute | solution.py:411
  20.1 9.1 %collective-permute-start.6 = (bf16[288,256]{1,0:T(8,128)(2,1)S(1)}, bf16[288,256]{1,0:T(8,128)(2,1)S(1)}, u32[]{:S(2)}, u32[]{:S(2)}) collective-permute-start(bf16[288,256]{1,0:T(8,128)(2,1)S(1)} %collective-permute-done.5.refs_0_), channel_id=1, source_target_pairs={{0,8},{1,9},{2,10},{3,11},{4,12},{5,13},{6,14},{7,15},{8,0},{9,1},... | collective-permute-start | bytes 442376 | tf_op jit(solution)/shard_map/ppermute | solution.py:411
  22.8 9.0 %collective-permute-start.7 = (bf16[288,256]{1,0:T(8,128)(2,1)S(1)}, bf16[288,256]{1,0:T(8,128)(2,1)S(1)}, u32[]{:S(2)}, u32[]{:S(2)}) collective-permute-start(bf16[288,256]{1,0:T(8,128)(2,1)S(1)} %collective-permute-done.5.refs_0_), channel_id=1, source_target_pairs={{0,24},{1,25},{2,26},{3,27},{4,28},{5,29},{6,30},{7,31},{8,16},{9,... | collective-permute-start | bytes 442376 | tf_op jit(solution)/shard_map/ppermute | solution.py:411
  23.7 9.3 %collective-permute-start.10 = (bf16[288,256]{1,0:T(8,128)(2,1)S(1)}, bf16[288,256]{1,0:T(8,128)(2,1)S(1)}, u32[]{:S(2)}, u32[]{:S(2)}) collective-permute-start(bf16[288,256]{1,0:T(8,128)(2,1)S(1)} %collective-permute-done.5.refs_0_), channel_id=1, source_target_pairs={{0,25},{1,24},{2,27},{3,26},{4,29},{5,28},{6,31},{7,30},{8,17},{9,... | collective-permute-start | bytes 442376 | tf_op jit(solution)/shard_map/ppermute | solution.py:411
  25.2 9.0 %collective-permute-start.14 = (bf16[288,256]{1,0:T(8,128)(2,1)S(1)}, bf16[288,256]{1,0:T(8,128)(2,1)S(1)}, u32[]{:S(2)}, u32[]{:S(2)}) collective-permute-start(bf16[288,256]{1,0:T(8,128)(2,1)S(1)} %collective-permute-done.11.refs_0_), channel_id=1, source_target_pairs={{0,1},{1,0},{2,3},{3,2},{4,5},{5,4},{6,7},{7,6},{8,9},{9,8},{10,11... | collective-permute-start | bytes 442376 | tf_op jit(solution)/shard_map/ppermute | solution.py:411
  26.1 9.0 %collective-permute-start.9 = (bf16[288,256]{1,0:T(8,128)(2,1)S(1)}, bf16[288,256]{1,0:T(8,128)(2,1)S(1)}, u32[]{:S(2)}, u32[]{:S(2)}) collective-permute-start(bf16[288,256]{1,0:T(8,128)(2,1)S(1)} %collective-permute-done.8.refs_3_), channel_id=1, source_target_pairs={{0,8},{1,9},{2,10},{3,11},{4,12},{5,13},{6,14},{7,15},{8,0},{9,1},... | collective-permute-start | bytes 442376 | tf_op jit(solution)/shard_map/ppermute | solution.py:411
  29.2 8.7 %collective-permute-start.12 = (bf16[288,256]{1,0:T(8,128)(2,1)S(1)}, bf16[288,256]{1,0:T(8,128)(2,1)S(1)}, u32[]{:S(2)}, u32[]{:S(2)}) collective-permute-start(bf16[288,256]{1,0:T(8,128)(2,1)S(1)} %collective-permute-done.11.refs_0_), channel_id=1, source_target_pairs={{0,8},{1,9},{2,10},{3,11},{4,12},{5,13},{6,14},{7,15},{8,0},{9,1},... | collective-permute-start | bytes 442376 | tf_op jit(solution)/shard_map/ppermute | solution.py:411
  31.8 9.3 %collective-permute-start.13 = (bf16[288,256]{1,0:T(8,128)(2,1)S(1)}, bf16[288,256]{1,0:T(8,128)(2,1)S(1)}, u32[]{:S(2)}, u32[]{:S(2)}) collective-permute-start(bf16[288,256]{1,0:T(8,128)(2,1)S(1)} %collective-permute-done.11.refs_0_), channel_id=1, source_target_pairs={{0,24},{1,25},{2,26},{3,27},{4,28},{5,29},{6,30},{7,31},{8,16},{9,... | collective-permute-start | bytes 442376 | tf_op jit(solution)/shard_map/ppermute | solution.py:411
  33.0 9.0 %collective-permute-start.16 = (bf16[288,256]{1,0:T(8,128)(2,1)S(1)}, bf16[288,256]{1,0:T(8,128)(2,1)S(1)}, u32[]{:S(2)}, u32[]{:S(2)}) collective-permute-start(bf16[288,256]{1,0:T(8,128)(2,1)S(1)} %collective-permute-done.11.refs_0_), channel_id=1, source_target_pairs={{0,25},{1,24},{2,27},{3,26},{4,29},{5,28},{6,31},{7,30},{8,17},{9,... | collective-permute-start | bytes 442376 | tf_op jit(solution)/shard_map/ppermute | solution.py:411
  34.1 8.8 %collective-permute-start.20 = (bf16[288,256]{1,0:T(8,128)(2,1)S(1)}, bf16[288,256]{1,0:T(8,128)(2,1)S(1)}, u32[]{:S(2)}, u32[]{:S(2)}) collective-permute-start(bf16[288,256]{1,0:T(8,128)(2,1)S(1)} %collective-permute-done.17.refs_0_), channel_id=1, source_target_pairs={{0,1},{1,0},{2,3},{3,2},{4,5},{5,4},{6,7},{7,6},{8,9},{9,8},{10,11... | collective-permute-start | bytes 442376 | tf_op jit(solution)/shard_map/ppermute | solution.py:411
  35.1 8.5 %collective-permute-start.15 = (bf16[288,256]{1,0:T(8,128)(2,1)S(1)}, bf16[288,256]{1,0:T(8,128)(2,1)S(1)}, u32[]{:S(2)}, u32[]{:S(2)}) collective-permute-start(bf16[288,256]{1,0:T(8,128)(2,1)S(1)} %collective-permute-done.14.refs_3_), channel_id=1, source_target_pairs={{0,8},{1,9},{2,10},{3,11},{4,12},{5,13},{6,14},{7,15},{8,0},{9,1},... | collective-permute-start | bytes 442376 | tf_op jit(solution)/shard_map/ppermute | solution.py:411
  37.9 8.5 %collective-permute-start.18 = (bf16[288,256]{1,0:T(8,128)(2,1)S(1)}, bf16[288,256]{1,0:T(8,128)(2,1)S(1)}, u32[]{:S(2)}, u32[]{:S(2)}) collective-permute-start(bf16[288,256]{1,0:T(8,128)(2,1)S(1)} %collective-permute-done.17.refs_0_), channel_id=1, source_target_pairs={{0,8},{1,9},{2,10},{3,11},{4,12},{5,13},{6,14},{7,15},{8,0},{9,1},... | collective-permute-start | bytes 442376 | tf_op jit(solution)/shard_map/ppermute | solution.py:411
  41.2 9.0 %collective-permute-start.19 = (bf16[288,256]{1,0:T(8,128)(2,1)S(1)}, bf16[288,256]{1,0:T(8,128)(2,1)S(1)}, u32[]{:S(2)}, u32[]{:S(2)}) collective-permute-start(bf16[288,256]{1,0:T(8,128)(2,1)S(1)} %collective-permute-done.17.refs_0_), channel_id=1, source_target_pairs={{0,24},{1,25},{2,26},{3,27},{4,28},{5,29},{6,30},{7,31},{8,16},{9,... | collective-permute-start | bytes 442376 | tf_op jit(solution)/shard_map/ppermute | solution.py:411
  42.0 8.2 %collective-permute-start.22 = (bf16[288,256]{1,0:T(8,128)(2,1)S(1)}, bf16[288,256]{1,0:T(8,128)(2,1)S(1)}, u32[]{:S(2)}, u32[]{:S(2)}) collective-permute-start(bf16[288,256]{1,0:T(8,128)(2,1)S(1)} %collective-permute-done.17.refs_0_), channel_id=1, source_target_pairs={{0,25},{1,24},{2,27},{3,26},{4,29},{5,28},{6,31},{7,30},{8,17},{9,... | collective-permute-start | bytes 442376 | tf_op jit(solution)/shard_map/ppermute | solution.py:411
  43.0 7.2 %collective-permute-start.21 = (bf16[288,256]{1,0:T(8,128)(2,1)S(1)}, bf16[288,256]{1,0:T(8,128)(2,1)S(1)}, u32[]{:S(2)}, u32[]{:S(2)}) collective-permute-start(bf16[288,256]{1,0:T(8,128)(2,1)S(1)} %collective-permute-done.20.refs_3_), channel_id=1, source_target_pairs={{0,8},{1,9},{2,10},{3,11},{4,12},{5,13},{6,14},{7,15},{8,0},{9,1},... | collective-permute-start | bytes 442376 | tf_op jit(solution)/shard_map/ppermute | solution.py:411
  50.2 2.9 %copy-start = (bf16[256,169]{0,1:T(8,128)(2,1)S(1)}, bf16[256,169]{0,1:T(8,128)(2,1)}, u32[]{:S(2)}) copy-start(bf16[256,169]{0,1:T(8,128)(2,1)} %param.23) | copy-start | bytes 259588

commit v3 on v2

--- a/solution.py
+++ b/solution.py
@@ -71,7 +71,8 @@
         self.slot = self.pairs // (2 * self.cells)
         self.part = self.fetch // 3
         self.groups = 3 * self.inner
-        self.meta = PLANES * self.groups
+        self.section = PLANES * self.groups
+        self.meta = 2 * self.section
         self.per_row = self.width // LIST
         self.rows = up(self.atoms + self.meta + -(-self.cells // self.per_row), 16)
         self.entries = w_out.shape[1]
@@ -82,6 +83,10 @@
     strip, cell = lax.axis_index("strip"), lax.axis_index("cell")
     even = lax.rem(strip, 2) == 0
     return cell, lax.div(cell, 2), lax.rem(cell, 2), even
+
+
+def sent_steps(n):
+    return [b for b in range(n.outer) if b < 2 or b % 2 == 0]
 
 
 def tiles_kernel(n, atom_ref, row_ref, slot_ref, dist_ref, list_ref, feat_ref, *outs):
@@ -111,12 +116,14 @@
     shape = (tail, PLANES * total)
     r = lax.broadcasted_iota(jnp.int32, shape, 0)
     q = lax.broadcasted_iota(jnp.int32, shape, 1)
-    g = whole_div(r, PLANES)
-    plane = r - g * PLANES
+    section = whole_div(r, n.section)
+    g = whole_div(r - section * n.section, PLANES)
+    plane = r - section * n.section - g * PLANES
     role = whole_div(g, n.inner)
     o = jnp.where(role == 0, 1, jnp.where((role == 1) == even, 2, 0))
     base = plane * total + o * n.cells + jnp.bitwise_xor(g - role * n.inner, xi)
     base = jnp.where(r < n.meta, base, -n.pairs)
+    section = jnp.where(r < n.meta, section, 0)
     e = list_ref[...]
     kk = lax.broadcasted_iota(jnp.int32, e.shape, 1)
     e = (e - (kk - whole_div(kk, 3) * 3) * n.atoms).astype(F32)
@@ -131,9 +138,9 @@
     put = (put_r == n.meta + whole_div(put_j, n.per_row)).astype(BF16)
     lists = dot(put, flat)
     feat = feat_ref[...]
-    for b, out in enumerate(outs):
-        zz = jnp.bitwise_xor(zi, b)
-        pick = (base + zz * n.inner == q).astype(BF16)
+    for b, out in zip(sent_steps(n), outs):
+        plane_of = jnp.bitwise_xor(jnp.bitwise_xor(zi, b), section)
+        pick = (base + plane_of * n.inner == q).astype(BF16)
         out[0 : n.atoms, :] = feat
         pairs = dot(pick, placed)
         if n.slot < n.width:
@@ -155,47 +162,54 @@
     args = (pair_atom, partner_row, transpose_slot, distance, send_rows, features)
     return pl.pallas_call(
         functools.partial(tiles_kernel, n),
-        out_shape=[jax.ShapeDtypeStruct((n.rows, n.width), BF16)] * n.outer,
+        out_shape=[jax.ShapeDtypeStruct((n.rows, n.width), BF16)] * len(sent_steps(n)),
         compiler_params=pltpu.CompilerParams(vmem_limit_bytes=LIMIT),
         cost_estimate=cost(600_000_000),
         name="place_pairs",
     )(*far(*args))
 
 
-def own_gate_kernel(n, dist_ref, atom_ref, feat_ref, *refs):
+def first_gate_kernel(n, step, dist_ref, atom_ref, feat_ref, *refs):
     sources, held_ref, flipped, left_ref = refs[:6], refs[6], refs[7:13], refs[13]
-
-    @pl.when(pl.program_id(0) == 0)
-    def _():
-        for src, dst in zip(sources[:5], flipped[:5]):
-            dst[...] = src[...].T
-        r = lax.broadcasted_iota(jnp.int32, (n.entries, n.entries), 0)
-        q = lax.broadcasted_iota(jnp.int32, (n.entries, n.entries), 1)
-        first = whole_div(r, n.orbitals)
-        swap = (q == (r - first * n.orbitals) * n.orbitals + first).astype(BF16)
-        flipped[5][...] = dot(swap, sources[5][...]).astype(BF16)
-        left_ref[...] = dot(flipped[0][...], feat_ref[...], 1, 1).astype(BF16)
-
-    gate = gate_of(dist_ref[...], flipped[2][...], flipped[3][...])
-    held_ref[...] = gate * dot(left_ref[...], onehot(atom_ref[...], n.atoms))
-
-
-def own_gate(n, step, distance, pair_atom, features, weights):
-    row = pl.BlockSpec((1, step), lambda i: (0, i))
+    for src, dst in zip(sources[:5], flipped[:5]):
+        dst[...] = src[...].T
+    r = lax.broadcasted_iota(jnp.int32, (n.entries, n.entries), 0)
+    q = lax.broadcasted_iota(jnp.int32, (n.entries, n.entries), 1)
+    first = whole_div(r, n.orbitals)
+    swap = (q == (r - first * n.orbitals) * n.orbitals + first).astype(BF16)
+    flipped[5][...] = dot(swap, sources[5][...]).astype(BF16)
+    left_ref[...] = dot(flipped[0][...], feat_ref[...], 1, 1).astype(BF16)
+    gate = gate_of(dist_ref[:, 0:step], flipped[2][...], flipped[3][...])
+    held_ref[...] = gate * dot(left_ref[...], onehot(atom_ref[:, 0:step], n.atoms))
+
+
+def second_gate_kernel(n, step, dist_ref, atom_ref, left_ref, w_in_ref, w_ro_ref, held_ref):
+    gate = gate_of(dist_ref[:, step:], w_in_ref[...], w_ro_ref[...])
+    held_ref[...] = gate * dot(left_ref[...], onehot(atom_ref[:, step:], n.atoms))
+
+
+def first_gate(n, step, distance, pair_atom, features, weights):
     turned = [jax.ShapeDtypeStruct(w.shape[::-1], BF16) for w in weights[:5]]
     turned.append(jax.ShapeDtypeStruct(weights[5].shape, BF16))
+    turned.append(jax.ShapeDtypeStruct((n.width, n.atoms), BF16))
     out = pl.pallas_call(
-        functools.partial(own_gate_kernel, n),
-        grid=(n.pairs // step,),
-        in_specs=[row, row] + [whole(a) for a in (features, *weights)],
-        out_specs=[pl.BlockSpec((n.width, step), lambda i: (0, i))] + [whole(a) for a in turned],
-        out_shape=[jax.ShapeDtypeStruct((n.width, n.pairs), F32)] + turned,
-        scratch_shapes=[pltpu.VMEM((n.width, n.atoms), BF16)],
+        functools.partial(first_gate_kernel, n, step),
+        out_shape=[jax.ShapeDtypeStruct((n.width, step), F32)] + turned,
         compiler_params=pltpu.CompilerParams(vmem_limit_bytes=LIMIT),
         cost_estimate=cost(3_000_000_000),
-        name="own_gate",
+        name="first_gate",
     )(*far(distance, pair_atom, features, *weights))
-    return out[0], out[1:]
+    return out[0], out[1:7], out[7]
+
+
+def second_gate(n, step, distance, pair_atom, left, w_in_t, w_ro_t):
+    return pl.pallas_call(
+        functools.partial(second_gate_kernel, n, step),
+        out_shape=jax.ShapeDtypeStruct((n.width, n.pairs - step), F32),
+        compiler_params=pltpu.CompilerParams(vmem_limit_bytes=LIMIT),
+        cost_estimate=cost(2_000_000_000),
+        name="second_gate",
+    )(*far(distance, pair_atom), left, w_in_t, w_ro_t)
 
 
 def partner_table(n, even, tiles, w_right_t, table_ref):
@@ -214,26 +228,35 @@
         table_ref[role] = dot(right, onehot(index.astype(jnp.int32), n.atoms)).astype(BF16)
 
 
-def received_kernel(n, steps, first, direct, count, *refs):
+def received_kernel(n, steps, sections, have, used, first, direct, count, final, *refs):
     held, refs = refs[:count], refs[count:]
+    if final:
+        calls, extra = final
+        mine, refs = refs[:extra], refs[extra:]
     if not first and direct:
         refs = refs[1:]
     outs, refs = refs[: 3 if first else 2], refs[3 if first else 2 :]
-    blocks_buf, sem_out = refs
-    block_ref, rows_buf = outs[:2]
+    if final:
+        (block_ref, own_ref), (rows_buf, own_buf, sem_own, blocks_buf, sem_out) = outs, refs
+    else:
+        (block_ref, rows_buf), (blocks_buf, sem_out) = outs[:2], refs
     need = held.__getitem__
 
     me, zi, xi, even = where_am_i()
     o_sib = jnp.where(even, 0, 2)
     roles = (1, o_sib, 2 - o_sib)
-    base = 6 * len(steps)
+    base = len(used)
     near = [(i, at) for i in range(len(steps)) for at in range(n.inner)]
-    order = [(role, i, at) for role in range(3) for i, at in near]
+    order = [(role, i, at) for role in have for i, at in near]
     number = {key: g for g, key in enumerate(order)}
     cells = {
         (i, at): jnp.bitwise_xor(zi, steps[i]) * n.inner + jnp.bitwise_xor(xi, at) for i, at in near
     }
-    tiles = {(role, i, at): need(6 * i + 3 * at + role) for role, i, at in order}
+    tiles = {
+        (u % 3, i, u // 3): need(used.index(u)).at[pl.ds(i * n.rows, n.rows)]
+        for u in used
+        for i in range(len(steps))
+    }
     done = []
     if first:
         own = [tiles[role, 0, 0] for role in range(3)]
@@ -246,7 +269,7 @@
 
     slabs = []
     for role, i, at in order:
-        top = (role * n.inner + at) * PLANES
+        top = sections[i] * n.section + (role * n.inner + at) * PLANES
         tail = tiles[role, i, at][n.atoms :, 0 : n.slot].astype(F32)
         slabs.append(tail[top : top + PLANES])
     meta = jnp.concatenate(slabs, 1)
@@ -259,7 +282,7 @@
 
     gate = gate_of(dists, need(base + 1)[...], need(base + 2)[...])
     rights = []
-    for role in range(3):
+    for role in have:
         place = [cut(spots, number[role, i, at]) + cells[i, at] * n.part for i, at in near]
         rights.append(dot(table[role], onehot(jnp.concatenate(place, 1), n.cells * n.part)))
     lefts = [
@@ -282,14 +305,14 @@
             done.append(out)
 
     rows = len(order) * n.part
-    mine = lax.broadcasted_iota(jnp.int32, (n.cells, n.fetch), 0) == me
+    my_list = lax.broadcasted_iota(jnp.int32, (n.cells, n.fetch), 0) == me
     index = []
     k = lax.broadcasted_iota(jnp.int32, (n.part, n.fetch), 1)
     m3 = 3 * lax.broadcasted_iota(jnp.int32, (n.part, n.fetch), 0)
     asked = {}
     for i, at in near:
         lists = lists_of(n, tiles[0, i, at])
-        asked[i, at] = jnp.sum(jnp.where(mine, lists, 0.0), 0, keepdims=True)
+        asked[i, at] = jnp.sum(jnp.where(my_list, lists, 0.0), 0, keepdims=True)
     for g, (role, i, at) in enumerate(order):
         o_own = 1 if role == 0 else 2 - roles[role]
         here = jnp.sum(jnp.where(k == m3 + o_own, asked[i, at], 0.0), 1, keepdims=True)
@@ -301,54 +324,73 @@
         out = pltpu.make_async_copy(blocks_buf, block_ref, sem_out.at[0])
         out.start()
         done.append(out)
+    if final:
+        w_mix = need(base + 3)
+        done += own_part(n, calls, mine, w_mix, rows_buf, own_buf, own_ref, sem_own, even, zi, xi)
     for out in done:
         out.wait()
 
 
-def received(n, steps, tiles, weights, table, w_right_t, into):
+def received(n, steps, sections, have, tiles, weights, table, w_right_t, into, own=None):
     first = table is None
     direct = n.slot % 128 == 0
-    operands = list(tiles) + list(weights) + [w_right_t if first else table]
+    used = [0, 1, 2, 3, 4, 5] if first else [0, 3] + [3 * at + r for at in (0, 1) for r in have if r]
+    if first and 2 not in have:
+        used.remove(5)
+    used = sorted(set(used))
+    operands = [tiles[u] for u in used] + list(weights) + [w_right_t if first else table]
     count = len(operands)
-    blocks = (n.entries, 6 * len(steps) * n.slot)
-    rows = (6 * len(steps) * n.part, n.width)
+    calls = None
+    if own is not None:
+        calls, extra = own
+        operands += extra
+    near = len(operands)
+    groups = n.inner * len(have) * len(steps)
+    blocks = (n.entries, groups * n.slot)
+    rows = (groups * n.part, n.width)
     shape = (3, n.width, n.cells * n.part)
-    out_shape = [
-        jax.ShapeDtypeStruct((n.entries, 3 * n.cells * n.slot) if direct else blocks, BF16),
-        jax.ShapeDtypeStruct(rows, BF16),
-    ]
+    out_shape = [jax.ShapeDtypeStruct((n.entries, 3 * n.cells * n.slot) if direct else blocks, BF16)]
+    scratch = [pltpu.VMEM(blocks, BF16), pltpu.SemaphoreType.DMA((groups,))]
+    fast, slow = pl.BlockSpec(memory_space=pltpu.VMEM), pl.BlockSpec(memory_space=pl.ANY)
+    if own is not None:
+        out_shape.append(jax.ShapeDtypeStruct((n.entries, n.pairs), BF16))
+        out_specs = [slow, slow]
+        scratch = [
+            pltpu.VMEM(rows, BF16),
+            pltpu.VMEM((n.entries, n.pairs), BF16),
+            pltpu.SemaphoreType.DMA((2,)),
+        ] + scratch
+    else:
+        out_shape.append(jax.ShapeDtypeStruct(rows, BF16))
+        out_specs = [slow, fast]
     if first:
         out_shape.append(jax.ShapeDtypeStruct(shape, BF16))
+        out_specs.append(fast)
     aliases = {}
     if direct and not first:
-        aliases = {count: 0}
+        aliases = {near: 0}
         operands.append(into)
     out = pl.pallas_call(
-        functools.partial(received_kernel, n, steps, first, direct, count),
-        in_specs=[pl.BlockSpec(memory_space=pltpu.VMEM)] * count + [pl.BlockSpec(memory_space=pl.ANY)] * (len(operands) - count),
-        out_specs=[pl.BlockSpec(memory_space=pl.ANY)] + [pl.BlockSpec(memory_space=pltpu.VMEM)] * (len(out_shape) - 1),
+        functools.partial(
+            received_kernel, n, steps, sections, have, tuple(used), first, direct, count,
+            (calls, near - count) if calls else None,
+        ),
+        in_specs=[fast] * near + [slow] * (len(operands) - near),
+        out_specs=out_specs,
         out_shape=out_shape,
-        scratch_shapes=[
-            pltpu.VMEM(blocks, BF16),
-            pltpu.SemaphoreType.DMA((6 * len(steps),)),
-        ],
+        scratch_shapes=scratch,
         input_output_aliases=aliases,
         compiler_params=pltpu.CompilerParams(vmem_limit_bytes=LIMIT),
-        cost_estimate=cost(3_000_000_000 * len(steps)),
+        cost_estimate=cost(500_000_000 * groups),
         name="received_blocks",
     )(*operands)
     return out[0], out[1], out[2] if first else table
 
 
-def own_blocks_kernel(n, per_call, row_ref, held_ref, w_right_ref, w_mix_ref, w_out_ref, *refs):
-    tables, out_ref, right_ref = refs[:-2], refs[-2], refs[-1]
-    _, zi, xi, even = where_am_i()
-
-    @pl.when(pl.program_id(0) == 0)
-    def _():
-        rows = jnp.concatenate([t[...] for t in tables], 0)
-        right_ref[...] = dot(w_right_ref[...], rows, 1, 1).astype(BF16)
-
+def own_part(n, calls, mine, w_mix, last, own_buf, own_ref, sem, even, zi, xi):
+    row_ref, halves, w_right_ref, w_out_ref, tables = mine[0], mine[1:3], mine[3], mine[4], mine[5:]
+    rows = jnp.concatenate([t[...] for t in tables] + [last[...]], 0)
+    table = dot(w_right_ref[...], rows, 1, 1).astype(BF16)
     v = row_ref[...]
     q = whole_div(v, n.fetch)
     k = v - q * n.fetch
@@ -359,31 +401,26 @@
     outer = whole_div(q, n.inner)
     inner = q - outer * n.inner
     b = jnp.bitwise_xor(outer, zi)
-    call = whole_div(b, per_call)
-    place = (call * 3 + role) * per_call + b - call * per_call
-    place = place * n.inner + jnp.bitwise_xor(inner, xi)
-    right = dot(right_ref[...], onehot(place * n.part + m, right_ref.shape[1]))
-    edge = (held_ref[...] * right).astype(BF16)
-    mixed = silu(dot(w_mix_ref[...], edge)).astype(BF16)
-    out_ref[...] = dot(w_out_ref[...], mixed).astype(BF16)
-
-
-def own_blocks_of(n, step, partner_row, held, w_right_t, w_mix_t, w_out_t, tables):
-    return pl.pallas_call(
-        functools.partial(own_blocks_kernel, n, n.outer // len(tables)),
-        grid=(n.pairs // step,),
-        in_specs=[
-            pl.BlockSpec((1, step), lambda i: (0, i)),
-            pl.BlockSpec((n.width, step), lambda i: (0, i)),
-        ]
-        + [whole(a) for a in (w_right_t, w_mix_t, w_out_t, *tables)],
-        out_specs=pl.BlockSpec((n.entries, step), lambda i: (0, i)),
-        out_shape=jax.ShapeDtypeStruct((n.entries, n.pairs), BF16),
-        scratch_shapes=[pltpu.VMEM((n.width, 3 * n.cells * n.part), BF16)],
-        compiler_params=pltpu.CompilerParams(vmem_limit_bytes=LIMIT),
-        cost_estimate=cost(3_000_000_000),
-        name="own_blocks",
-    )(*far(partner_row), held, w_right_t, w_mix_t, w_out_t, *tables)
+    place, top = b, 0
+    for steps, have in calls:
+        for r in have:
+            for step in steps:
+                place = jnp.where((b == step) & (role == r), top, place)
+                top += 1
+    place = (place * n.inner + jnp.bitwise_xor(inner, xi)) * n.part + m
+    done, at = [], 0
+    for i, half in enumerate(halves):
+        step = half.shape[1]
+        right = dot(table, onehot(place[:, at : at + step], table.shape[1]))
+        edge = (half[...] * right).astype(BF16)
+        mixed = silu(dot(w_mix[...], edge)).astype(BF16)
+        own_buf[:, at : at + step] = dot(w_out_ref[...], mixed).astype(BF16)
+        part = pl.ds(at, step)
+        out = pltpu.make_async_copy(own_buf.at[:, part], own_ref.at[:, part], sem.at[i])
+        out.start()
+        done.append(out)
+        at += step
+    return done
 
 
 def body(
@@ -422,18 +459,20 @@
     def other(s, c):
         return (s - 1 if s % 2 == 0 else s + 1) % n.strips, c
 
-    def corner(s, c):
-        return other(s, c)[0], c ^ 1
-
     row = lambda a: a.reshape(1, -1)
     pair_atom, partner_row = row(pair_atom), row(partner_row)
     transpose_slot, distance = row(transpose_slot), row(distance)
     tiles = make_tiles(
         n, pair_atom, partner_row, transpose_slot, distance, send_rows, features
     )
-    lines_in = [tiles[0]] + [exchange(tiles[b], along(b)) for b in range(1, n.outer)]
+    lines_in = {0: tiles[0]}
+    for b, tile in zip(sent_steps(n), tiles):
+        if b:
+            lines_in[b] = exchange(tile, along(b))
+    for b in range(3, n.outer, 2):
+        lines_in[b] = exchange(lines_in[b - 1], along(1))
     step = n.pairs // 2
-    held, turned = own_gate(
+    held, turned, left = first_gate(
         n,
         step,
         distance,
@@ -441,37 +480,54 @@
         features,
         (w_left, w_right, w_radial_in, w_radial_out, w_mix, w_out.T),
     )
+    second = second_gate(n, step, distance, pair_atom, left, turned[2], turned[3])
+    lines_in[1], lines_in[2], second = lax.optimization_barrier((lines_in[1], lines_in[2], second))
     w_left_t, w_right_t, w_in_t, w_ro_t, w_mix_t, w_flip_t = turned
     weights = (w_left_t, w_in_t, w_ro_t, w_mix_t, w_flip_t)
-    table, into, tables, parts = None, None, [], []
-    half = 1
-    for at in range(0, n.outer, half):
-        steps, group = tuple(range(at, at + half)), []
-        for b in steps:
-            tile = lines_in[b]
-            across = exchange(tile, beside)
-            group += [
-                tile,
-                exchange(tile, sibling),
-                exchange(tile, other),
-                across,
-                exchange(across, sibling),
-                exchange(tile, corner),
-            ]
-        into, rows, table = received(n, steps, group, weights, table, w_right_t, into)
+    table, into, tables, parts, calls = None, None, [], [], []
+
+    def take(at, have, table, into, own=None):
+        steps, sections, group = sets[at]
+        into, rows, table = received(
+            n, steps, sections, have, group, weights, table, w_right_t, into, own
+        )
         tables.append(rows)
-        parts.append((steps, into))
+        parts.append(into)
+        calls.append((steps, have))
+        return table, into
+
+    sets, chain = [], []
+    for b in range(0, n.outer, 2):
+        tile = jnp.concatenate([lines_in[b], lines_in[b + 1]], 0)
+        chain.append([tile, exchange(tile, sibling), exchange(tile, other), exchange(tile, beside)])
+        if b:
+            before, now = chain[-2], chain[-1]
+            before[3], now[1] = lax.optimization_barrier((before[3], now[1]))
+    for i, (tile, close, away, across) in enumerate(chain):
+        steps, sections = (2 * i, 2 * i + 1), (0, 1 if i else 0)
+        if i:
+            table, into = take(i - 1, (0, 1), table, into)
+        corner = exchange(across, other) if i % 2 else exchange(away, beside)
+        group = [tile, close, away, across, exchange(across, sibling), corner]
+        sets.append((steps, sections, group))
+    last = len(sets) - 1
+    table, into = take(last, (0, 1), table, into)
+    for i in range(last):
+        table, into = take(i, (2,), table, into)
+    every = tuple(calls) + ((sets[last][0], (2,)),)
+    own = (every, [*far(partner_row), held, second, w_right_t, w_out.T, *tables])
+    table, into = take(last, (2,), table, into, own)
+    own = tables.pop()
     if n.slot % 128:
         cell, strip = lax.axis_index("cell"), lax.axis_index("strip")
         o_sib = jnp.where(strip % 2 == 0, 0, 2)
         into = jnp.zeros((n.entries, 3 * n.cells * n.slot), BF16)
-        for steps, blocks in parts:
-            order = [(o, b, at) for o in (1, o_sib, 2 - o_sib) for b in steps for at in (0, 1)]
-            for g, (o, b, at) in enumerate(order):
+        for (steps, have), blocks in zip(calls, parts):
+            order = [(role, b, at) for role in have for b in steps for at in (0, 1)]
+            for g, (role, b, at) in enumerate(order):
                 piece = blocks[:, g * n.slot : (g + 1) * n.slot]
-                spot = o * n.cells + (cell ^ (b * n.inner + at))
+                spot = (1, o_sib, 2 - o_sib)[role] * n.cells + (cell ^ (b * n.inner + at))
                 into = lax.dynamic_update_slice(into, piece, (0, spot * n.slot))
-    own = own_blocks_of(n, step, partner_row, held, w_right_t, w_mix_t, w_out.T, tables)
     return own, into
 
 

time: 58.3 us -> 50.6 us (0.87)
  starting transfers between devices: 22.7 us -> 17.2 us
  waiting for transfers between devices: 11.2 us -> 8.93 us
    ppermute x23 -> x13, starting transfers between devices: 22.7 us -> 17.2 us  [exchange(): return lax.ppermute(x, AXES, pairs)]
    ppermute x23 -> x13, waiting for transfers between devices: 11.2 us -> 8.93 us  [exchange(): return lax.ppermute(x, AXES, pairs)]
  transfers between devices with their start and end apart: 23 -> 13, of which waited for: 4 -> 7; matrix products, arithmetic and copies ran while one was open for 0% -> 0% of each run, Pallas kernels for 23% -> 29%
where the time goes in v3:
time: 50.6 us; the launch traced here: 50.1 us
  Pallas kernels  23 us (45%)
  starting transfers between devices  17.2 us (34%)
  waiting for transfers between devices  8.93 us (18%)
  between operations  0.9 us (2%)
    ppermute x13, starting transfers between devices, exchange(): return lax.ppermute(x, AXES, pairs)  17.2 us
    pallas_call x4, Pallas kernels, received(): pl.pallas_call(functools.partial(received_kernel, n, steps, sections, hav...  16.1 us
    ppermute x13, waiting for transfers between devices, exchange(): return lax.ppermute(x, AXES, pairs)  8.93 us
    pallas_call x1, Pallas kernels, first_gate(): pl.pallas_call(functools.partial(first_gate_kernel, n, step), out_shape=[...  2.7 us
    pallas_call x1, Pallas kernels, second_gate(): pl.pallas_call(functools.partial(second_gate_kernel, n, step), out_shape=...  2.15 us
    pallas_call x1, Pallas kernels, make_tiles(): pl.pallas_call(functools.partial(tiles_kernel, n), out_shape=[jax.ShapeDt...  2.1 us
  transfers between devices with their start and end apart: 13, of which 7 were waited for; matrix products, arithmetic and copies ran while one was open for 0% of the time, Pallas kernels for 29%

profile of v3, /device:TPU:0, one launch (start us, length us, event | category | flops | bytes accessed | tf_op | source)
XLA Modules:
  0.0 50.1 jit_solution(7005363678103555660)
XLA Ops:
  0.6 2.1 %place_pairs.1 = (bf16[320,256]{1,0:T(8,128)(2,1)S(1)}, bf16[320,256]{1,0:T(8,128)(2,1)S(1)}, bf16[320,256]{1,0:T(8,128)(2,1)S(1)}) custom-call(s32[1,4096]{1,0:T(1,128)} %bitcast.10, s32[1,4096]{1,0:T(1,128)} %bitcast.7, s32[1,4096]{1,0:T(1,128)} %bitcast.9, f32[1,4096]{1,0:T(1,128)} %bitcast.13, s32[8,48]{1,0:T(8,128)} %list_ref.1, bf16[256,256]{1,0:T(8,128)(2,1)} %feat_ref.3), custom_call_target="tpu_custom_call" | custom-call | flops 600000000 | bytes 1048576 | tf_op jit(solution)/shard_map/place_pairs/pallas_call | solution.py:163
  2.7 4.1 %collective-permute-start.1 = (bf16[320,256]{1,0:T(8,128)(2,1)S(1)}, bf16[320,256]{1,0:T(8,128)(2,1)S(1)}, u32[]{:S(2)}, u32[]{:S(2)}) collective-permute-start(bf16[320,256]{1,0:T(8,128)(2,1)S(1)} %get-tuple-element.28), channel_id=1, source_target_pairs={{0,4},{1,5},{2,6},{3,7},{4,0},{5,1},{6,2},{7,3},{8,12},{9,13},{10,... | collective-permute-start | bytes 491528 | tf_op jit(solution)/shard_map/ppermute | solution.py:448
  6.8 1.6 %collective-permute-start = (bf16[320,256]{1,0:T(8,128)(2,1)S(1)}, bf16[320,256]{1,0:T(8,128)(2,1)S(1)}, u32[]{:S(2)}, u32[]{:S(2)}) collective-permute-start(bf16[320,256]{1,0:T(8,128)(2,1)S(1)} %get-tuple-element.27), channel_id=1, source_target_pairs={{0,2},{1,3},{2,0},{3,1},{4,6},{5,7},{6,4},{7,5},{8,10},{9,11},{10,... | collective-permute-start | bytes 491528 | tf_op jit(solution)/shard_map/ppermute | solution.py:448
  8.4 2.7 %first_gate.1 = (f32[256,2048]{1,0:T(8,128)S(1)}, bf16[256,256]{1,0:T(8,128)(2,1)S(1)}, bf16[256,256]{1,0:T(8,128)(2,1)S(1)}, bf16[256,128]{1,0:T(8,128)(2,1)S(1...) custom-call(f32[1,4096]{1,0:T(1,128)} %bitcast.14, ...), custom_call_target="tpu_custom_call" | custom-call | flops 3000000000 | bytes 1048576 | tf_op jit(solution)/shard_map/first_gate/pallas_call | solution.py:195
  11.1 2.2 %second_gate.1.refs_12_ = f32[256,2048]{1,0:T(8,128)S(1)} custom-call(f32[1,4096]{1,0:T(1,128)} %bitcast.15, s32[1,4096]{1,0:T(1,128)} %bitcast.12, bf16[256,256]{1,0:T(8,128)(2,1)S(1)} %get-tuple-element.29.left_ref, bf16[256,128]{1,0:T(8,128)(2,1)S(1)} %get-tuple-element.30.w_in_ref.refs_6_.refs_5_, ...), custom_call_target="tpu_custom_call" | custom-call | flops 2000000000 | bytes 1048576 | tf_op jit(solution)/shard_map/second_gate/pallas_call | solution.py:206
  13.3 1.4 %collective-permute-done.1 = bf16[320,256]{1,0:T(8,128)(2,1)S(1)} collective-permute-done((bf16[320,256]{1,0:T(8,128)(2,1)S(1)}, bf16[320,256]{1,0:T(8,128)(2,1)S(1)}, u32[]{:S(2)}, u32[]{:S(2)}) %collective-permute-start.1) | collective-permute-done | bytes 163872 | tf_op jit(solution)/shard_map/ppermute | solution.py:448
  14.6 0.2 collective-permute-done
  14.8 1.5 %collective-permute-start.2 = (bf16[320,256]{1,0:T(8,128)(2,1)S(1)}, bf16[320,256]{1,0:T(8,128)(2,1)S(1)}, u32[]{:S(2)}, u32[]{:S(2)}) collective-permute-start(bf16[320,256]{1,0:T(8,128)(2,1)S(1)} %collective-permute-done.1), channel_id=1, source_target_pairs={{0,2},{1,3},{2,0},{3,1},{4,6},{5,7},{6,4},{7,5},{8,10},{9,11},{10,... | collective-permute-start | bytes 491528 | tf_op jit(solution)/shard_map/ppermute | solution.py:448
  16.3 1.6 %collective-permute-start.8 = (bf16[640,256]{1,0:T(8,128)(2,1)S(1)}, bf16[640,256]{1,0:T(8,128)(2,1)S(1)}, u32[]{:S(2)}, u32[]{:S(2)}) collective-permute-start(bf16[640,256]{1,0:T(8,128)(2,1)S(1)} %constant_dynamic-update-slice_fusion.2.refs_0_), channel_id=1, source_target_pairs={{0,1},{1,0},{2,3},{3,2},{4,5},{5,4},{6,7},{7,6},{8,9},{9,8},{10,11... | collective-permute-start | bytes 983048 | tf_op jit(solution)/shard_map/ppermute | solution.py:448
  17.9 2.2 %collective-permute-done.2 = bf16[320,256]{1,0:T(8,128)(2,1)S(1)} collective-permute-done((bf16[320,256]{1,0:T(8,128)(2,1)S(1)}, bf16[320,256]{1,0:T(8,128)(2,1)S(1)}, u32[]{:S(2)}, u32[]{:S(2)}) %collective-permute-start.2) | collective-permute-done | bytes 163872 | tf_op jit(solution)/shard_map/ppermute | solution.py:448
  20.2 1.7 %collective-permute-start.7 = (bf16[640,256]{1,0:T(8,128)(2,1)S(1)}, bf16[640,256]{1,0:T(8,128)(2,1)S(1)}, u32[]{:S(2)}, u32[]{:S(2)}) collective-permute-start(bf16[640,256]{1,0:T(8,128)(2,1)S(1)} %constant_dynamic-update-slice_fusion.2.refs_0_), channel_id=1, source_target_pairs={{0,24},{1,25},{2,26},{3,27},{4,28},{5,29},{6,30},{7,31},{8,16},{9,... | collective-permute-start | bytes 983048 | tf_op jit(solution)/shard_map/ppermute | solution.py:448
  22.0 1.5 %collective-permute-start.4 = (bf16[640,256]{1,0:T(8,128)(2,1)S(1)}, bf16[640,256]{1,0:T(8,128)(2,1)S(1)}, u32[]{:S(2)}, u32[]{:S(2)}) collective-permute-start(bf16[640,256]{1,0:T(8,128)(2,1)S(1)} %constant_dynamic-update-slice_fusion.refs_0_), channel_id=1, source_target_pairs={{0,1},{1,0},{2,3},{3,2},{4,5},{5,4},{6,7},{7,6},{8,9},{9,8},{10,11... | collective-permute-start | bytes 983048 | tf_op jit(solution)/shard_map/ppermute | solution.py:448
  23.5 1.2 %collective-permute-done.8.refs_3_.refs_2_ = bf16[640,256]{1,0:T(8,128)(2,1)S(1)} collective-permute-done((bf16[640,256]{1,0:T(8,128)(2,1)S(1)}, bf16[640,256]{1,0:T(8,128)(2,1)S(1)}, u32[]{:S(2)}, u32[]{:S(2)}) %collective-permute-start.8) | collective-permute-done | bytes 327712 | tf_op jit(solution)/shard_map/ppermute | solution.py:448
  24.7 2.3 %collective-permute-start.3 = (bf16[640,256]{1,0:T(8,128)(2,1)S(1)}, bf16[640,256]{1,0:T(8,128)(2,1)S(1)}, u32[]{:S(2)}, u32[]{:S(2)}) collective-permute-start(bf16[640,256]{1,0:T(8,128)(2,1)S(1)} %constant_dynamic-update-slice_fusion.refs_0_), channel_id=1, source_target_pairs={{0,24},{1,25},{2,26},{3,27},{4,28},{5,29},{6,30},{7,31},{8,16},{9,... | collective-permute-start | bytes 983048 | tf_op jit(solution)/shard_map/ppermute | solution.py:448
  27.0 3.0 %collective-permute-done.7.refs_2_.refs_1_ = bf16[640,256]{1,0:T(8,128)(2,1)S(1)} collective-permute-done((bf16[640,256]{1,0:T(8,128)(2,1)S(1)}, bf16[640,256]{1,0:T(8,128)(2,1)S(1)}, u32[]{:S(2)}, u32[]{:S(2)}) %collective-permute-start.7) | collective-permute-done | bytes 327712 | tf_op jit(solution)/shard_map/ppermute | solution.py:448
  30.0 1.5 %collective-permute-start.12 = (bf16[640,256]{1,0:T(8,128)(2,1)S(1)}, bf16[640,256]{1,0:T(8,128)(2,1)S(1)}, u32[]{:S(2)}, u32[]{:S(2)}) collective-permute-start(bf16[640,256]{1,0:T(8,128)(2,1)S(1)} %collective-permute-done.7.refs_2_.refs_1_), channel_id=1, source_target_pairs={{0,1},{1,0},{2,3},{3,2},{4,5},{5,4},{6,7},{7,6},{8,9},{9,8},{10,11... | collective-permute-start | bytes 983048 | tf_op jit(solution)/shard_map/ppermute | solution.py:448
  31.5 0.6 %collective-permute-done.4.refs_2_ = bf16[640,256]{1,0:T(8,128)(2,1)S(1)} collective-permute-done((bf16[640,256]{1,0:T(8,128)(2,1)S(1)}, bf16[640,256]{1,0:T(8,128)(2,1)S(1)}, u32[]{:S(2)}, u32[]{:S(2)}) %collective-permute-start.4) | collective-permute-done | bytes 327712 | tf_op jit(solution)/shard_map/ppermute | solution.py:448
  32.1 0.2 collective-permute-start.11
  32.3 1.2 %collective-permute-start.5 = (bf16[640,256]{1,0:T(8,128)(2,1)S(1)}, bf16[640,256]{1,0:T(8,128)(2,1)S(1)}, u32[]{:S(2)}, u32[]{:S(2)}) collective-permute-start(bf16[640,256]{1,0:T(8,128)(2,1)S(1)} %collective-permute-done.4.refs_2_), channel_id=1, source_target_pairs={{0,24},{1,25},{2,26},{3,27},{4,28},{5,29},{6,30},{7,31},{8,16},{9,... | collective-permute-start | bytes 983048 | tf_op jit(solution)/shard_map/ppermute | solution.py:448
  33.5 4.0 %received_blocks.4 = (bf16[169,6144]{1,0:T(8,128)(2,1)}, bf16[128,256]{1,0:T(8,128)(2,1)S(1)}, bf16[3,256,128]{2,1,0:T(8,128)(2,1)S(1)}) custom-call(bf16[640,256]{1,0:T(8,128)(2,1)S(1)} %constant_dynamic-update-slice_fusion.2.refs_0_, bf16[640,256]{1,0:T(8,128)(2,1)S(1)} %collective-permute-done.6.refs_1_, ...), custom_call_target="tpu_custom_call" | custom-call | flops 4000000000 | bytes 1048576 | tf_op jit(solution)/shard_map/received_blocks/pallas_call | solution.py:373
  37.5 3.7 %received_blocks.5 = (bf16[169,6144]{1,0:T(8,128)(2,1)}, bf16[128,256]{1,0:T(8,128)(2,1)S(1)}) custom-call(bf16[640,256]{1,0:T(8,128)(2,1)S(1)} %constant_dynamic-update-slice_fusion.refs_0_, bf16[640,256]{1,0:T(8,128)(2,1)S(1)} %collective-permute-done.9.refs_1_, ...), custom_call_target="tpu_custom_call", output_to_operand_aliasing={{0}: (10, {})} | custom-call | flops 4000000000 | bytes 1048576 | tf_op jit(solution)/shard_map/received_blocks/pallas_call | solution.py:373
  41.2 2.2 %received_blocks.6 = (bf16[169,6144]{1,0:T(8,128)(2,1)}, bf16[64,256]{1,0:T(8,128)(2,1)S(1)}) custom-call(bf16[640,256]{1,0:T(8,128)(2,1)S(1)} %constant_dynamic-update-slice_fusion.2.refs_0_, bf16[640,256]{1,0:T(8,128)(2,1)S(1)} %collective-permute-done.7.refs_2_.refs_1_, ...), custom_call_target="tpu_custom_call", output_to_operand_aliasing={{0}: (10, {})} | custom-call | flops 2000000000 | bytes 1048576 | tf_op jit(solution)/shard_map/received_blocks/pallas_call | solution.py:373
  43.4 0.4 collective-permute-done.5.refs_3_
  43.8 6.2 %received_blocks.7 = (bf16[169,6144]{1,0:T(8,128)(2,1)}, bf16[169,4096]{1,0:T(8,128)(2,1)}) custom-call(bf16[640,256]{1,0:T(8,128)(2,1)S(1)} %constant_dynamic-update-slice_fusion.refs_0_, bf16[640,256]{1,0:T(8,128)(2,1)S(1)} %collective-permute-done.3.refs_1_, ...), custom_call_target="tpu_custom_call", output_to_operand_aliasing={{0}: (18, {})} | custom-call | flops 2000000000 | bytes 1048576 | tf_op jit(solution)/shard_map/received_blocks/pallas_call | solution.py:373
  (15 shorter events, 0.2 us)
Async XLA Ops:
  2.7 11.9 %collective-permute-start.1 = (bf16[320,256]{1,0:T(8,128)(2,1)S(1)}, bf16[320,256]{1,0:T(8,128)(2,1)S(1)}, u32[]{:S(2)}, u32[]{:S(2)}) collective-permute-start(bf16[320,256]{1,0:T(8,128)(2,1)S(1)} %get-tuple-element.28), channel_id=1, source_target_pairs={{0,4},{1,5},{2,6},{3,7},{4,0},{5,1},{6,2},{7,3},{8,12},{9,13},{10,... | collective-permute-start | bytes 491528 | tf_op jit(solution)/shard_map/ppermute | solution.py:448
  6.8 8.0 %collective-permute-start = (bf16[320,256]{1,0:T(8,128)(2,1)S(1)}, bf16[320,256]{1,0:T(8,128)(2,1)S(1)}, u32[]{:S(2)}, u32[]{:S(2)}) collective-permute-start(bf16[320,256]{1,0:T(8,128)(2,1)S(1)} %get-tuple-element.27), channel_id=1, source_target_pairs={{0,2},{1,3},{2,0},{3,1},{4,6},{5,7},{6,4},{7,5},{8,10},{9,11},{10,... | collective-permute-start | bytes 491528 | tf_op jit(solution)/shard_map/ppermute | solution.py:448
  14.8 5.3 %collective-permute-start.2 = (bf16[320,256]{1,0:T(8,128)(2,1)S(1)}, bf16[320,256]{1,0:T(8,128)(2,1)S(1)}, u32[]{:S(2)}, u32[]{:S(2)}) collective-permute-start(bf16[320,256]{1,0:T(8,128)(2,1)S(1)} %collective-permute-done.1), channel_id=1, source_target_pairs={{0,2},{1,3},{2,0},{3,1},{4,6},{5,7},{6,4},{7,5},{8,10},{9,11},{10,... | collective-permute-start | bytes 491528 | tf_op jit(solution)/shard_map/ppermute | solution.py:448
  16.3 8.4 %collective-permute-start.8 = (bf16[640,256]{1,0:T(8,128)(2,1)S(1)}, bf16[640,256]{1,0:T(8,128)(2,1)S(1)}, u32[]{:S(2)}, u32[]{:S(2)}) collective-permute-start(bf16[640,256]{1,0:T(8,128)(2,1)S(1)} %constant_dynamic-update-slice_fusion.2.refs_0_), channel_id=1, source_target_pairs={{0,1},{1,0},{2,3},{3,2},{4,5},{5,4},{6,7},{7,6},{8,9},{9,8},{10,11... | collective-permute-start | bytes 983048 | tf_op jit(solution)/shard_map/ppermute | solution.py:448
  20.2 4.5 %collective-permute-start.9 = (bf16[640,256]{1,0:T(8,128)(2,1)S(1)}, bf16[640,256]{1,0:T(8,128)(2,1)S(1)}, u32[]{:S(2)}, u32[]{:S(2)}) collective-permute-start(bf16[640,256]{1,0:T(8,128)(2,1)S(1)} %constant_dynamic-update-slice_fusion.refs_0_), channel_id=1, source_target_pairs={{0,8},{1,9},{2,10},{3,11},{4,12},{5,13},{6,14},{7,15},{8,0},{9,1},... | collective-permute-start | bytes 983048 | tf_op jit(solution)/shard_map/ppermute | solution.py:448
  20.2 9.7 %collective-permute-start.7 = (bf16[640,256]{1,0:T(8,128)(2,1)S(1)}, bf16[640,256]{1,0:T(8,128)(2,1)S(1)}, u32[]{:S(2)}, u32[]{:S(2)}) collective-permute-start(bf16[640,256]{1,0:T(8,128)(2,1)S(1)} %constant_dynamic-update-slice_fusion.2.refs_0_), channel_id=1, source_target_pairs={{0,24},{1,25},{2,26},{3,27},{4,28},{5,29},{6,30},{7,31},{8,16},{9,... | collective-permute-start | bytes 983048 | tf_op jit(solution)/shard_map/ppermute | solution.py:448
  21.9 10.3 %collective-permute-start.6 = (bf16[640,256]{1,0:T(8,128)(2,1)S(1)}, bf16[640,256]{1,0:T(8,128)(2,1)S(1)}, u32[]{:S(2)}, u32[]{:S(2)}) collective-permute-start(bf16[640,256]{1,0:T(8,128)(2,1)S(1)} %constant_dynamic-update-slice_fusion.2.refs_0_), channel_id=1, source_target_pairs={{0,8},{1,9},{2,10},{3,11},{4,12},{5,13},{6,14},{7,15},{8,0},{9,1},... | collective-permute-start | bytes 983048 | tf_op jit(solution)/shard_map/ppermute | solution.py:448
  22.0 10.1 %collective-permute-start.4 = (bf16[640,256]{1,0:T(8,128)(2,1)S(1)}, bf16[640,256]{1,0:T(8,128)(2,1)S(1)}, u32[]{:S(2)}, u32[]{:S(2)}) collective-permute-start(bf16[640,256]{1,0:T(8,128)(2,1)S(1)} %constant_dynamic-update-slice_fusion.refs_0_), channel_id=1, source_target_pairs={{0,1},{1,0},{2,3},{3,2},{4,5},{5,4},{6,7},{7,6},{8,9},{9,8},{10,11... | collective-permute-start | bytes 983048 | tf_op jit(solution)/shard_map/ppermute | solution.py:448
  24.7 8.8 %collective-permute-start.10 = (bf16[640,256]{1,0:T(8,128)(2,1)S(1)}, bf16[640,256]{1,0:T(8,128)(2,1)S(1)}, u32[]{:S(2)}, u32[]{:S(2)}) collective-permute-start(bf16[640,256]{1,0:T(8,128)(2,1)S(1)} %collective-permute-done.8.refs_3_.refs_2_), channel_id=1, source_target_pairs={{0,8},{1,9},{2,10},{3,11},{4,12},{5,13},{6,14},{7,15},{8,0},{9,1},... | collective-permute-start | bytes 983048 | tf_op jit(solution)/shard_map/ppermute | solution.py:448
  24.7 18.7 %collective-permute-start.3 = (bf16[640,256]{1,0:T(8,128)(2,1)S(1)}, bf16[640,256]{1,0:T(8,128)(2,1)S(1)}, u32[]{:S(2)}, u32[]{:S(2)}) collective-permute-start(bf16[640,256]{1,0:T(8,128)(2,1)S(1)} %constant_dynamic-update-slice_fusion.refs_0_), channel_id=1, source_target_pairs={{0,24},{1,25},{2,26},{3,27},{4,28},{5,29},{6,30},{7,31},{8,16},{9,... | collective-permute-start | bytes 983048 | tf_op jit(solution)/shard_map/ppermute | solution.py:448
  30.0 11.2 %collective-permute-start.12 = (bf16[640,256]{1,0:T(8,128)(2,1)S(1)}, bf16[640,256]{1,0:T(8,128)(2,1)S(1)}, u32[]{:S(2)}, u32[]{:S(2)}) collective-permute-start(bf16[640,256]{1,0:T(8,128)(2,1)S(1)} %collective-permute-done.7.refs_2_.refs_1_), channel_id=1, source_target_pairs={{0,1},{1,0},{2,3},{3,2},{4,5},{5,4},{6,7},{7,6},{8,9},{9,8},{10,11... | collective-permute-start | bytes 983048 | tf_op jit(solution)/shard_map/ppermute | solution.py:448
  32.1 5.4 %collective-permute-start.11 = (bf16[640,256]{1,0:T(8,128)(2,1)S(1)}, bf16[640,256]{1,0:T(8,128)(2,1)S(1)}, u32[]{:S(2)}, u32[]{:S(2)}) collective-permute-start(bf16[640,256]{1,0:T(8,128)(2,1)S(1)} %collective-permute-done.4.refs_2_), channel_id=1, source_target_pairs={{0,8},{1,9},{2,10},{3,11},{4,12},{5,13},{6,14},{7,15},{8,0},{9,1},... | collective-permute-start | bytes 983048 | tf_op jit(solution)/shard_map/ppermute | solution.py:448
  32.3 11.5 %collective-permute-start.5 = (bf16[640,256]{1,0:T(8,128)(2,1)S(1)}, bf16[640,256]{1,0:T(8,128)(2,1)S(1)}, u32[]{:S(2)}, u32[]{:S(2)}) collective-permute-start(bf16[640,256]{1,0:T(8,128)(2,1)S(1)} %collective-permute-done.4.refs_2_), channel_id=1, source_target_pairs={{0,24},{1,25},{2,26},{3,27},{4,28},{5,29},{6,30},{7,31},{8,16},{9,... | collective-permute-start | bytes 983048 | tf_op jit(solution)/shard_map/ppermute | solution.py:448
  41.2 2.6 %copy-start = (bf16[256,169]{0,1:T(8,128)(2,1)S(1)}, bf16[256,169]{0,1:T(8,128)(2,1)}, u32[]{:S(2)}) copy-start(bf16[256,169]{0,1:T(8,128)(2,1)} %param.23) | copy-start | bytes 259588

commit v4 on v3

--- a/solution.py
+++ b/solution.py
@@ -71,10 +71,10 @@
         self.slot = self.pairs // (2 * self.cells)
         self.part = self.fetch // 3
         self.groups = 3 * self.inner
-        self.section = PLANES * self.groups
-        self.meta = 2 * self.section
+        self.meta = PLANES * self.groups
         self.per_row = self.width // LIST
-        self.rows = up(self.atoms + self.meta + -(-self.cells // self.per_row), 16)
+        self.tail = up(self.meta + -(-self.cells // self.per_row), 16)
+        self.rows = self.atoms + self.tail
         self.entries = w_out.shape[1]
         self.orbitals = int(self.entries**0.5 + 0.5)
 
@@ -112,18 +112,15 @@
     mask = lax.broadcasted_iota(jnp.int32, (total, n.pairs), 0) == hi
     spread = jnp.concatenate([jnp.where(mask, p, 0.0) for p in planes], 0).astype(BF16)
     placed = dot(spread, onehot(lo, n.slot), 1, 1).astype(BF16)
-    tail = n.rows - n.atoms
-    shape = (tail, PLANES * total)
+    shape = (n.tail, PLANES * total)
     r = lax.broadcasted_iota(jnp.int32, shape, 0)
     q = lax.broadcasted_iota(jnp.int32, shape, 1)
-    section = whole_div(r, n.section)
-    g = whole_div(r - section * n.section, PLANES)
-    plane = r - section * n.section - g * PLANES
+    g = whole_div(r, PLANES)
+    plane = r - g * PLANES
     role = whole_div(g, n.inner)
     o = jnp.where(role == 0, 1, jnp.where((role == 1) == even, 2, 0))
     base = plane * total + o * n.cells + jnp.bitwise_xor(g - role * n.inner, xi)
     base = jnp.where(r < n.meta, base, -n.pairs)
-    section = jnp.where(r < n.meta, section, 0)
     e = list_ref[...]
     kk = lax.broadcasted_iota(jnp.int32, e.shape, 1)
     e = (e - (kk - whole_div(kk, 3) * 3) * n.atoms).astype(F32)
@@ -133,23 +130,30 @@
     lane = lax.broadcasted_iota(jnp.int32, flat.shape, 1)
     at_row = whole_div(j, n.per_row)
     flat = jnp.where(whole_div(lane, LIST) == j - at_row * n.per_row, flat, 0.0).astype(BF16)
-    put_r = lax.broadcasted_iota(jnp.int32, (tail, n.cells), 0)
-    put_j = lax.broadcasted_iota(jnp.int32, (tail, n.cells), 1)
+    put_r = lax.broadcasted_iota(jnp.int32, (n.tail, n.cells), 0)
+    put_j = lax.broadcasted_iota(jnp.int32, (n.tail, n.cells), 1)
     put = (put_r == n.meta + whole_div(put_j, n.per_row)).astype(BF16)
     lists = dot(put, flat)
     feat = feat_ref[...]
-    for b, out in zip(sent_steps(n), outs):
-        plane_of = jnp.bitwise_xor(jnp.bitwise_xor(zi, b), section)
-        pick = (base + plane_of * n.inner == q).astype(BF16)
-        out[0 : n.atoms, :] = feat
+
+    def tail(b):
+        pick = (base + jnp.bitwise_xor(zi, b) * n.inner == q).astype(BF16)
         pairs = dot(pick, placed)
         if n.slot < n.width:
-            pairs = jnp.concatenate([pairs, jnp.zeros((tail, n.width - n.slot), F32)], 1)
-        out[n.atoms :, :] = (pairs + lists).astype(BF16)
-
-
-def lists_of(n, tile):
-    tail = tile[n.atoms :, :].astype(F32)
+            pairs = jnp.concatenate([pairs, jnp.zeros((n.tail, n.width - n.slot), F32)], 1)
+        return (pairs + lists).astype(BF16)
+
+    for b, out in zip(sent_steps(n), outs):
+        top = 0
+        if b > 1:
+            out[0 : n.tail, :] = tail(b + 1)
+            top = n.tail
+        out[top : top + n.atoms, :] = feat
+        out[top + n.atoms :, :] = tail(b)
+
+
+def lists_of(n, tail):
+    tail = tail.astype(F32)
     rows = []
     for j in range(n.cells):
         r = n.meta + j // n.per_row
@@ -162,7 +166,10 @@
     args = (pair_atom, partner_row, transpose_slot, distance, send_rows, features)
     return pl.pallas_call(
         functools.partial(tiles_kernel, n),
-        out_shape=[jax.ShapeDtypeStruct((n.rows, n.width), BF16)] * len(sent_steps(n)),
+        out_shape=[
+            jax.ShapeDtypeStruct((n.rows + (n.tail if b > 1 else 0), n.width), BF16)
+            for b in sent_steps(n)
+        ],
         compiler_params=pltpu.CompilerParams(vmem_limit_bytes=LIMIT),
         cost_estimate=cost(600_000_000),
         name="place_pairs",
@@ -212,8 +219,8 @@
     )(*far(distance, pair_atom), left, w_in_t, w_ro_t)
 
 
-def partner_table(n, even, tiles, w_right_t, table_ref):
-    right = dot(w_right_t, tiles[0][0 : n.atoms, :], 1, 1).astype(BF16)
+def partner_table(n, even, feat, tails, w_right_t, table_ref):
+    right = dot(w_right_t, feat, 1, 1).astype(BF16)
     lanes = n.cells * n.part
     k = lax.broadcasted_iota(jnp.int32, (n.fetch, lanes), 0)
     lane = lax.broadcasted_iota(jnp.int32, (n.fetch, lanes), 1)
@@ -222,24 +229,23 @@
     cell = whole_div(lax.broadcasted_iota(jnp.int32, (n.cells, lanes), 1), n.part)
     o_sib = jnp.where(even, 0, 2)
     for role, o in enumerate((1, o_sib, 2 - o_sib)):
-        lists = lists_of(n, tiles[role]).astype(BF16)
+        lists = lists_of(n, tails[role]).astype(BF16)
         per = dot(lists, (k == m3 + o).astype(BF16))
         index = jnp.sum(jnp.where(mine == cell, per, 0.0), 0, keepdims=True)
         table_ref[role] = dot(right, onehot(index.astype(jnp.int32), n.atoms)).astype(BF16)
 
 
-def received_kernel(n, steps, sections, have, used, first, direct, count, final, *refs):
+def received_kernel(n, steps, have, used, first, direct, count, final, *refs):
     held, refs = refs[:count], refs[count:]
     if final:
-        calls, extra = final
+        calls, extra, old = final
         mine, refs = refs[:extra], refs[extra:]
-    if not first and direct:
-        refs = refs[1:]
-    outs, refs = refs[: 3 if first else 2], refs[3 if first else 2 :]
     if final:
-        (block_ref, own_ref), (rows_buf, own_buf, sem_own, blocks_buf, sem_out) = outs, refs
+        earlier, mine = mine[:old], mine[old:]
+        block_ref, own_ref, rows_buf, own_buf, sem_own, blocks_buf, sem_out = refs
     else:
-        (block_ref, rows_buf), (blocks_buf, sem_out) = outs[:2], refs
+        blocks_buf, rows_buf = refs[:2]
+    need = held.__getitem__
     need = held.__getitem__
 
     me, zi, xi, even = where_am_i()
@@ -247,30 +253,53 @@
     roles = (1, o_sib, 2 - o_sib)
     base = len(used)
     near = [(i, at) for i in range(len(steps)) for at in range(n.inner)]
-    order = [(role, i, at) for role in have for i, at in near]
+    order = [(role, i, at) for role, at in have for i in range(len(steps))]
     number = {key: g for g, key in enumerate(order)}
     cells = {
         (i, at): jnp.bitwise_xor(zi, steps[i]) * n.inner + jnp.bitwise_xor(xi, at) for i, at in near
     }
-    tiles = {
-        (u % 3, i, u // 3): need(used.index(u)).at[pl.ds(i * n.rows, n.rows)]
-        for u in used
-        for i in range(len(steps))
-    }
+    u_at = {u: j for j, u in enumerate(used)}
+    feat_of, tail_of = {}, {}
+    for u in used:
+        for i, b in enumerate(steps):
+            tail_first = b > 1 and b % 2 == 1
+            top, end = i * n.rows, (i + 1) * n.rows
+            cut_at = top + (n.tail if tail_first else n.atoms)
+            parts = need(u_at[u]).at[pl.ds(top, cut_at - top)], need(u_at[u]).at[pl.ds(cut_at, end - cut_at)]
+            tail_of[u % 3, i, u // 3], feat_of[u % 3, i, u // 3] = parts if tail_first else parts[::-1]
     done = []
+
+    def put(buf, at, order):
+        for g, (role, b, beside) in enumerate(order):
+            cell = jnp.bitwise_xor(zi, b) * n.inner + jnp.bitwise_xor(xi, beside)
+            start = pl.multiple_of((roles[role] * n.cells + cell) * n.slot, n.slot)
+            out = pltpu.make_async_copy(
+                buf.at[:, pl.ds(g * n.slot, n.slot)],
+                block_ref.at[:, pl.ds(start, n.slot)],
+                sem_out.at[at + g],
+            )
+            out.start()
+            done.append(out)
+
+    if final and direct:
+        sent = len(order)
+        for buf, (planes, kinds) in zip(earlier, calls):
+            spots = [(role, b, beside) for role, beside in kinds for b in planes]
+            put(buf, sent, spots)
+            sent += len(spots)
     if first:
-        own = [tiles[role, 0, 0] for role in range(3)]
-        table = outs[2]
-        partner_table(n, even, own, need(base + 5)[...], table)
+        tails = [tail_of[role, 0, 0][...] for role in range(3)]
+        table = refs[2]
+        partner_table(n, even, feat_of[0, 0, 0][...], tails, need(base + 5)[...], table)
     else:
         table = need(base + 5)
-    feats = jnp.concatenate([tiles[key][0 : n.atoms, :] for key in order], 0)
+    feats = jnp.concatenate([feat_of[key][...] for key in order], 0)
     left = dot(need(base)[...], feats, 1, 1).astype(BF16)
 
     slabs = []
     for role, i, at in order:
-        top = sections[i] * n.section + (role * n.inner + at) * PLANES
-        tail = tiles[role, i, at][n.atoms :, 0 : n.slot].astype(F32)
+        top = (role * n.inner + at) * PLANES
+        tail = tail_of[role, i, at][:, 0 : n.slot].astype(F32)
         slabs.append(tail[top : top + PLANES])
     meta = jnp.concatenate(slabs, 1)
     dists = meta[0:1] + meta[1:2] + meta[2:3]
@@ -282,8 +311,9 @@
 
     gate = gate_of(dists, need(base + 1)[...], need(base + 2)[...])
     rights = []
-    for role in have:
-        place = [cut(spots, number[role, i, at]) + cells[i, at] * n.part for i, at in near]
+    for role in sorted({role for role, _ in have}):
+        asking = [key for key in order if key[0] == role]
+        place = [cut(spots, number[key]) + cells[key[1:]] * n.part for key in asking]
         rights.append(dot(table[role], onehot(jnp.concatenate(place, 1), n.cells * n.part)))
     lefts = [
         dot(left[:, g * n.atoms : (g + 1) * n.atoms], onehot(cut(atoms, g), n.atoms))
@@ -292,17 +322,8 @@
     edge = jnp.concatenate(lefts, 1) * jnp.concatenate(rights, 1) * gate
     mixed = silu(dot(need(base + 3)[...], edge.astype(BF16))).astype(BF16)
     blocks_buf[...] = dot(need(base + 4)[...], mixed).astype(BF16)
-    if direct:
-        for g, (role, i, at) in enumerate(order):
-            place = roles[role] * n.cells + cells[i, at]
-            start = pl.multiple_of(place * n.slot, n.slot)
-            out = pltpu.make_async_copy(
-                blocks_buf.at[:, pl.ds(g * n.slot, n.slot)],
-                block_ref.at[:, pl.ds(start, n.slot)],
-                sem_out.at[g],
-            )
-            out.start()
-            done.append(out)
+    if final and direct:
+        put(blocks_buf, 0, [(role, steps[i], at) for role, i, at in order])
 
     rows = len(order) * n.part
     my_list = lax.broadcasted_iota(jnp.int32, (n.cells, n.fetch), 0) == me
@@ -310,8 +331,8 @@
     k = lax.broadcasted_iota(jnp.int32, (n.part, n.fetch), 1)
     m3 = 3 * lax.broadcasted_iota(jnp.int32, (n.part, n.fetch), 0)
     asked = {}
-    for i, at in near:
-        lists = lists_of(n, tiles[0, i, at])
+    for i, at in sorted({key[1:] for key in order}):
+        lists = lists_of(n, tail_of[0, i, at][...])
         asked[i, at] = jnp.sum(jnp.where(my_list, lists, 0.0), 0, keepdims=True)
     for g, (role, i, at) in enumerate(order):
         o_own = 1 if role == 0 else 2 - roles[role]
@@ -320,7 +341,7 @@
     lane = lax.broadcasted_iota(jnp.int32, (rows, len(order) * n.atoms), 1)
     pick = (lane == jnp.concatenate(index, 0)).astype(BF16)
     rows_buf[...] = dot(pick, feats).astype(BF16)
-    if not direct:
+    if final and not direct:
         out = pltpu.make_async_copy(blocks_buf, block_ref, sem_out.at[0])
         out.start()
         done.append(out)
@@ -331,60 +352,53 @@
         out.wait()
 
 
-def received(n, steps, sections, have, tiles, weights, table, w_right_t, into, own=None):
+def received(n, steps, have, tiles, weights, table, w_right_t, own=None):
     first = table is None
     direct = n.slot % 128 == 0
-    used = [0, 1, 2, 3, 4, 5] if first else [0, 3] + [3 * at + r for at in (0, 1) for r in have if r]
-    if first and 2 not in have:
-        used.remove(5)
-    used = sorted(set(used))
+    used = {u for role, at in have for u in (3 * at, 3 * at + role)}
+    used = sorted(used | ({0, 1, 2} if first else set()))
     operands = [tiles[u] for u in used] + list(weights) + [w_right_t if first else table]
     count = len(operands)
-    calls = None
-    if own is not None:
-        calls, extra = own
-        operands += extra
-    near = len(operands)
-    groups = n.inner * len(have) * len(steps)
+    groups = len(have) * len(steps)
     blocks = (n.entries, groups * n.slot)
     rows = (groups * n.part, n.width)
-    shape = (3, n.width, n.cells * n.part)
-    out_shape = [jax.ShapeDtypeStruct((n.entries, 3 * n.cells * n.slot) if direct else blocks, BF16)]
-    scratch = [pltpu.VMEM(blocks, BF16), pltpu.SemaphoreType.DMA((groups,))]
     fast, slow = pl.BlockSpec(memory_space=pltpu.VMEM), pl.BlockSpec(memory_space=pl.ANY)
-    if own is not None:
-        out_shape.append(jax.ShapeDtypeStruct((n.entries, n.pairs), BF16))
+    final, scratch = None, []
+    if own is None:
+        out_shape = [jax.ShapeDtypeStruct(blocks, BF16), jax.ShapeDtypeStruct(rows, BF16)]
+        out_specs = [fast, fast]
+        if first:
+            shape = (3, n.width, n.cells * n.part)
+            out_shape.append(jax.ShapeDtypeStruct(shape, BF16))
+            out_specs.append(fast)
+    else:
+        calls, earlier, extra = own
+        total = 3 * n.cells
+        operands += [*earlier, *extra]
+        final = calls, len(operands) - count, len(earlier)
+        shape = (n.entries, total * n.slot) if direct else blocks
+        out_shape = [
+            jax.ShapeDtypeStruct(shape, BF16),
+            jax.ShapeDtypeStruct((n.entries, n.pairs), BF16),
+        ]
         out_specs = [slow, slow]
         scratch = [
             pltpu.VMEM(rows, BF16),
             pltpu.VMEM((n.entries, n.pairs), BF16),
             pltpu.SemaphoreType.DMA((2,)),
-        ] + scratch
-    else:
-        out_shape.append(jax.ShapeDtypeStruct(rows, BF16))
-        out_specs = [slow, fast]
-    if first:
-        out_shape.append(jax.ShapeDtypeStruct(shape, BF16))
-        out_specs.append(fast)
-    aliases = {}
-    if direct and not first:
-        aliases = {near: 0}
-        operands.append(into)
-    out = pl.pallas_call(
-        functools.partial(
-            received_kernel, n, steps, sections, have, tuple(used), first, direct, count,
-            (calls, near - count) if calls else None,
-        ),
-        in_specs=[fast] * near + [slow] * (len(operands) - near),
+            pltpu.VMEM(blocks, BF16),
+            pltpu.SemaphoreType.DMA((total if direct else 1,)),
+        ]
+    return pl.pallas_call(
+        functools.partial(received_kernel, n, steps, have, tuple(used), first, direct, count, final),
+        in_specs=[fast] * len(operands),
         out_specs=out_specs,
         out_shape=out_shape,
         scratch_shapes=scratch,
-        input_output_aliases=aliases,
         compiler_params=pltpu.CompilerParams(vmem_limit_bytes=LIMIT),
         cost_estimate=cost(500_000_000 * groups),
         name="received_blocks",
     )(*operands)
-    return out[0], out[1], out[2] if first else table
 
 
 def own_part(n, calls, mine, w_mix, last, own_buf, own_ref, sem, even, zi, xi):
@@ -403,11 +417,12 @@
     b = jnp.bitwise_xor(outer, zi)
     place, top = b, 0
     for steps, have in calls:
-        for r in have:
+        for r, beside in have:
             for step in steps:
-                place = jnp.where((b == step) & (role == r), top, place)
+                here = (b == step) & (role == r) & (jnp.bitwise_xor(inner, xi) == beside)
+                place = jnp.where(here, top, place)
                 top += 1
-    place = (place * n.inner + jnp.bitwise_xor(inner, xi)) * n.part + m
+    place = place * n.part + m
     done, at = [], 0
     for i, half in enumerate(halves):
         step = half.shape[1]
@@ -484,46 +499,42 @@
     lines_in[1], lines_in[2], second = lax.optimization_barrier((lines_in[1], lines_in[2], second))
     w_left_t, w_right_t, w_in_t, w_ro_t, w_mix_t, w_flip_t = turned
     weights = (w_left_t, w_in_t, w_ro_t, w_mix_t, w_flip_t)
-    table, into, tables, parts, calls = None, None, [], [], []
-
-    def take(at, have, table, into, own=None):
-        steps, sections, group = sets[at]
-        into, rows, table = received(
-            n, steps, sections, have, group, weights, table, w_right_t, into, own
-        )
+    tables, parts, calls = [], [], []
+
+    def take(at, have, table):
+        steps, group = sets[at]
+        blocks, rows, *new = received(n, steps, have, group, weights, table, w_right_t)
         tables.append(rows)
-        parts.append(into)
+        parts.append(blocks)
         calls.append((steps, have))
-        return table, into
+        return new[0] if new else table
 
     sets, chain = [], []
     for b in range(0, n.outer, 2):
-        tile = jnp.concatenate([lines_in[b], lines_in[b + 1]], 0)
+        tile = jnp.concatenate([lines_in[b][-n.rows :], lines_in[b + 1][: n.rows]], 0)
         chain.append([tile, exchange(tile, sibling), exchange(tile, other), exchange(tile, beside)])
-        if b:
-            before, now = chain[-2], chain[-1]
-            before[3], now[1] = lax.optimization_barrier((before[3], now[1]))
     for i, (tile, close, away, across) in enumerate(chain):
-        steps, sections = (2 * i, 2 * i + 1), (0, 1 if i else 0)
-        if i:
-            table, into = take(i - 1, (0, 1), table, into)
-        corner = exchange(across, other) if i % 2 else exchange(away, beside)
-        group = [tile, close, away, across, exchange(across, sibling), corner]
-        sets.append((steps, sections, group))
-    last = len(sets) - 1
-    table, into = take(last, (0, 1), table, into)
+        corner_tile = exchange(across, other) if i % 2 else exchange(away, beside)
+        group = [tile, close, away, across, exchange(across, sibling), corner_tile]
+        sets.append(((2 * i, 2 * i + 1), group))
+    last, table = len(sets) - 1, None
+    same_strips, away_near, away_far = ((0, 0), (0, 1), (1, 0), (1, 1)), ((2, 0),), ((2, 1),)
+    for i in range(last + 1):
+        table = take(i, same_strips, table)
     for i in range(last):
-        table, into = take(i, (2,), table, into)
-    every = tuple(calls) + ((sets[last][0], (2,)),)
-    own = (every, [*far(partner_row), held, second, w_right_t, w_out.T, *tables])
-    table, into = take(last, (2,), table, into, own)
-    own = tables.pop()
+        table = take(i, away_near + away_far, table)
+    table = take(last, away_near, table)
+    every = (*calls, (sets[last][0], away_far))
+    earlier = parts if n.slot % 128 == 0 else []
+    own = (every, earlier, [*far(partner_row), held, second, w_right_t, w_out.T, *tables])
+    into, own = received(n, sets[last][0], away_far, sets[last][1], weights, table, w_right_t, own)
     if n.slot % 128:
         cell, strip = lax.axis_index("cell"), lax.axis_index("strip")
         o_sib = jnp.where(strip % 2 == 0, 0, 2)
+        parts.append(into)
         into = jnp.zeros((n.entries, 3 * n.cells * n.slot), BF16)
-        for (steps, have), blocks in zip(calls, parts):
-            order = [(role, b, at) for role in have for b in steps for at in (0, 1)]
+        for (steps, have), blocks in zip(every, parts):
+            order = [(role, b, at) for role, at in have for b in steps]
             for g, (role, b, at) in enumerate(order):
                 piece = blocks[:, g * n.slot : (g + 1) * n.slot]
                 spot = (1, o_sib, 2 - o_sib)[role] * n.cells + (cell ^ (b * n.inner + at))

time: 50.6 us -> 47.7 us (0.943)
  starting transfers between devices: 17.2 us -> 15.4 us
  Pallas kernels: 23 us -> 21.8 us
    ppermute x13, starting transfers between devices: 17.2 us -> 15.4 us  [exchange(): return lax.ppermute(x, AXES, pairs)]
    pallas_call x4 -> x5, Pallas kernels: 16.1 us -> 14.9 us  [received(): pl.pallas_call(functools.partial(received_kernel, n, steps, have, tuple(u...]
  transfers between devices with their start and end apart: 13 -> 13, of which waited for: 7 -> 5; matrix products, arithmetic and copies ran while one was open for 0% -> 0% of each run, Pallas kernels for 29% -> 29%
where the time goes in v4:
time: 47.7 us; the launch traced here: 47.2 us
  Pallas kernels  21.8 us (46%)
  starting transfers between devices  15.4 us (32%)
  waiting for transfers between devices  8.89 us (19%)
  between operations  0.93 us (2%)
    ppermute x13, starting transfers between devices, exchange(): return lax.ppermute(x, AXES, pairs)  15.4 us
    pallas_call x5, Pallas kernels, received(): pl.pallas_call(functools.partial(received_kernel, n, steps, have, tuple(u...  14.9 us
    ppermute x13, waiting for transfers between devices, exchange(): return lax.ppermute(x, AXES, pairs)  8.89 us
    pallas_call x1, Pallas kernels, first_gate(): pl.pallas_call(functools.partial(first_gate_kernel, n, step), out_shape=[...  2.67 us
    pallas_call x1, Pallas kernels, second_gate(): pl.pallas_call(functools.partial(second_gate_kernel, n, step), out_shape=...  2.13 us
    pallas_call x1, Pallas kernels, make_tiles(): pl.pallas_call(functools.partial(tiles_kernel, n), out_shape=[jax.ShapeDt...  2.09 us
  transfers between devices with their start and end apart: 13, of which 5 were waited for; matrix products, arithmetic and copies ran while one was open for 0% of the time, Pallas kernels for 29%

profile of v4, /device:TPU:0, one launch (start us, length us, event | category | flops | bytes accessed | tf_op | source)
XLA Modules:
  0.0 47.2 jit_solution(1563468566190934239)
XLA Ops:
  0.6 2.1 %place_pairs.1 = (bf16[288,256]{1,0:T(8,128)(2,1)S(1)}, bf16[288,256]{1,0:T(8,128)(2,1)S(1)}, bf16[320,256]{1,0:T(8,128)(2,1)S(1)}) custom-call(s32[1,4096]{1,0:T(1,128)} %bitcast.10, s32[1,4096]{1,0:T(1,128)} %bitcast.7, s32[1,4096]{1,0:T(1,128)} %bitcast.9, f32[1,4096]{1,0:T(1,128)} %bitcast.13, s32[8,48]{1,0:T(8,128)} %list_ref.1, bf16[256,256]{1,0:T(8,128)(2,1)} %feat_ref.3), custom_call_target="tpu_custom_call" | custom-call | flops 600000000 | bytes 1048576 | tf_op jit(solution)/shard_map/place_pairs/pallas_call | solution.py:167
  2.7 3.1 %collective-permute-start = (bf16[288,256]{1,0:T(8,128)(2,1)S(1)}, bf16[288,256]{1,0:T(8,128)(2,1)S(1)}, u32[]{:S(2)}, u32[]{:S(2)}) collective-permute-start(bf16[288,256]{1,0:T(8,128)(2,1)S(1)} %get-tuple-element.27), channel_id=1, source_target_pairs={{0,2},{1,3},{2,0},{3,1},{4,6},{5,7},{6,4},{7,5},{8,10},{9,11},{10,... | collective-permute-start | bytes 442376 | tf_op jit(solution)/shard_map/ppermute | solution.py:463
  5.8 2.6 %collective-permute-start.1 = (bf16[320,256]{1,0:T(8,128)(2,1)S(1)}, bf16[320,256]{1,0:T(8,128)(2,1)S(1)}, u32[]{:S(2)}, u32[]{:S(2)}) collective-permute-start(bf16[320,256]{1,0:T(8,128)(2,1)S(1)} %get-tuple-element.28), channel_id=1, source_target_pairs={{0,4},{1,5},{2,6},{3,7},{4,0},{5,1},{6,2},{7,3},{8,12},{9,13},{10,... | collective-permute-start | bytes 491528 | tf_op jit(solution)/shard_map/ppermute | solution.py:463
  8.4 2.7 %first_gate.1 = (f32[256,2048]{1,0:T(8,128)S(1)}, bf16[256,256]{1,0:T(8,128)(2,1)S(1)}, bf16[256,256]{1,0:T(8,128)(2,1)S(1)}, bf16[256,128]{1,0:T(8,128)(2,1)S(1...) custom-call(f32[1,4096]{1,0:T(1,128)} %bitcast.14, ...), custom_call_target="tpu_custom_call" | custom-call | flops 3000000000 | bytes 1048576 | tf_op jit(solution)/shard_map/first_gate/pallas_call | solution.py:202
  11.1 2.1 %second_gate.1.refs_14_ = f32[256,2048]{1,0:T(8,128)S(1)} custom-call(f32[1,4096]{1,0:T(1,128)} %bitcast.15, s32[1,4096]{1,0:T(1,128)} %bitcast.12, bf16[256,256]{1,0:T(8,128)(2,1)S(1)} %get-tuple-element.29.left_ref, bf16[256,128]{1,0:T(8,128)(2,1)S(1)} %get-tuple-element.30.w_in_ref.refs_6_.refs_5_.refs_3_, ...), custom_call_target="tpu_custom_call" | custom-call | flops 2000000000 | bytes 1048576 | tf_op jit(solution)/shard_map/second_gate/pallas_call | solution.py:213
  13.3 2.7 %collective-permute-done.1 = bf16[320,256]{1,0:T(8,128)(2,1)S(1)} collective-permute-done((bf16[320,256]{1,0:T(8,128)(2,1)S(1)}, bf16[320,256]{1,0:T(8,128)(2,1)S(1)}, u32[]{:S(2)}, u32[]{:S(2)}) %collective-permute-start.1) | collective-permute-done | bytes 163872 | tf_op jit(solution)/shard_map/ppermute | solution.py:463
  16.0 1.6 %collective-permute-start.7 = (bf16[576,256]{1,0:T(8,128)(2,1)S(1)}, bf16[576,256]{1,0:T(8,128)(2,1)S(1)}, u32[]{:S(2)}, u32[]{:S(2)}) collective-permute-start(bf16[576,256]{1,0:T(8,128)(2,1)S(1)} %constant_dynamic-update-slice_fusion.refs_0_), channel_id=1, source_target_pairs={{0,1},{1,0},{2,3},{3,2},{4,5},{5,4},{6,7},{7,6},{8,9},{9,8},{10,11... | collective-permute-start | bytes 884744 | tf_op jit(solution)/shard_map/ppermute | solution.py:463
  17.5 0.1 collective-permute-start.2
  17.6 1.6 %collective-permute-start.5 = (bf16[576,256]{1,0:T(8,128)(2,1)S(1)}, bf16[576,256]{1,0:T(8,128)(2,1)S(1)}, u32[]{:S(2)}, u32[]{:S(2)}) collective-permute-start(bf16[576,256]{1,0:T(8,128)(2,1)S(1)} %constant_dynamic-update-slice_fusion.refs_0_), channel_id=1, source_target_pairs={{0,8},{1,9},{2,10},{3,11},{4,12},{5,13},{6,14},{7,15},{8,0},{9,1},... | collective-permute-start | bytes 884744 | tf_op jit(solution)/shard_map/ppermute | solution.py:463
  19.3 3.6 %collective-permute-done.2 = bf16[320,256]{1,0:T(8,128)(2,1)S(1)} collective-permute-done((bf16[320,256]{1,0:T(8,128)(2,1)S(1)}, bf16[320,256]{1,0:T(8,128)(2,1)S(1)}, u32[]{:S(2)}, u32[]{:S(2)}) %collective-permute-start.2) | collective-permute-done | bytes 163872 | tf_op jit(solution)/shard_map/ppermute | solution.py:463
  22.9 0.6 %collective-permute-start.3 = (bf16[576,256]{1,0:T(8,128)(2,1)S(1)}, bf16[576,256]{1,0:T(8,128)(2,1)S(1)}, u32[]{:S(2)}, u32[]{:S(2)}) collective-permute-start(bf16[576,256]{1,0:T(8,128)(2,1)S(1)} %pad_maximum_fusion.refs_0_), channel_id=1, source_target_pairs={{0,1},{1,0},{2,3},{3,2},{4,5},{5,4},{6,7},{7,6},{8,9},{9,8},{10,11... | collective-permute-start | bytes 884744 | tf_op jit(solution)/shard_map/ppermute | solution.py:463
  23.5 2.3 %collective-permute-start.12 = (bf16[576,256]{1,0:T(8,128)(2,1)S(1)}, bf16[576,256]{1,0:T(8,128)(2,1)S(1)}, u32[]{:S(2)}, u32[]{:S(2)}) collective-permute-start(bf16[576,256]{1,0:T(8,128)(2,1)S(1)} %pad_maximum_fusion.refs_0_), channel_id=1, source_target_pairs={{0,24},{1,25},{2,26},{3,27},{4,28},{5,29},{6,30},{7,31},{8,16},{9,... | collective-permute-start | bytes 884744 | tf_op jit(solution)/shard_map/ppermute | solution.py:463
  25.7 1.1 %collective-permute-done.6.refs_2_.refs_1_ = bf16[576,256]{1,0:T(8,128)(2,1)S(1)} collective-permute-done((bf16[576,256]{1,0:T(8,128)(2,1)S(1)}, bf16[576,256]{1,0:T(8,128)(2,1)S(1)}, u32[]{:S(2)}, u32[]{:S(2)}) %collective-permute-start.6) | collective-permute-done | bytes 294944 | tf_op jit(solution)/shard_map/ppermute | solution.py:463
  26.8 0.2 collective-permute-start.9
  27.0 1.3 %collective-permute-start.11 = (bf16[576,256]{1,0:T(8,128)(2,1)S(1)}, bf16[576,256]{1,0:T(8,128)(2,1)S(1)}, u32[]{:S(2)}, u32[]{:S(2)}) collective-permute-start(bf16[576,256]{1,0:T(8,128)(2,1)S(1)} %collective-permute-done.6.refs_2_.refs_1_), channel_id=1, source_target_pairs={{0,1},{1,0},{2,3},{3,2},{4,5},{5,4},{6,7},{7,6},{8,9},{9,8},{10,11... | collective-permute-start | bytes 884744 | tf_op jit(solution)/shard_map/ppermute | solution.py:463
  28.3 1.4 %collective-permute-done.3.refs_2_.refs_0_ = bf16[576,256]{1,0:T(8,128)(2,1)S(1)} collective-permute-done((bf16[576,256]{1,0:T(8,128)(2,1)S(1)}, bf16[576,256]{1,0:T(8,128)(2,1)S(1)}, u32[]{:S(2)}, u32[]{:S(2)}) %collective-permute-start.3) | collective-permute-done | bytes 294944 | tf_op jit(solution)/shard_map/ppermute | solution.py:463
  29.7 2.1 %collective-permute-start.4 = (bf16[576,256]{1,0:T(8,128)(2,1)S(1)}, bf16[576,256]{1,0:T(8,128)(2,1)S(1)}, u32[]{:S(2)}, u32[]{:S(2)}) collective-permute-start(bf16[576,256]{1,0:T(8,128)(2,1)S(1)} %collective-permute-done.3.refs_2_.refs_0_), channel_id=1, source_target_pairs={{0,24},{1,25},{2,26},{3,27},{4,28},{5,29},{6,30},{7,31},{8,16},{9,... | collective-permute-start | bytes 884744 | tf_op jit(solution)/shard_map/ppermute | solution.py:463
  31.8 3.1 %received_blocks.5 = (bf16[169,2048]{1,0:T(8,128)(2,1)S(1)}, bf16[128,256]{1,0:T(8,128)(2,1)S(1)}, bf16[3,256,128]{2,1,0:T(8,128)(2,1)S(1)}) custom-call(bf16[576,256]{1,0:T(8,128)(2,1)S(1)} %constant_dynamic-update-slice_fusion.refs_0_, bf16[576,256]{1,0:T(8,128)(2,1)S(1)} %collective-permute-done.5.refs_1_, ...), custom_call_target="tpu_custom_call" | custom-call | flops 4000000000 | bytes 1048576 | tf_op jit(solution)/shard_map/received_blocks/pallas_call | solution.py:392
  34.9 1.2 %received_blocks.8 = (bf16[169,512]{1,0:T(8,128)(2,1)S(1)}, bf16[32,256]{1,0:T(8,128)(2,1)S(1)}) custom-call(bf16[576,256]{1,0:T(8,128)(2,1)S(1)} %pad_maximum_fusion.refs_0_, bf16[576,256]{1,0:T(8,128)(2,1)S(1)} %collective-permute-done.12.refs_1_, bf16[256,256]{1,0:T(8,128)(2,1)S(1)} %get-tuple-element.33.refs_5_.refs_4_.refs_2_, ...), custom_call_target="tpu_custom_call" | custom-call | flops 1000000000 | bytes 1048576 | tf_op jit(solution)/shard_map/received_blocks/pallas_call | solution.py:392
  36.1 0.2 collective-permute-done.11.refs_3_
  36.3 1.4 %received_blocks.7 = (bf16[169,1024]{1,0:T(8,128)(2,1)S(1)}, bf16[64,256]{1,0:T(8,128)(2,1)S(1)}) custom-call(bf16[576,256]{1,0:T(8,128)(2,1)S(1)} %constant_dynamic-update-slice_fusion.refs_0_, bf16[576,256]{1,0:T(8,128)(2,1)S(1)} %collective-permute-done.6.refs_2_.refs_1_, bf16[576,256]{1,0:T(8,128)(2,1)S(1)} %collective-permute-done.7.refs_3_.refs_2_, ...), custom_call_target="tpu_custom_call" | custom-call | flops 2000000000 | bytes 1048576 | tf_op jit(solution)/shard_map/received_blocks/pallas_call | solution.py:392
  37.7 0.0 copy-start
  37.8 3.0 %received_blocks.6 = (bf16[169,2048]{1,0:T(8,128)(2,1)S(1)}, bf16[128,256]{1,0:T(8,128)(2,1)S(1)}) custom-call(bf16[576,256]{1,0:T(8,128)(2,1)S(1)} %pad_maximum_fusion.refs_0_, bf16[576,256]{1,0:T(8,128)(2,1)S(1)} %collective-permute-done.9.refs_1_, bf16[576,256]{1,0:T(8,128)(2,1)S(1)} %collective-permute-done.3.refs_2_.refs_0_, ...), custom_call_target="tpu_custom_call" | custom-call | flops 4000000000 | bytes 1048576 | tf_op jit(solution)/shard_map/received_blocks/pallas_call | solution.py:392
  40.8 6.2 %received_blocks.9 = (bf16[169,6144]{1,0:T(8,128)(2,1)}, bf16[169,4096]{1,0:T(8,128)(2,1)}) custom-call(bf16[576,256]{1,0:T(8,128)(2,1)S(1)} %collective-permute-done.3.refs_2_.refs_0_, bf16[576,256]{1,0:T(8,128)(2,1)S(1)} %collective-permute-done.4.refs_1_, bf16[256,256]{1,0:T(8,128)(2,1)S(1)} %get-tuple-element.33.refs_5_.refs_4_.refs_2_, ...), custom_call_target="tpu_custom_call" | custom-call | flops 1000000000 | bytes 1048576 | tf_op jit(solution)/shard_map/received_blocks/pallas_call | solution.py:392
  (17 shorter events, 0.1 us)
Async XLA Ops:
  2.7 10.5 %collective-permute-start = (bf16[288,256]{1,0:T(8,128)(2,1)S(1)}, bf16[288,256]{1,0:T(8,128)(2,1)S(1)}, u32[]{:S(2)}, u32[]{:S(2)}) collective-permute-start(bf16[288,256]{1,0:T(8,128)(2,1)S(1)} %get-tuple-element.27), channel_id=1, source_target_pairs={{0,2},{1,3},{2,0},{3,1},{4,6},{5,7},{6,4},{7,5},{8,10},{9,11},{10,... | collective-permute-start | bytes 442376 | tf_op jit(solution)/shard_map/ppermute | solution.py:463
  5.8 10.1 %collective-permute-start.1 = (bf16[320,256]{1,0:T(8,128)(2,1)S(1)}, bf16[320,256]{1,0:T(8,128)(2,1)S(1)}, u32[]{:S(2)}, u32[]{:S(2)}) collective-permute-start(bf16[320,256]{1,0:T(8,128)(2,1)S(1)} %get-tuple-element.28), channel_id=1, source_target_pairs={{0,4},{1,5},{2,6},{3,7},{4,0},{5,1},{6,2},{7,3},{8,12},{9,13},{10,... | collective-permute-start | bytes 491528 | tf_op jit(solution)/shard_map/ppermute | solution.py:463
  16.0 7.5 %collective-permute-start.7 = (bf16[576,256]{1,0:T(8,128)(2,1)S(1)}, bf16[576,256]{1,0:T(8,128)(2,1)S(1)}, u32[]{:S(2)}, u32[]{:S(2)}) collective-permute-start(bf16[576,256]{1,0:T(8,128)(2,1)S(1)} %constant_dynamic-update-slice_fusion.refs_0_), channel_id=1, source_target_pairs={{0,1},{1,0},{2,3},{3,2},{4,5},{5,4},{6,7},{7,6},{8,9},{9,8},{10,11... | collective-permute-start | bytes 884744 | tf_op jit(solution)/shard_map/ppermute | solution.py:463
  17.5 5.3 %collective-permute-start.2 = (bf16[320,256]{1,0:T(8,128)(2,1)S(1)}, bf16[320,256]{1,0:T(8,128)(2,1)S(1)}, u32[]{:S(2)}, u32[]{:S(2)}) collective-permute-start(bf16[320,256]{1,0:T(8,128)(2,1)S(1)} %collective-permute-done.1), channel_id=1, source_target_pairs={{0,2},{1,3},{2,0},{3,1},{4,6},{5,7},{6,4},{7,5},{8,10},{9,11},{10,... | collective-permute-start | bytes 491528 | tf_op jit(solution)/shard_map/ppermute | solution.py:463
  17.6 9.2 %collective-permute-start.6 = (bf16[576,256]{1,0:T(8,128)(2,1)S(1)}, bf16[576,256]{1,0:T(8,128)(2,1)S(1)}, u32[]{:S(2)}, u32[]{:S(2)}) collective-permute-start(bf16[576,256]{1,0:T(8,128)(2,1)S(1)} %constant_dynamic-update-slice_fusion.refs_0_), channel_id=1, source_target_pairs={{0,24},{1,25},{2,26},{3,27},{4,28},{5,29},{6,30},{7,31},{8,16},{9,... | collective-permute-start | bytes 884744 | tf_op jit(solution)/shard_map/ppermute | solution.py:463
  17.6 9.4 %collective-permute-start.5 = (bf16[576,256]{1,0:T(8,128)(2,1)S(1)}, bf16[576,256]{1,0:T(8,128)(2,1)S(1)}, u32[]{:S(2)}, u32[]{:S(2)}) collective-permute-start(bf16[576,256]{1,0:T(8,128)(2,1)S(1)} %constant_dynamic-update-slice_fusion.refs_0_), channel_id=1, source_target_pairs={{0,8},{1,9},{2,10},{3,11},{4,12},{5,13},{6,14},{7,15},{8,0},{9,1},... | collective-permute-start | bytes 884744 | tf_op jit(solution)/shard_map/ppermute | solution.py:463
  22.9 6.8 %collective-permute-start.3 = (bf16[576,256]{1,0:T(8,128)(2,1)S(1)}, bf16[576,256]{1,0:T(8,128)(2,1)S(1)}, u32[]{:S(2)}, u32[]{:S(2)}) collective-permute-start(bf16[576,256]{1,0:T(8,128)(2,1)S(1)} %pad_maximum_fusion.refs_0_), channel_id=1, source_target_pairs={{0,1},{1,0},{2,3},{3,2},{4,5},{5,4},{6,7},{7,6},{8,9},{9,8},{10,11... | collective-permute-start | bytes 884744 | tf_op jit(solution)/shard_map/ppermute | solution.py:463
  23.5 6.2 %collective-permute-start.8 = (bf16[576,256]{1,0:T(8,128)(2,1)S(1)}, bf16[576,256]{1,0:T(8,128)(2,1)S(1)}, u32[]{:S(2)}, u32[]{:S(2)}) collective-permute-start(bf16[576,256]{1,0:T(8,128)(2,1)S(1)} %collective-permute-done.7.refs_3_.refs_2_), channel_id=1, source_target_pairs={{0,8},{1,9},{2,10},{3,11},{4,12},{5,13},{6,14},{7,15},{8,0},{9,1},... | collective-permute-start | bytes 884744 | tf_op jit(solution)/shard_map/ppermute | solution.py:463
  23.5 11.4 %collective-permute-start.12 = (bf16[576,256]{1,0:T(8,128)(2,1)S(1)}, bf16[576,256]{1,0:T(8,128)(2,1)S(1)}, u32[]{:S(2)}, u32[]{:S(2)}) collective-permute-start(bf16[576,256]{1,0:T(8,128)(2,1)S(1)} %pad_maximum_fusion.refs_0_), channel_id=1, source_target_pairs={{0,24},{1,25},{2,26},{3,27},{4,28},{5,29},{6,30},{7,31},{8,16},{9,... | collective-permute-start | bytes 884744 | tf_op jit(solution)/shard_map/ppermute | solution.py:463
  26.8 10.9 %collective-permute-start.9 = (bf16[576,256]{1,0:T(8,128)(2,1)S(1)}, bf16[576,256]{1,0:T(8,128)(2,1)S(1)}, u32[]{:S(2)}, u32[]{:S(2)}) collective-permute-start(bf16[576,256]{1,0:T(8,128)(2,1)S(1)} %pad_maximum_fusion.refs_0_), channel_id=1, source_target_pairs={{0,8},{1,9},{2,10},{3,11},{4,12},{5,13},{6,14},{7,15},{8,0},{9,1},... | collective-permute-start | bytes 884744 | tf_op jit(solution)/shard_map/ppermute | solution.py:463
  27.0 9.2 %collective-permute-start.11 = (bf16[576,256]{1,0:T(8,128)(2,1)S(1)}, bf16[576,256]{1,0:T(8,128)(2,1)S(1)}, u32[]{:S(2)}, u32[]{:S(2)}) collective-permute-start(bf16[576,256]{1,0:T(8,128)(2,1)S(1)} %collective-permute-done.6.refs_2_.refs_1_), channel_id=1, source_target_pairs={{0,1},{1,0},{2,3},{3,2},{4,5},{5,4},{6,7},{7,6},{8,9},{9,8},{10,11... | collective-permute-start | bytes 884744 | tf_op jit(solution)/shard_map/ppermute | solution.py:463
  29.7 8.1 %collective-permute-start.10 = (bf16[576,256]{1,0:T(8,128)(2,1)S(1)}, bf16[576,256]{1,0:T(8,128)(2,1)S(1)}, u32[]{:S(2)}, u32[]{:S(2)}) collective-permute-start(bf16[576,256]{1,0:T(8,128)(2,1)S(1)} %collective-permute-done.3.refs_2_.refs_0_), channel_id=1, source_target_pairs={{0,8},{1,9},{2,10},{3,11},{4,12},{5,13},{6,14},{7,15},{8,0},{9,1},... | collective-permute-start | bytes 884744 | tf_op jit(solution)/shard_map/ppermute | solution.py:463
  29.7 11.1 %collective-permute-start.4 = (bf16[576,256]{1,0:T(8,128)(2,1)S(1)}, bf16[576,256]{1,0:T(8,128)(2,1)S(1)}, u32[]{:S(2)}, u32[]{:S(2)}) collective-permute-start(bf16[576,256]{1,0:T(8,128)(2,1)S(1)} %collective-permute-done.3.refs_2_.refs_0_), channel_id=1, source_target_pairs={{0,24},{1,25},{2,26},{3,27},{4,28},{5,29},{6,30},{7,31},{8,16},{9,... | collective-permute-start | bytes 884744 | tf_op jit(solution)/shard_map/ppermute | solution.py:463
  37.7 3.0 %copy-start = (bf16[256,169]{0,1:T(8,128)(2,1)S(1)}, bf16[256,169]{0,1:T(8,128)(2,1)}, u32[]{:S(2)}) copy-start(bf16[256,169]{0,1:T(8,128)(2,1)} %param.23) | copy-start | bytes 259588

commit v5 on v4

--- a/solution.py
+++ b/solution.py
@@ -178,6 +178,7 @@
 
 def first_gate_kernel(n, step, dist_ref, atom_ref, feat_ref, *refs):
     sources, held_ref, flipped, left_ref = refs[:6], refs[6], refs[7:13], refs[13]
+    refs[14][...] = sources[5][...]
     for src, dst in zip(sources[:5], flipped[:5]):
         dst[...] = src[...].T
     r = lax.broadcasted_iota(jnp.int32, (n.entries, n.entries), 0)
@@ -190,15 +191,29 @@
     held_ref[...] = gate * dot(left_ref[...], onehot(atom_ref[:, 0:step], n.atoms))
 
 
-def second_gate_kernel(n, step, dist_ref, atom_ref, left_ref, w_in_ref, w_ro_ref, held_ref):
+def second_gate_kernel(n, step, dist_ref, atom_ref, row_ref, left_ref, w_in_ref, w_ro_ref, *outs):
+    held_ref, place_ref = outs
     gate = gate_of(dist_ref[:, step:], w_in_ref[...], w_ro_ref[...])
     held_ref[...] = gate * dot(left_ref[...], onehot(atom_ref[:, step:], n.atoms))
+    _, zi, xi, even = where_am_i()
+    v = row_ref[...]
+    q = whole_div(v, n.fetch)
+    k = v - q * n.fetch
+    m = whole_div(k, 3)
+    o = k - 3 * m
+    sibling = jnp.where(even, 2, 0)
+    role = jnp.where(o == 1, 0, jnp.where(o == sibling, 1, 2))
+    outer = whole_div(q, n.inner)
+    beside = jnp.bitwise_xor(q - outer * n.inner, xi)
+    b = jnp.bitwise_xor(outer, zi)
+    place_ref[...] = ((b * 3 + role) * n.inner + beside) * n.part + m
 
 
 def first_gate(n, step, distance, pair_atom, features, weights):
     turned = [jax.ShapeDtypeStruct(w.shape[::-1], BF16) for w in weights[:5]]
     turned.append(jax.ShapeDtypeStruct(weights[5].shape, BF16))
     turned.append(jax.ShapeDtypeStruct((n.width, n.atoms), BF16))
+    turned.append(jax.ShapeDtypeStruct(weights[5].shape, BF16))
     out = pl.pallas_call(
         functools.partial(first_gate_kernel, n, step),
         out_shape=[jax.ShapeDtypeStruct((n.width, step), F32)] + turned,
@@ -206,17 +221,20 @@
         cost_estimate=cost(3_000_000_000),
         name="first_gate",
     )(*far(distance, pair_atom, features, *weights))
-    return out[0], out[1:7], out[7]
-
-
-def second_gate(n, step, distance, pair_atom, left, w_in_t, w_ro_t):
+    return out[0], out[1:7], out[7], out[8]
+
+
+def second_gate(n, step, distance, pair_atom, partner_row, left, w_in_t, w_ro_t):
     return pl.pallas_call(
         functools.partial(second_gate_kernel, n, step),
-        out_shape=jax.ShapeDtypeStruct((n.width, n.pairs - step), F32),
+        out_shape=[
+            jax.ShapeDtypeStruct((n.width, n.pairs - step), F32),
+            jax.ShapeDtypeStruct((1, n.pairs), jnp.int32),
+        ],
         compiler_params=pltpu.CompilerParams(vmem_limit_bytes=LIMIT),
         cost_estimate=cost(2_000_000_000),
         name="second_gate",
-    )(*far(distance, pair_atom), left, w_in_t, w_ro_t)
+    )(*far(distance, pair_atom, partner_row), left, w_in_t, w_ro_t)
 
 
 def partner_table(n, even, feat, tails, w_right_t, table_ref):
@@ -402,27 +420,15 @@
 
 
 def own_part(n, calls, mine, w_mix, last, own_buf, own_ref, sem, even, zi, xi):
-    row_ref, halves, w_right_ref, w_out_ref, tables = mine[0], mine[1:3], mine[3], mine[4], mine[5:]
-    rows = jnp.concatenate([t[...] for t in tables] + [last[...]], 0)
+    place_ref, halves, w_right_ref, w_out_ref, tables = mine[0], mine[1:3], mine[3], mine[4], mine[5:]
+    pieces = {}
+    for (steps, have), found in zip(calls, (*tables, last)):
+        keys = [(step, role, beside) for role, beside in have for step in steps]
+        for g, key in enumerate(keys):
+            pieces[key] = found[g * n.part : (g + 1) * n.part, :]
+    rows = jnp.concatenate([pieces[key] for key in sorted(pieces)], 0)
     table = dot(w_right_ref[...], rows, 1, 1).astype(BF16)
-    v = row_ref[...]
-    q = whole_div(v, n.fetch)
-    k = v - q * n.fetch
-    m = whole_div(k, 3)
-    o = k - 3 * m
-    sibling = jnp.where(even, 2, 0)
-    role = jnp.where(o == 1, 0, jnp.where(o == sibling, 1, 2))
-    outer = whole_div(q, n.inner)
-    inner = q - outer * n.inner
-    b = jnp.bitwise_xor(outer, zi)
-    place, top = b, 0
-    for steps, have in calls:
-        for r, beside in have:
-            for step in steps:
-                here = (b == step) & (role == r) & (jnp.bitwise_xor(inner, xi) == beside)
-                place = jnp.where(here, top, place)
-                top += 1
-    place = place * n.part + m
+    place = place_ref[...]
     done, at = [], 0
     for i, half in enumerate(halves):
         step = half.shape[1]
@@ -487,7 +493,7 @@
     for b in range(3, n.outer, 2):
         lines_in[b] = exchange(lines_in[b - 1], along(1))
     step = n.pairs // 2
-    held, turned, left = first_gate(
+    held, turned, left, w_out_t = first_gate(
         n,
         step,
         distance,
@@ -495,7 +501,9 @@
         features,
         (w_left, w_right, w_radial_in, w_radial_out, w_mix, w_out.T),
     )
-    second = second_gate(n, step, distance, pair_atom, left, turned[2], turned[3])
+    second, place = second_gate(
+        n, step, distance, pair_atom, partner_row, left, turned[2], turned[3]
+    )
     lines_in[1], lines_in[2], second = lax.optimization_barrier((lines_in[1], lines_in[2], second))
     w_left_t, w_right_t, w_in_t, w_ro_t, w_mix_t, w_flip_t = turned
     weights = (w_left_t, w_in_t, w_ro_t, w_mix_t, w_flip_t)
@@ -526,7 +534,7 @@
     table = take(last, away_near, table)
     every = (*calls, (sets[last][0], away_far))
     earlier = parts if n.slot % 128 == 0 else []
-    own = (every, earlier, [*far(partner_row), held, second, w_right_t, w_out.T, *tables])
+    own = (every, earlier, [place, held, second, w_right_t, w_out_t, *tables])
     into, own = received(n, sets[last][0], away_far, sets[last][1], weights, table, w_right_t, own)
     if n.slot % 128:
         cell, strip = lax.axis_index("cell"), lax.axis_index("strip")

time: 47.7 us -> 46.6 us (0.977)
  Pallas kernels: 21.8 us -> 21 us
    pallas_call x5, Pallas kernels: 14.9 us -> 14.1 us  [received(): pl.pallas_call(functools.partial(received_kernel, n, steps, have, tuple(u...]
where the time goes in v5:
time: 46.6 us; the launch traced here: 46.3 us
  Pallas kernels  21 us (45%)
  starting transfers between devices  15.4 us (33%)
  waiting for transfers between devices  8.86 us (19%)
  between operations  0.91 us (2%)
    ppermute x13, starting transfers between devices, exchange(): return lax.ppermute(x, AXES, pairs)  15.4 us
    pallas_call x5, Pallas kernels, received(): pl.pallas_call(functools.partial(received_kernel, n, steps, have, tuple(u...  14.1 us
    ppermute x13, waiting for transfers between devices, exchange(): return lax.ppermute(x, AXES, pairs)  8.86 us
    pallas_call x1, Pallas kernels, first_gate(): pl.pallas_call(functools.partial(first_gate_kernel, n, step), out_shape=[...  2.69 us
    pallas_call x1, Pallas kernels, second_gate(): pl.pallas_call(functools.partial(second_gate_kernel, n, step), out_shape=...  2.18 us
    pallas_call x1, Pallas kernels, make_tiles(): pl.pallas_call(functools.partial(tiles_kernel, n), out_shape=[jax.ShapeDt...  2.09 us
  transfers between devices with their start and end apart: 13, of which 5 were waited for; matrix products, arithmetic and copies ran while one was open for 0% of the time, Pallas kernels for 29%

profile of v5, /device:TPU:0, one launch (start us, length us, event | category | flops | bytes accessed | tf_op | source)
XLA Modules:
  0.0 46.3 jit_solution(9309335091833020978)
XLA Ops:
  0.6 2.1 %place_pairs.1 = (bf16[288,256]{1,0:T(8,128)(2,1)S(1)}, bf16[288,256]{1,0:T(8,128)(2,1)S(1)}, bf16[320,256]{1,0:T(8,128)(2,1)S(1)}) custom-call(s32[1,4096]{1,0:T(1,128)} %bitcast.7, s32[1,4096]{1,0:T(1,128)} %bitcast.10, s32[1,4096]{1,0:T(1,128)} %bitcast.6, f32[1,4096]{1,0:T(1,128)} %bitcast.12, s32[8,48]{1,0:T(8,128)} %list_ref.1, bf16[256,256]{1,0:T(8,128)(2,1)} %feat_ref.3), custom_call_target="tpu_custom_call" | custom-call | flops 600000000 | bytes 1048576 | tf_op jit(solution)/shard_map/place_pairs/pallas_call | solution.py:167
  2.7 3.1 %collective-permute-start = (bf16[288,256]{1,0:T(8,128)(2,1)S(1)}, bf16[288,256]{1,0:T(8,128)(2,1)S(1)}, u32[]{:S(2)}, u32[]{:S(2)}) collective-permute-start(bf16[288,256]{1,0:T(8,128)(2,1)S(1)} %get-tuple-element.30), channel_id=1, source_target_pairs={{0,2},{1,3},{2,0},{3,1},{4,6},{5,7},{6,4},{7,5},{8,10},{9,11},{10,... | collective-permute-start | bytes 442376 | tf_op jit(solution)/shard_map/ppermute | solution.py:469
  5.8 2.6 %collective-permute-start.1 = (bf16[320,256]{1,0:T(8,128)(2,1)S(1)}, bf16[320,256]{1,0:T(8,128)(2,1)S(1)}, u32[]{:S(2)}, u32[]{:S(2)}) collective-permute-start(bf16[320,256]{1,0:T(8,128)(2,1)S(1)} %get-tuple-element.31), channel_id=1, source_target_pairs={{0,4},{1,5},{2,6},{3,7},{4,0},{5,1},{6,2},{7,3},{8,12},{9,13},{10,... | collective-permute-start | bytes 491528 | tf_op jit(solution)/shard_map/ppermute | solution.py:469
  8.4 2.7 %first_gate.1 = (f32[256,2048]{1,0:T(8,128)S(1)}, bf16[256,256]{1,0:T(8,128)(2,1)S(1)}, bf16[256,256]{1,0:T(8,128)(2,1)S(1)}, bf16[256,128]{1,0:T(8,128)(2,1)S(1...) custom-call(f32[1,4096]{1,0:T(1,128)} %bitcast.13, ...), custom_call_target="tpu_custom_call" | custom-call | flops 3000000000 | bytes 1048576 | tf_op jit(solution)/shard_map/first_gate/pallas_call | solution.py:217
  11.1 2.2 %second_gate.1 = (f32[256,2048]{1,0:T(8,128)S(1)}, s32[1,4096]{1,0:T(1,128)S(1)}) custom-call(f32[1,4096]{1,0:T(1,128)} %bitcast.14, s32[1,4096]{1,0:T(1,128)} %bitcast.9, s32[1,4096]{1,0:T(1,128)} %bitcast.11, bf16[256,256]{1,0:T(8,128)(2,1)S(1)} %get-tuple-element.32.left_ref, bf16[256,128]{1,0:T(8,128)(2,1)S(1)} %get-tuple-element.33.w_in_ref.refs_6_.refs_5_.refs_3_, ...), custom_call_target="tpu_custom_call" | custom-call | flops 2000000000 | bytes 1048576 | tf_op jit(solution)/shard_map/second_gate/pallas_call | solution.py:228
  13.3 0.0 collective-permute-done
  13.3 2.6 %collective-permute-done.1 = bf16[320,256]{1,0:T(8,128)(2,1)S(1)} collective-permute-done((bf16[320,256]{1,0:T(8,128)(2,1)S(1)}, bf16[320,256]{1,0:T(8,128)(2,1)S(1)}, u32[]{:S(2)}, u32[]{:S(2)}) %collective-permute-start.1) | collective-permute-done | bytes 163872 | tf_op jit(solution)/shard_map/ppermute | solution.py:469
  16.0 1.6 %collective-permute-start.7 = (bf16[576,256]{1,0:T(8,128)(2,1)S(1)}, bf16[576,256]{1,0:T(8,128)(2,1)S(1)}, u32[]{:S(2)}, u32[]{:S(2)}) collective-permute-start(bf16[576,256]{1,0:T(8,128)(2,1)S(1)} %constant_dynamic-update-slice_fusion.refs_0_), channel_id=1, source_target_pairs={{0,1},{1,0},{2,3},{3,2},{4,5},{5,4},{6,7},{7,6},{8,9},{9,8},{10,11... | collective-permute-start | bytes 884744 | tf_op jit(solution)/shard_map/ppermute | solution.py:469
  17.5 0.1 collective-permute-start.2
  17.6 1.6 %collective-permute-start.5 = (bf16[576,256]{1,0:T(8,128)(2,1)S(1)}, bf16[576,256]{1,0:T(8,128)(2,1)S(1)}, u32[]{:S(2)}, u32[]{:S(2)}) collective-permute-start(bf16[576,256]{1,0:T(8,128)(2,1)S(1)} %constant_dynamic-update-slice_fusion.refs_0_), channel_id=1, source_target_pairs={{0,8},{1,9},{2,10},{3,11},{4,12},{5,13},{6,14},{7,15},{8,0},{9,1},... | collective-permute-start | bytes 884744 | tf_op jit(solution)/shard_map/ppermute | solution.py:469
  19.3 3.6 %collective-permute-done.2 = bf16[320,256]{1,0:T(8,128)(2,1)S(1)} collective-permute-done((bf16[320,256]{1,0:T(8,128)(2,1)S(1)}, bf16[320,256]{1,0:T(8,128)(2,1)S(1)}, u32[]{:S(2)}, u32[]{:S(2)}) %collective-permute-start.2) | collective-permute-done | bytes 163872 | tf_op jit(solution)/shard_map/ppermute | solution.py:469
  22.9 0.6 %collective-permute-start.3 = (bf16[576,256]{1,0:T(8,128)(2,1)S(1)}, bf16[576,256]{1,0:T(8,128)(2,1)S(1)}, u32[]{:S(2)}, u32[]{:S(2)}) collective-permute-start(bf16[576,256]{1,0:T(8,128)(2,1)S(1)} %pad_maximum_fusion.refs_0_), channel_id=1, source_target_pairs={{0,1},{1,0},{2,3},{3,2},{4,5},{5,4},{6,7},{7,6},{8,9},{9,8},{10,11... | collective-permute-start | bytes 884744 | tf_op jit(solution)/shard_map/ppermute | solution.py:469
  23.5 2.3 %collective-permute-start.12 = (bf16[576,256]{1,0:T(8,128)(2,1)S(1)}, bf16[576,256]{1,0:T(8,128)(2,1)S(1)}, u32[]{:S(2)}, u32[]{:S(2)}) collective-permute-start(bf16[576,256]{1,0:T(8,128)(2,1)S(1)} %pad_maximum_fusion.refs_0_), channel_id=1, source_target_pairs={{0,24},{1,25},{2,26},{3,27},{4,28},{5,29},{6,30},{7,31},{8,16},{9,... | collective-permute-start | bytes 884744 | tf_op jit(solution)/shard_map/ppermute | solution.py:469
  25.7 1.1 %collective-permute-done.6.refs_2_.refs_1_ = bf16[576,256]{1,0:T(8,128)(2,1)S(1)} collective-permute-done((bf16[576,256]{1,0:T(8,128)(2,1)S(1)}, bf16[576,256]{1,0:T(8,128)(2,1)S(1)}, u32[]{:S(2)}, u32[]{:S(2)}) %collective-permute-start.6) | collective-permute-done | bytes 294944 | tf_op jit(solution)/shard_map/ppermute | solution.py:469
  26.8 0.2 collective-permute-start.9
  27.0 1.3 %collective-permute-start.11 = (bf16[576,256]{1,0:T(8,128)(2,1)S(1)}, bf16[576,256]{1,0:T(8,128)(2,1)S(1)}, u32[]{:S(2)}, u32[]{:S(2)}) collective-permute-start(bf16[576,256]{1,0:T(8,128)(2,1)S(1)} %collective-permute-done.6.refs_2_.refs_1_), channel_id=1, source_target_pairs={{0,1},{1,0},{2,3},{3,2},{4,5},{5,4},{6,7},{7,6},{8,9},{9,8},{10,11... | collective-permute-start | bytes 884744 | tf_op jit(solution)/shard_map/ppermute | solution.py:469
  28.3 1.4 %collective-permute-done.3.refs_2_.refs_0_ = bf16[576,256]{1,0:T(8,128)(2,1)S(1)} collective-permute-done((bf16[576,256]{1,0:T(8,128)(2,1)S(1)}, bf16[576,256]{1,0:T(8,128)(2,1)S(1)}, u32[]{:S(2)}, u32[]{:S(2)}) %collective-permute-start.3) | collective-permute-done | bytes 294944 | tf_op jit(solution)/shard_map/ppermute | solution.py:469
  29.7 2.1 %collective-permute-start.4 = (bf16[576,256]{1,0:T(8,128)(2,1)S(1)}, bf16[576,256]{1,0:T(8,128)(2,1)S(1)}, u32[]{:S(2)}, u32[]{:S(2)}) collective-permute-start(bf16[576,256]{1,0:T(8,128)(2,1)S(1)} %collective-permute-done.3.refs_2_.refs_0_), channel_id=1, source_target_pairs={{0,24},{1,25},{2,26},{3,27},{4,28},{5,29},{6,30},{7,31},{8,16},{9,... | collective-permute-start | bytes 884744 | tf_op jit(solution)/shard_map/ppermute | solution.py:469
  31.8 3.1 %received_blocks.5 = (bf16[169,2048]{1,0:T(8,128)(2,1)S(1)}, bf16[128,256]{1,0:T(8,128)(2,1)S(1)}, bf16[3,256,128]{2,1,0:T(8,128)(2,1)S(1)}) custom-call(bf16[576,256]{1,0:T(8,128)(2,1)S(1)} %constant_dynamic-update-slice_fusion.refs_0_, bf16[576,256]{1,0:T(8,128)(2,1)S(1)} %collective-permute-done.5.refs_1_, ...), custom_call_target="tpu_custom_call" | custom-call | flops 4000000000 | bytes 1048576 | tf_op jit(solution)/shard_map/received_blocks/pallas_call | solution.py:410
  34.9 1.2 %received_blocks.8 = (bf16[169,512]{1,0:T(8,128)(2,1)S(1)}, bf16[32,256]{1,0:T(8,128)(2,1)S(1)}) custom-call(bf16[576,256]{1,0:T(8,128)(2,1)S(1)} %pad_maximum_fusion.refs_0_, bf16[576,256]{1,0:T(8,128)(2,1)S(1)} %collective-permute-done.12.refs_1_, bf16[256,256]{1,0:T(8,128)(2,1)S(1)} %get-tuple-element.37.refs_5_.refs_4_.refs_2_, ...), custom_call_target="tpu_custom_call" | custom-call | flops 1000000000 | bytes 1048576 | tf_op jit(solution)/shard_map/received_blocks/pallas_call | solution.py:410
  36.1 0.2 collective-permute-done.11.refs_3_
  36.3 1.4 %received_blocks.7 = (bf16[169,1024]{1,0:T(8,128)(2,1)S(1)}, bf16[64,256]{1,0:T(8,128)(2,1)S(1)}) custom-call(bf16[576,256]{1,0:T(8,128)(2,1)S(1)} %constant_dynamic-update-slice_fusion.refs_0_, bf16[576,256]{1,0:T(8,128)(2,1)S(1)} %collective-permute-done.6.refs_2_.refs_1_, bf16[576,256]{1,0:T(8,128)(2,1)S(1)} %collective-permute-done.7.refs_3_.refs_2_, ...), custom_call_target="tpu_custom_call" | custom-call | flops 2000000000 | bytes 1048576 | tf_op jit(solution)/shard_map/received_blocks/pallas_call | solution.py:410
  37.7 2.9 %received_blocks.6 = (bf16[169,2048]{1,0:T(8,128)(2,1)S(1)}, bf16[128,256]{1,0:T(8,128)(2,1)S(1)}) custom-call(bf16[576,256]{1,0:T(8,128)(2,1)S(1)} %pad_maximum_fusion.refs_0_, bf16[576,256]{1,0:T(8,128)(2,1)S(1)} %collective-permute-done.9.refs_1_, bf16[576,256]{1,0:T(8,128)(2,1)S(1)} %collective-permute-done.3.refs_2_.refs_0_, ...), custom_call_target="tpu_custom_call" | custom-call | flops 4000000000 | bytes 1048576 | tf_op jit(solution)/shard_map/received_blocks/pallas_call | solution.py:410
  40.7 5.5 %received_blocks.9 = (bf16[169,6144]{1,0:T(8,128)(2,1)}, bf16[169,4096]{1,0:T(8,128)(2,1)}) custom-call(bf16[576,256]{1,0:T(8,128)(2,1)S(1)} %collective-permute-done.3.refs_2_.refs_0_, bf16[576,256]{1,0:T(8,128)(2,1)S(1)} %collective-permute-done.4.refs_1_, bf16[256,256]{1,0:T(8,128)(2,1)S(1)} %get-tuple-element.37.refs_5_.refs_4_.refs_2_, ...), custom_call_target="tpu_custom_call" | custom-call | flops 1000000000 | bytes 1048576 | tf_op jit(solution)/shard_map/received_blocks/pallas_call | solution.py:410
  (15 shorter events, 0.1 us)
Async XLA Ops:
  2.7 10.6 %collective-permute-start = (bf16[288,256]{1,0:T(8,128)(2,1)S(1)}, bf16[288,256]{1,0:T(8,128)(2,1)S(1)}, u32[]{:S(2)}, u32[]{:S(2)}) collective-permute-start(bf16[288,256]{1,0:T(8,128)(2,1)S(1)} %get-tuple-element.30), channel_id=1, source_target_pairs={{0,2},{1,3},{2,0},{3,1},{4,6},{5,7},{6,4},{7,5},{8,10},{9,11},{10,... | collective-permute-start | bytes 442376 | tf_op jit(solution)/shard_map/ppermute | solution.py:469
  5.8 10.1 %collective-permute-start.1 = (bf16[320,256]{1,0:T(8,128)(2,1)S(1)}, bf16[320,256]{1,0:T(8,128)(2,1)S(1)}, u32[]{:S(2)}, u32[]{:S(2)}) collective-permute-start(bf16[320,256]{1,0:T(8,128)(2,1)S(1)} %get-tuple-element.31), channel_id=1, source_target_pairs={{0,4},{1,5},{2,6},{3,7},{4,0},{5,1},{6,2},{7,3},{8,12},{9,13},{10,... | collective-permute-start | bytes 491528 | tf_op jit(solution)/shard_map/ppermute | solution.py:469
  16.0 7.5 %collective-permute-start.7 = (bf16[576,256]{1,0:T(8,128)(2,1)S(1)}, bf16[576,256]{1,0:T(8,128)(2,1)S(1)}, u32[]{:S(2)}, u32[]{:S(2)}) collective-permute-start(bf16[576,256]{1,0:T(8,128)(2,1)S(1)} %constant_dynamic-update-slice_fusion.refs_0_), channel_id=1, source_target_pairs={{0,1},{1,0},{2,3},{3,2},{4,5},{5,4},{6,7},{7,6},{8,9},{9,8},{10,11... | collective-permute-start | bytes 884744 | tf_op jit(solution)/shard_map/ppermute | solution.py:469
  17.5 5.3 %collective-permute-start.2 = (bf16[320,256]{1,0:T(8,128)(2,1)S(1)}, bf16[320,256]{1,0:T(8,128)(2,1)S(1)}, u32[]{:S(2)}, u32[]{:S(2)}) collective-permute-start(bf16[320,256]{1,0:T(8,128)(2,1)S(1)} %collective-permute-done.1), channel_id=1, source_target_pairs={{0,2},{1,3},{2,0},{3,1},{4,6},{5,7},{6,4},{7,5},{8,10},{9,11},{10,... | collective-permute-start | bytes 491528 | tf_op jit(solution)/shard_map/ppermute | solution.py:469
  17.6 9.2 %collective-permute-start.6 = (bf16[576,256]{1,0:T(8,128)(2,1)S(1)}, bf16[576,256]{1,0:T(8,128)(2,1)S(1)}, u32[]{:S(2)}, u32[]{:S(2)}) collective-permute-start(bf16[576,256]{1,0:T(8,128)(2,1)S(1)} %constant_dynamic-update-slice_fusion.refs_0_), channel_id=1, source_target_pairs={{0,24},{1,25},{2,26},{3,27},{4,28},{5,29},{6,30},{7,31},{8,16},{9,... | collective-permute-start | bytes 884744 | tf_op jit(solution)/shard_map/ppermute | solution.py:469
  17.6 9.4 %collective-permute-start.5 = (bf16[576,256]{1,0:T(8,128)(2,1)S(1)}, bf16[576,256]{1,0:T(8,128)(2,1)S(1)}, u32[]{:S(2)}, u32[]{:S(2)}) collective-permute-start(bf16[576,256]{1,0:T(8,128)(2,1)S(1)} %constant_dynamic-update-slice_fusion.refs_0_), channel_id=1, source_target_pairs={{0,8},{1,9},{2,10},{3,11},{4,12},{5,13},{6,14},{7,15},{8,0},{9,1},... | collective-permute-start | bytes 884744 | tf_op jit(solution)/shard_map/ppermute | solution.py:469
  22.9 6.8 %collective-permute-start.3 = (bf16[576,256]{1,0:T(8,128)(2,1)S(1)}, bf16[576,256]{1,0:T(8,128)(2,1)S(1)}, u32[]{:S(2)}, u32[]{:S(2)}) collective-permute-start(bf16[576,256]{1,0:T(8,128)(2,1)S(1)} %pad_maximum_fusion.refs_0_), channel_id=1, source_target_pairs={{0,1},{1,0},{2,3},{3,2},{4,5},{5,4},{6,7},{7,6},{8,9},{9,8},{10,11... | collective-permute-start | bytes 884744 | tf_op jit(solution)/shard_map/ppermute | solution.py:469
  23.5 6.2 %collective-permute-start.8 = (bf16[576,256]{1,0:T(8,128)(2,1)S(1)}, bf16[576,256]{1,0:T(8,128)(2,1)S(1)}, u32[]{:S(2)}, u32[]{:S(2)}) collective-permute-start(bf16[576,256]{1,0:T(8,128)(2,1)S(1)} %collective-permute-done.7.refs_3_.refs_2_), channel_id=1, source_target_pairs={{0,8},{1,9},{2,10},{3,11},{4,12},{5,13},{6,14},{7,15},{8,0},{9,1},... | collective-permute-start | bytes 884744 | tf_op jit(solution)/shard_map/ppermute | solution.py:469
  23.5 11.4 %collective-permute-start.12 = (bf16[576,256]{1,0:T(8,128)(2,1)S(1)}, bf16[576,256]{1,0:T(8,128)(2,1)S(1)}, u32[]{:S(2)}, u32[]{:S(2)}) collective-permute-start(bf16[576,256]{1,0:T(8,128)(2,1)S(1)} %pad_maximum_fusion.refs_0_), channel_id=1, source_target_pairs={{0,24},{1,25},{2,26},{3,27},{4,28},{5,29},{6,30},{7,31},{8,16},{9,... | collective-permute-start | bytes 884744 | tf_op jit(solution)/shard_map/ppermute | solution.py:469
  26.8 10.9 %collective-permute-start.9 = (bf16[576,256]{1,0:T(8,128)(2,1)S(1)}, bf16[576,256]{1,0:T(8,128)(2,1)S(1)}, u32[]{:S(2)}, u32[]{:S(2)}) collective-permute-start(bf16[576,256]{1,0:T(8,128)(2,1)S(1)} %pad_maximum_fusion.refs_0_), channel_id=1, source_target_pairs={{0,8},{1,9},{2,10},{3,11},{4,12},{5,13},{6,14},{7,15},{8,0},{9,1},... | collective-permute-start | bytes 884744 | tf_op jit(solution)/shard_map/ppermute | solution.py:469
  27.0 9.2 %collective-permute-start.11 = (bf16[576,256]{1,0:T(8,128)(2,1)S(1)}, bf16[576,256]{1,0:T(8,128)(2,1)S(1)}, u32[]{:S(2)}, u32[]{:S(2)}) collective-permute-start(bf16[576,256]{1,0:T(8,128)(2,1)S(1)} %collective-permute-done.6.refs_2_.refs_1_), channel_id=1, source_target_pairs={{0,1},{1,0},{2,3},{3,2},{4,5},{5,4},{6,7},{7,6},{8,9},{9,8},{10,11... | collective-permute-start | bytes 884744 | tf_op jit(solution)/shard_map/ppermute | solution.py:469
  29.7 8.1 %collective-permute-start.10 = (bf16[576,256]{1,0:T(8,128)(2,1)S(1)}, bf16[576,256]{1,0:T(8,128)(2,1)S(1)}, u32[]{:S(2)}, u32[]{:S(2)}) collective-permute-start(bf16[576,256]{1,0:T(8,128)(2,1)S(1)} %collective-permute-done.3.refs_2_.refs_0_), channel_id=1, source_target_pairs={{0,8},{1,9},{2,10},{3,11},{4,12},{5,13},{6,14},{7,15},{8,0},{9,1},... | collective-permute-start | bytes 884744 | tf_op jit(solution)/shard_map/ppermute | solution.py:469
  29.7 11.0 %collective-permute-start.4 = (bf16[576,256]{1,0:T(8,128)(2,1)S(1)}, bf16[576,256]{1,0:T(8,128)(2,1)S(1)}, u32[]{:S(2)}, u32[]{:S(2)}) collective-permute-start(bf16[576,256]{1,0:T(8,128)(2,1)S(1)} %collective-permute-done.3.refs_2_.refs_0_), channel_id=1, source_target_pairs={{0,24},{1,25},{2,26},{3,27},{4,28},{5,29},{6,30},{7,31},{8,16},{9,... | collective-permute-start | bytes 884744 | tf_op jit(solution)/shard_map/ppermute | solution.py:469
